TPU v7x, 32 devices: a whole 2x2x4 slice. The times are simulated.
32 devices in a mesh: groups: 2 (over y), ep: 16 (over z, x, core).
Axes of the slice: x: 2, y: 2, z: 4, core: 2. Of those that a mesh axis runs over, the one named last changes fastest.
Arguments:
- tokens: bfloat16 [4096, 7168], P(('groups', 'ep')), parts along dimension 0, may hold values from -6 to 6
- norm_gain: float32 [7168], replicated, may hold values from 0.1 to 1.9
- expert_gate: bfloat16 [7168, 16384], P(None, 'ep'), may hold values from -0.0625 to 0.0625
- expert_up: bfloat16 [7168, 16384], P(None, 'ep'), may hold values from -0.0625 to 0.0625
- expert_down: bfloat16 [16384, 7168], P('ep'), may hold values from -0.1875 to 0.1875
- route_ids: int32 [4096, 1], P(('groups', 'ep')), parts along dimension 0, may hold values from 0 to 15; in each aligned block of 128 rows (0 to 127, 128 to 255, ...) at most 8 rows name the same one
- route_gates: float32 [4096, 1], P(('groups', 'ep')), parts along dimension 0, may hold values from 0.1 to 1
Outputs:
- layer_out: bfloat16 [4096, 7168], P(('groups', 'ep')), parts along dimension 0
There are 2 independent parts, one for each index of `groups`. A program takes and returns all parts, laid end to end along the dimension named above; an argument that names none is the same for every part. Nothing has to cross between parts.
Inputs may be any that keep to these rules, and one draw needn't show every extreme that they name: `route_ids`: among the rows of one device no expert is named by more than 8 routes, and in every draw some device names some expert exactly 8 times.
All inputs are finite; a program needn't handle non-finite values.
Results may differ from a plain program's by a relative error of at most 0.0042.
Values may be sent and summed in bfloat16 or wider, within the bound.
No kernel may reach another device: no remote copies, remote signals or barrier semaphores. Data moves between devices by JAX's collectives and lax.ppermute only.
A program may use at most 128 MiB of HBM per device.

v0:
```python
import jax
import jax.numpy as jnp
from jax import lax
from jax.sharding import PartitionSpec as P

EXPERTS = 16
CAP = 8


def rms_scale(values, scale_gain):
    wide = values.astype(jnp.float32)
    mean_square = jnp.mean(wide * wide, axis=-1, keepdims=True)
    return (wide * lax.rsqrt(mean_square + 1e-05) * scale_gain).astype(jnp.bfloat16)


def swiglu(inputs, w_gate, w_up):
    gate_proj = jnp.dot(inputs, w_gate, preferred_element_type=jnp.float32)
    up_proj = jnp.dot(inputs, w_up, preferred_element_type=jnp.float32)
    return (jax.nn.silu(gate_proj) * up_proj).astype(jnp.bfloat16)


def per_device(tokens, norm_gain, expert_gate, expert_up, expert_down, route_ids, route_gates):
    device_count = lax.axis_size("ep")
    tok_rows = tokens.shape[0]
    model_width = tokens.shape[1]
    top_count = route_ids.shape[1]
    expert_count = EXPERTS
    shards = device_count // expert_count
    capacity = CAP
    normed = rms_scale(tokens, norm_gain)
    pair_count = tok_rows * top_count
    flat_ids = route_ids.reshape(pair_count)
    flat_gates = route_gates.reshape(pair_count)
    expert_hit = (flat_ids[:, None] == jnp.arange(expert_count, dtype=jnp.int32)[None, :]).astype(
        jnp.float32
    )
    pair_order = jnp.arange(pair_count, dtype=jnp.int32)
    earlier = (pair_order[:, None] > pair_order[None, :]).astype(jnp.float32)
    before = jnp.dot(earlier, expert_hit, precision=lax.Precision.HIGHEST)
    slot_index = jnp.sum(before * expert_hit, axis=1)
    slot_hit = (slot_index[:, None] == jnp.arange(capacity, dtype=jnp.float32)[None, :]).astype(
        jnp.float32
    )
    slot_table = (expert_hit[:, :, None] * slot_hit[:, None, :]).reshape(
        pair_count, expert_count * capacity
    )
    token_owner = (
        (pair_order // top_count)[:, None] == jnp.arange(tok_rows, dtype=jnp.int32)[None, :]
    ).astype(jnp.float32)
    pick_table = jnp.dot(slot_table.T, token_owner, precision=lax.Precision.HIGHEST)
    send_rows = jnp.dot(
        pick_table.astype(jnp.bfloat16), normed, preferred_element_type=jnp.float32
    ).astype(jnp.bfloat16)
    send_rows = send_rows.reshape(expert_count, 1, capacity, model_width)
    send_all = jnp.broadcast_to(send_rows, (expert_count, shards, capacity, model_width)).reshape(
        device_count, capacity, model_width
    )
    received = lax.all_to_all(send_all, "ep", split_axis=0, concat_axis=0, tiled=True)
    flat_rows = received.reshape(-1, model_width)
    routed_hidden = swiglu(flat_rows, expert_gate, expert_up)
    partial_value = jnp.dot(routed_hidden, expert_down, preferred_element_type=jnp.float32).astype(
        jnp.bfloat16
    )
    partials = partial_value.reshape(received.shape)
    returned = lax.all_to_all(partials, "ep", split_axis=0, concat_axis=0, tiled=True)
    summed = jnp.sum(
        returned.reshape(expert_count, shards, capacity, model_width).astype(jnp.float32), axis=1
    )
    summed = summed.reshape(expert_count * capacity, model_width)
    gate_table = jnp.dot(
        (token_owner * flat_gates[:, None]).T, slot_table, precision=lax.Precision.HIGHEST
    )
    routed = jnp.dot(gate_table, summed, precision=lax.Precision.HIGHEST)
    return (tokens.astype(jnp.float32) + routed).astype(jnp.bfloat16)


def solution(mesh):
    in_specs = (
        P(("groups", "ep"), None),
        P(),
        P(None, "ep"),
        P(None, "ep"),
        P("ep", None),
        P(("groups", "ep"), None),
        P(("groups", "ep"), None),
    )
    out_specs = P(("groups", "ep"), None)
    return jax.shard_map(
        per_device, mesh=mesh, in_specs=in_specs, out_specs=out_specs, check_vma=False
    )
```

profile of v0, /device:TPU:9, one launch (start us, length us, event | category | flops | bytes accessed | tf_op | source)
XLA Modules:
  0.0 121.1 jit_solution(17882506263149651276)
XLA Ops:
  0.0 0.7 fusion.33
  0.7 0.9 fusion.20
  1.6 1.9 %fusion.3 = f32[128]{0:T(128)S(1)} fusion(bf16[128,7168]{1,0:T(8,128)(2,1)} %param.7), kind=kLoop, calls=%fused_computation.8 | loop fusion | flops 2752384 | bytes 1835520 | tf_op jit(solution)/shard_map/reduce_sum | solution.py:12
  3.5 0.2 convolution_convert_fusion.2
  3.7 2.3 %fusion.1 = bf16[16,8,7168]{2,1,0:T(8,128)(2,1)S(1)} fusion(bf16[128,128]{1,0:T(8,128)(2,1)S(1)} %convolution_convert_fusion.2, bf16[128,7168]{1,0:T(8,128)(2,1)} %param.7, f32[7168]{0:T(1024)} %param.8, f32[128]{0:T(128)S(1)} %add_rsqrt_fusion), kind=kOutput, calls=%fused_computation.4 | convolution fusion | flops 239468544 | bytes 3731968 | tf_op jit(solution)/shard_map/dot_general | solution.py:51
  6.0 0.0 slice-start
  6.0 49.1 %all_to_all.10 = bf16[16,8,7168]{2,1,0:T(8,128)(2,1)S(1)} all-to-all(bf16[16,8,7168]{2,1,0:T(8,128)(2,1)S(1)} %fusion.1), channel_id=1, replica_groups=mesh['groups'=2,'ep'=16] {'ep'}, dimensions={0} | all-to-all | bytes 3670016 | tf_op jit(solution)/shard_map/all_to_all | solution.py:58
  55.1 0.0 slice-start.1
  55.1 0.0 slice-start.2
  55.1 0.0 slice-start.3
  55.1 0.0 slice-start.4
  55.1 0.0 slice-start.5
  55.1 0.0 slice-start.6
  55.1 7.6 %fusion.10 = f32[128,1024]{1,0:T(8,128)S(1)} fusion(bf16[7168,1024]{1,0:T(8,128)(2,1)} %param.9, bf16[16,8,7168]{2,1,0:T(8,128)(2,1)S(1)} %all_to_all.10), kind=kOutput, calls=%fused_computation.14 | convolution fusion | flops 1879048192 | bytes 17039360 | tf_op jit(solution)/shard_map/dot_general | solution.py:17
  62.7 0.0 slice-done
  62.7 0.0 slice-done.1
  62.7 0.0 slice-done.2
  62.7 0.6 slice-done.3
  63.3 0.0 slice-start.7
  63.3 2.2 %fusion.17 = bf16[128,1024]{1,0:T(8,128)(2,1)S(1)} fusion(bf16[7168,1024]{1,0:T(8,128)(2,1)S(1)} %bitcast.30, bf16[16,8,7168]{2,1,0:T(8,128)(2,1)S(1)} %all_to_all.10, f32[128,1024]{1,0:T(8,128)S(1)} %fusion.10), kind=kOutput, calls=%fused_computation.19 | convolution fusion | flops 1879834624 | bytes 17301504 | tf_op jit(solution)/shard_map/dot_general | solution.py:18
  65.5 0.0 slice-done.4
  65.6 0.1 slice-done.5
  65.7 1.2 slice-done.6
  66.9 0.8 slice-done.7
  67.7 3.4 %fusion.2 = bf16[16,8,7168]{2,1,0:T(8,128)(2,1)} fusion(bf16[128,1024]{1,0:T(8,128)(2,1)S(1)} %fusion.17, bf16[1024,7168]{1,0:T(8,128)(2,1)S(1)} %bitcast.32), kind=kOutput, calls=%fused_computation.5 | convolution fusion | flops 1879965696 | bytes 16777216 | tf_op jit(solution)/shard_map/dot_general | solution.py:61
  71.1 0.0 copy-start.1
  71.1 0.0 copy-start
  71.1 4.7 %all-to-all-start.1 = ((bf16[16,8,7168]{2,1,0:T(8,128)(2,1)}), bf16[16,8,7168]{2,1,0:T(8,128)(2,1)}, u32[]{:S(2)}, u32[]{:S(2)}) async-start(bf16[16,8,7168]{2,1,0:T(8,128)(2,1)} %fusion.2), calls=%async_computation.1 | async-start | bytes 3670016 | tf_op jit(solution)/shard_map/all_to_all | solution.py:65
  75.8 0.0 copy-done.1
  75.8 0.4 fusion.22
  76.2 40.5 %all-to-all-done.1 = bf16[16,8,7168]{2,1,0:T(8,128)(2,1)} async-done(((bf16[16,8,7168]{2,1,0:T(8,128)(2,1)}), bf16[16,8,7168]{2,1,0:T(8,128)(2,1)}, u32[]{:S(2)}, u32[]{:S(2)}) %all-to-all-start.1) | async-done | bytes 1835040 | tf_op jit(solution)/shard_map/all_to_all | solution.py:65
  116.7 0.0 copy-done
  116.7 4.4 %fusion = bf16[128,7168]{1,0:T(8,128)(2,1)} fusion(f32[128,128]{1,0:T(8,128)S(1)} %fusion.22, bf16[128,7168]{1,0:T(8,128)(2,1)S(1)} %copy-done, bf16[16,8,7168]{2,1,0:T(8,128)(2,1)} %all-to-all-done.1), kind=kOutput, calls=%fused_computation.1 | convolution fusion | flops 1412038656 | bytes 5570560 | tf_op jit(solution)/shard_map/dot_general | solution.py:73
  (4 shorter events, 0.0 us)
Async XLA Ops:
  6.0 56.7 %slice-start = ((s8[14680064]{0:T(1024)(128)(4,1)}), s8[4194304]{0:T(1024)(128)(4,1)S(1)}, s32[]{:S(2)}) async-start(s8[14680064]{0:T(1024)(128)(4,1)} %bitcast.29), calls=%async_computation.2 | async-start | bytes 8388608
  55.1 7.6 %slice-start.1 = ((s8[14680064]{0:T(1024)(128)(4,1)}), s8[4194304]{0:T(1024)(128)(4,1)S(1)}, s32[]{:S(2)}) async-start(s8[14680064]{0:T(1024)(128)(4,1)} %bitcast.29), calls=%async_computation.3 | async-start | bytes 8388608
  55.1 7.6 %slice-start.2 = ((s8[14680064]{0:T(1024)(128)(4,1)}), s8[4194304]{0:T(1024)(128)(4,1)S(1)}, s32[]{:S(2)}) async-start(s8[14680064]{0:T(1024)(128)(4,1)} %bitcast.29), calls=%async_computation.4 | async-start | bytes 8388608
  55.1 8.2 %slice-start.3 = ((s8[14680064]{0:T(1024)(128)(4,1)}), s8[2097152]{0:T(1024)(128)(4,1)S(1)}, s32[]{:S(2)}) async-start(s8[14680064]{0:T(1024)(128)(4,1)} %bitcast.29), calls=%async_computation.5 | async-start | bytes 4194304
  55.1 10.5 %slice-start.4 = ((s8[14680064]{0:T(1024)(128)(4,1)}), s8[4194304]{0:T(1024)(128)(4,1)S(1)}, s32[]{:S(2)}) async-start(s8[14680064]{0:T(1024)(128)(4,1)} %bitcast.31), calls=%async_computation.6 | async-start | bytes 8388608
  55.1 10.6 %slice-start.5 = ((s8[14680064]{0:T(1024)(128)(4,1)}), s8[4194304]{0:T(1024)(128)(4,1)S(1)}, s32[]{:S(2)}) async-start(s8[14680064]{0:T(1024)(128)(4,1)} %bitcast.31), calls=%async_computation.7 | async-start | bytes 8388608
  55.1 11.8 %slice-start.6 = ((s8[14680064]{0:T(1024)(128)(4,1)}), s8[4194304]{0:T(1024)(128)(4,1)S(1)}, s32[]{:S(2)}) async-start(s8[14680064]{0:T(1024)(128)(4,1)} %bitcast.31), calls=%async_computation.8 | async-start | bytes 8388608
  63.3 4.4 %slice-start.7 = ((s8[14680064]{0:T(1024)(128)(4,1)}), s8[2097152]{0:T(1024)(128)(4,1)S(1)}, s32[]{:S(2)}) async-start(s8[14680064]{0:T(1024)(128)(4,1)} %bitcast.31), calls=%async_computation.9 | async-start | bytes 4194304
  71.1 4.7 %copy-start.1 = (f32[128,1]{0,1:T(1,128)S(1)}, f32[128,1]{0,1:T(1,128)}, u32[]{:S(2)}) copy-start(f32[128,1]{0,1:T(1,128)} %param.13) | copy-start | bytes 1540
  71.1 45.6 %copy-start = (bf16[128,7168]{1,0:T(8,128)(2,1)S(1)}, bf16[128,7168]{1,0:T(8,128)(2,1)}, u32[]{:S(2)}) copy-start(bf16[128,7168]{1,0:T(8,128)(2,1)} %param.7) | copy-start | bytes 5505028
  71.1 45.6 %all-to-all-start.1 = ((bf16[16,8,7168]{2,1,0:T(8,128)(2,1)}), bf16[16,8,7168]{2,1,0:T(8,128)(2,1)}, u32[]{:S(2)}, u32[]{:S(2)}) async-start(bf16[16,8,7168]{2,1,0:T(8,128)(2,1)} %fusion.2), calls=%async_computation.1 | async-start | bytes 3670016 | tf_op jit(solution)/shard_map/all_to_all | solution.py:65
where the time goes:
time: 122 us; the launch traced here: 121 us
  blocking collectives  49.1 us (40%)
  waiting for transfers between devices  40.5 us (33%)
  matrix products  21.2 us (17%)
  starting transfers between devices  4.74 us (4%)
  local copies, waits for them, and re-layouts  2.8 us (2%)
  other arithmetic  2.63 us (2%)
    all_to_all x1, blocking collectives, per_device(): lax.all_to_all(send_all, 'ep', split_axis=0, concat_axis=0, tiled=True)  49.1 us
    all_to_all x1, waiting for transfers between devices, per_device(): lax.all_to_all(partials, 'ep', split_axis=0, concat_axis=0, tiled=True)  40.5 us
    dot_general x1, matrix products, swiglu(): gate_proj = jnp.dot(inputs, w_gate, preferred_element_type=jnp.float32)  7.56 us
    all_to_all x1, starting transfers between devices, per_device(): lax.all_to_all(partials, 'ep', split_axis=0, concat_axis=0, tiled=True)  4.74 us
    dot_general x1, matrix products, per_device(): routed = jnp.dot(gate_table, summed, precision=lax.Precision.HIGHEST)  4.42 us
    dot_general x1, matrix products, per_device(): jnp.dot(routed_hidden, expert_down, preferred_element_type=jnp.float32)  3.35 us
    unnamed x20, local copies, waits for them, and re-layouts  2.8 us
  transfers between devices with their start and end apart: 1, of which 1 were waited for; matrix products, arithmetic and copies ran while one was open for 0% of the time, Pallas kernels for 0%

commit v1 on v0

v1 whole, which is shorter than its diff:
```python
import functools

import jax
import jax.numpy as jnp
from jax import lax
from jax.experimental import pallas as pl
from jax.experimental.pallas import tpu as pltpu
from jax.sharding import PartitionSpec as P

EXPERTS = 16
CAP = 8
PAIRS = EXPERTS // 2
GROUPS = ((4, 6, 0, 1, 2), (5, 7, 3))
RING = 3
SPLIT = 2
PREP_VMEM = 12 * 2**20
HBM = pl.BlockSpec(memory_space=pltpu.HBM)
VMEM = pl.BlockSpec(memory_space=pltpu.VMEM)


def tile_of(extent, most):
    size = min(most, extent)
    while extent % size:
        size -= 128
    return size


def turned(values, axis):
    count = max(values.shape)
    spread = jnp.broadcast_to(values, (count, count))
    row_at = lax.broadcasted_iota(jnp.int32, (count, count), 0)
    column_at = lax.broadcasted_iota(jnp.int32, (count, count), 1)
    return jnp.sum(jnp.where(row_at == column_at, spread, 0.0), axis=axis, keepdims=True)


def ranks(ids_row, axis):
    count = ids_row.shape[1]
    row_at = lax.broadcasted_iota(jnp.int32, (count, count), 0)
    column_at = lax.broadcasted_iota(jnp.int32, (count, count), 1)
    same = turned(ids_row, 1) == ids_row
    before = row_at < column_at if axis == 0 else column_at < row_at
    return jnp.sum(jnp.where(same & before, 1.0, 0.0), axis=axis, keepdims=True)


def prep_kernel(shards, tokens_hbm, gain_hbm, ids_hbm, gates_hbm, *refs):
    out_refs = refs[:PAIRS]
    slot_ref, gate_ref, tokens_ref, gain_ref, ids_ref, gates_ref, sems = refs[PAIRS:]
    count, width = tokens_ref.shape
    chunk = tile_of(width, 1024)
    starts = list(range(0, width, chunk))
    pairs = [(ids_hbm, ids_ref), (gates_hbm, gates_ref), (gain_hbm, gain_ref)]
    pairs += [(tokens_hbm.at[:, pl.ds(at, chunk)], tokens_ref.at[:, pl.ds(at, chunk)]) for at in starts]
    copies = [
        pltpu.make_async_copy(source, target, sems.at[i]) for i, (source, target) in enumerate(pairs)
    ]
    for copy in copies:
        copy.start()
    mine = lax.axis_index("ep") // shards
    copies[0].wait()
    ids_row = ids_ref[...]
    rank_row = ranks(ids_row.astype(jnp.float32), 0).astype(jnp.int32)
    slot_row = (ids_row ^ mine) * CAP + rank_row
    slots = EXPERTS * CAP
    pick = (lax.broadcasted_iota(jnp.int32, (slots, count), 0) == slot_row).astype(jnp.bfloat16)
    slot_ref[...] = jnp.broadcast_to(slot_row, slot_ref.shape)
    copies[1].wait()
    gate_ref[...] = jnp.broadcast_to(gates_ref[...], gate_ref.shape)
    square_sum = jnp.zeros((count, 128), jnp.float32)
    for first, copy in zip(starts, copies[3:]):
        copy.wait()
        for lane in range(first, first + chunk, 128):
            wide = tokens_ref[:, lane : lane + 128].astype(jnp.float32)
            square_sum = square_sum + wide * wide
    scale = lax.rsqrt(jnp.sum(square_sum, axis=1, keepdims=True) / width + 1e-05)
    copies[2].wait()
    for first in starts:
        part = slice(first, first + chunk)
        wide = tokens_ref[:, part].astype(jnp.float32)
        normed = (wide * scale * gain_ref[:, part]).astype(jnp.bfloat16)
        rows = jnp.dot(pick, normed, preferred_element_type=jnp.float32).astype(jnp.bfloat16)
        for k, out_ref in enumerate(out_refs):
            out_ref[:, part] = rows[k * 2 * CAP : (k + 1) * 2 * CAP]


def prepare(tokens, gain, ids, gates, shards):
    count, width = tokens.shape
    return pl.pallas_call(
        functools.partial(prep_kernel, shards),
        in_specs=[HBM] * 4,
        out_shape=[jax.ShapeDtypeStruct((2 * CAP, width), jnp.bfloat16)] * PAIRS
        + [
            jax.ShapeDtypeStruct((8, count), jnp.int32),
            jax.ShapeDtypeStruct((8, count), jnp.float32),
        ],
        scratch_shapes=[
            pltpu.VMEM((count, width), jnp.bfloat16),
            pltpu.VMEM((1, width), jnp.float32),
            pltpu.VMEM((1, count), jnp.int32),
            pltpu.VMEM((1, count), jnp.float32),
            pltpu.SemaphoreType.DMA((width // tile_of(width, 1024) + 3,)),
        ],
        compiler_params=pltpu.CompilerParams(vmem_limit_bytes=PREP_VMEM),
        cost_estimate=pl.CostEstimate(
            flops=2 * count * count * width, bytes_accessed=4 * count * width, transcendentals=0
        ),
        name="prepare",
    )(tokens, gain, ids, gates)


def halves_kernel(count, *refs):
    out_ref = refs[-1]
    width = out_ref.shape[1]
    chunk = tile_of(width, 1024)
    for first in range(0, width, chunk):
        part = slice(first, first + chunk)
        out_ref[:, part] = jnp.concatenate(
            [ref[:, part].astype(jnp.float32)[CAP:] for ref in refs[:count]], axis=0
        ).astype(jnp.bfloat16)


def second_halves(blocks, waits=()):
    width = blocks[0].shape[1]
    return pl.pallas_call(
        functools.partial(halves_kernel, len(blocks)),
        in_specs=[VMEM] * len(blocks) + [VMEM] * len(waits),
        out_specs=VMEM,
        out_shape=jax.ShapeDtypeStruct((CAP * len(blocks), width), jnp.bfloat16),
        compiler_params=pltpu.CompilerParams(vmem_limit_bytes=12 * 2**20),
        cost_estimate=pl.CostEstimate(
            flops=0, bytes_accessed=4 * CAP * len(blocks) * width, transcendentals=0
        ),
        name="second_halves",
    )(*blocks, *waits)


def zip_kernel(waits, upper_ref, lower_ref, *refs):
    out_refs = refs[waits:]
    width = upper_ref.shape[1]
    chunk = tile_of(width, 1024)
    for first in range(0, width, chunk):
        part = slice(first, first + chunk)
        upper = upper_ref[:, part].astype(jnp.float32)
        lower = lower_ref[:, part].astype(jnp.float32)
        for k, out_ref in enumerate(out_refs):
            rows = slice(k * CAP, (k + 1) * CAP)
            both = jnp.concatenate([upper[rows], lower[rows]], axis=0)
            out_ref[:, part] = both.astype(jnp.bfloat16)


def zipped(upper, lower, waits=()):
    rows, width = upper.shape
    return pl.pallas_call(
        functools.partial(zip_kernel, len(waits)),
        in_specs=[VMEM] * 2 + [VMEM] * len(waits),
        out_specs=[VMEM] * (rows // CAP),
        out_shape=[jax.ShapeDtypeStruct((2 * CAP, width), jnp.bfloat16)] * (rows // CAP),
        compiler_params=pltpu.CompilerParams(vmem_limit_bytes=12 * 2**20),
        cost_estimate=pl.CostEstimate(flops=0, bytes_accessed=8 * rows * width, transcendentals=0),
        name="zipped",
    )(upper, lower, *waits)


def after_kernel(count, *refs):
    for block_ref, out_ref in zip(refs[:count], refs[-count:]):
        out_ref[...] = block_ref[...]


def after(blocks, waits):
    count = len(blocks)
    return pl.pallas_call(
        functools.partial(after_kernel, count),
        in_specs=[VMEM] * (count + len(waits)),
        out_specs=[VMEM] * count,
        out_shape=[jax.ShapeDtypeStruct(block.shape, block.dtype) for block in blocks],
        compiler_params=pltpu.CompilerParams(vmem_limit_bytes=12 * 2**20),
        cost_estimate=pl.CostEstimate(flops=0, bytes_accessed=0, transcendentals=0),
        name="after",
    )(*blocks, *waits)


def ffn_kernel(takes, outs, gate_hbm, up_hbm, down_hbm, *refs):
    parts = len(takes)
    x_refs, out_refs = refs[:parts], refs[parts : parts + outs]
    x_all, gate_sum, up_sum, hidden, gate_ring, up_ring, down_ring, sems = refs[
        parts + outs :
    ]
    depth, columns = gate_ring.shape[1], down_ring.shape[2]
    width = x_all.shape[1]
    up_steps, down_steps = width // depth, width // columns
    ahead = min(RING, up_steps)
    down_ahead = min(RING, down_steps)

    def up_copies(step):
        slot = lax.rem(step, RING)
        share = depth // SPLIT
        copies = []
        for part in range(SPLIT):
            rows = pl.ds(pl.multiple_of(step * depth + part * share, share), share)
            to = pl.ds(part * share, share)
            for i, (hbm, ring) in enumerate(((gate_hbm, gate_ring), (up_hbm, up_ring))):
                copies.append(
                    pltpu.make_async_copy(hbm.at[rows], ring.at[slot, to], sems.at[i, slot, part])
                )
        return copies

    def down_copies(step):
        slot = lax.rem(step, RING)
        cols = pl.ds(pl.multiple_of(step * columns, columns), columns)
        share = down_ring.shape[1] // SPLIT
        return [
            pltpu.make_async_copy(
                down_hbm.at[pl.ds(part * share, share), cols],
                down_ring.at[slot, pl.ds(part * share, share)],
                sems.at[2, slot, part],
            )
            for part in range(SPLIT)
        ]

    for step in range(ahead):
        for copy in up_copies(step):
            copy.start()
    for step in range(down_ahead):
        for copy in down_copies(step):
            copy.start()
    for first in range(0, width, depth):
        x_all[:, first : first + depth] = jnp.concatenate(
            [
                ref[:, first : first + depth].astype(jnp.float32)[:take]
                for ref, take in zip(x_refs, takes)
            ],
            axis=0,
        ).astype(jnp.bfloat16)
    gate_sum[...] = jnp.zeros_like(gate_sum)
    up_sum[...] = jnp.zeros_like(up_sum)

    def up_step(step, carry):
        for copy in up_copies(step):
            copy.wait()
        slot = lax.rem(step, RING)
        x = x_all[:, pl.ds(pl.multiple_of(step * depth, depth), depth)]
        gate_sum[...] += jnp.dot(x, gate_ring[slot], preferred_element_type=jnp.float32)
        up_sum[...] += jnp.dot(x, up_ring[slot], preferred_element_type=jnp.float32)

        @pl.when(step + RING < up_steps)
        def _():
            for copy in up_copies(step + RING):
                copy.start()

        return carry

    lax.fori_loop(0, up_steps, up_step, 0)
    gate = gate_sum[...]
    hidden[...] = (gate / (1.0 + jnp.exp(-gate)) * up_sum[...]).astype(jnp.bfloat16)

    def down_step(step, carry):
        for copy in down_copies(step):
            copy.wait()
        part = jnp.dot(
            hidden[...], down_ring[lax.rem(step, RING)], preferred_element_type=jnp.float32
        )
        at = pl.ds(pl.multiple_of(step * columns, columns), columns)
        low = 0
        for out_ref in out_refs:
            rows = out_ref.shape[0]
            out_ref[:, at] = part[low : low + rows].astype(jnp.bfloat16)
            low += rows

        @pl.when(step + RING < down_steps)
        def _():
            for copy in down_copies(step + RING):
                copy.start()

        return carry

    lax.fori_loop(0, down_steps, down_step, 0)


def ffn(x_list, takes, out_rows, gate, up, down):
    parts = len(x_list)
    width = x_list[0].shape[1]
    units = gate.shape[1]
    depth = tile_of(width, 1024)
    columns = tile_of(width, 1024)
    total = sum(takes)
    return pl.pallas_call(
        functools.partial(ffn_kernel, takes, len(out_rows)),
        in_specs=[HBM] * 3 + [VMEM] * parts,
        out_specs=[VMEM] * len(out_rows),
        out_shape=[jax.ShapeDtypeStruct((rows, width), jnp.bfloat16) for rows in out_rows],
        scratch_shapes=[
            pltpu.VMEM((total, width), jnp.bfloat16),
            pltpu.VMEM((total, units), jnp.float32),
            pltpu.VMEM((total, units), jnp.float32),
            pltpu.VMEM((total, units), jnp.bfloat16),
            pltpu.VMEM((RING, depth, units), jnp.bfloat16),
            pltpu.VMEM((RING, depth, units), jnp.bfloat16),
            pltpu.VMEM((RING, units, columns), jnp.bfloat16),
            pltpu.SemaphoreType.DMA((3, RING, SPLIT)),
        ],
        compiler_params=pltpu.CompilerParams(vmem_limit_bytes=8 * 2**20 + 6 * RING * depth * units + 8 * total * width),
        cost_estimate=pl.CostEstimate(
            flops=6 * total * width * units,
            bytes_accessed=6 * width * units + 4 * total * width,
            transcendentals=total * units,
        ),
        name="ffn",
    )(gate, up, down, *x_list)


def combine_kernel(tokens_ref, slot_ref, gates_ref, *refs):
    back_refs, out_hbm, staged, sems = refs[:-3], refs[-3], refs[-2], refs[-1]
    count, width = tokens_ref.shape
    chunk = tile_of(width, 1024)
    slot = turned(slot_ref[0:1].astype(jnp.float32), 1).astype(jnp.int32)
    gates = turned(gates_ref[0:1], 1)
    slots = EXPERTS * CAP
    table = (lax.broadcasted_iota(jnp.int32, (count, slots), 1) == slot).astype(jnp.bfloat16)
    copies = []
    for i, first in enumerate(range(0, width, chunk)):
        part = slice(first, first + chunk)
        back = jnp.concatenate([ref[:, part] for ref in back_refs], axis=0)
        summed = jnp.dot(table, back, preferred_element_type=jnp.float32)
        wide = tokens_ref[:, part].astype(jnp.float32)
        staged[:, part] = (wide + gates * summed).astype(jnp.bfloat16)
        copies.append(
            pltpu.make_async_copy(
                staged.at[:, pl.ds(first, chunk)], out_hbm.at[:, pl.ds(first, chunk)], sems.at[i]
            )
        )
        copies[-1].start()
    for copy in copies:
        copy.wait()


def combine(tokens, slot_row, gates_row, back_list):
    count, width = tokens.shape
    return pl.pallas_call(
        combine_kernel,
        in_specs=[VMEM] * (3 + len(back_list)),
        out_specs=HBM,
        out_shape=jax.ShapeDtypeStruct((count, width), jnp.bfloat16),
        scratch_shapes=[
            pltpu.VMEM((count, width), jnp.bfloat16),
            pltpu.SemaphoreType.DMA((width // tile_of(width, 1024),)),
        ],
        compiler_params=pltpu.CompilerParams(vmem_limit_bytes=16 * 2**20),
        cost_estimate=pl.CostEstimate(
            flops=2 * count * count * width, bytes_accessed=6 * count * width, transcendentals=0
        ),
        name="combine",
    )(tokens, slot_row, gates_row, *back_list)


def per_device(tokens, norm_gain, expert_gate, expert_up, expert_down, route_ids, route_gates):
    devices = lax.axis_size("ep")
    shards = devices // EXPERTS
    count, width = tokens.shape
    weights = (expert_gate, expert_up, expert_down)
    holders = [[e * shards + s for s in range(shards)] for e in range(EXPERTS)]

    def across(block, k):
        if k == 0:
            return block
        pairs = [(d, (d // shards ^ k) * shards + d % shards) for d in range(devices)]
        return lax.ppermute(block, "ep", pairs)

    def expert(blocks, swapped):
        half = swapped.shape[0]
        takes = [CAP] * len(blocks) + [half]
        if shards == 1:
            return ffn(blocks + [swapped], takes, [half, half], *weights)
        rows = jnp.concatenate([block[:CAP] for block in blocks] + [swapped], axis=0)
        rows = lax.all_gather(rows, "ep", axis_index_groups=holders, tiled=True)
        (part,) = ffn([rows], [rows.shape[0]], [rows.shape[0]], *weights)
        part = lax.all_to_all(part, "ep", 0, 0, axis_index_groups=holders, tiled=True)
        part = part.reshape(shards, 2 * half, width).astype(jnp.float32)
        part = jnp.sum(part, axis=0).astype(jnp.bfloat16)
        return part[:half], part[half:]

    ids_row = route_ids.reshape(1, count)
    gates_row = route_gates.reshape(1, count)
    *sent, slot_row, gates_row = prepare(
        tokens, norm_gain.reshape(1, width), ids_row, gates_row, shards
    )
    early, late = GROUPS
    held = {m: across(sent[m], 2 * m) for m in early}
    later = after([sent[m] for m in late], [held[early[0]]])
    held.update({m: across(block, 2 * m) for m, block in zip(late, later)})
    back = {}
    for group in GROUPS:
        blocks = [held[m] for m in group]
        swapped = across(second_halves(blocks), 1)
        own, other = expert(blocks, swapped)
        waits = [held[m] for m in late] if group is early else [back[m] for m in early[:2]]
        (other,) = after([other], waits)
        blocks = dict(zip(group, zipped(own, across(other, 1))))
        if group is early:
            last = {m: blocks.pop(m) for m in early[2:]}
        else:
            near = [m for m in last if m]
            moved = after([last[m] for m in near], [blocks[late[0]]])
            blocks.update(zip(near, moved))
            blocks.update({m: block for m, block in last.items() if not m})
        back.update({m: across(block, 2 * m) for m, block in blocks.items()})
    return combine(tokens, slot_row, gates_row, [back[m] for m in range(PAIRS)])


def solution(mesh):
    in_specs = (
        P(("groups", "ep"), None),
        P(),
        P(None, "ep"),
        P(None, "ep"),
        P("ep", None),
        P(("groups", "ep"), None),
        P(("groups", "ep"), None),
    )
    out_specs = P(("groups", "ep"), None)
    return jax.shard_map(
        per_device, mesh=mesh, in_specs=in_specs, out_specs=out_specs, check_vma=False
    )
```

time: 122 us -> 112 us (0.918)
  the two profiles are of different devices: /device:TPU:9 before, /device:TPU:0 now
where the time goes in v1:
time: 112 us
  waiting for transfers between devices  39.4 us (35%)
  starting transfers between devices  31.8 us (28%)
  Pallas kernels  31.7 us (28%)
  local copies, waits for them, and re-layouts  8.74 us (8%)
    ppermute x18, waiting for transfers between devices, across(): return lax.ppermute(block, 'ep', pairs)  39.4 us
    ppermute x18, starting transfers between devices, across(): return lax.ppermute(block, 'ep', pairs)  31.8 us
    pallas_call x2, Pallas kernels, ffn(): pl.pallas_call(functools.partial(ffn_kernel, takes, len(out_rows)), in_sp...  28.3 us
    unnamed x14, local copies, waits for them, and re-layouts  8.74 us
  transfers between devices with their start and end apart: 18, of which 8 were waited for; matrix products, arithmetic and copies ran while one was open for 0% of the time, Pallas kernels for 25%

profile of v1, /device:TPU:0, one launch (start us, length us, event | category | flops | bytes accessed | tf_op | source)
XLA Modules:
  0.0 111.8 jit_solution(14024144941694507793)
XLA Ops:
  0.0 0.0 copy-start.2
  0.0 1.5 %copy-done.2 = bf16[128,7168]{1,0:T(8,128)(2,1)S(1)} copy-done((bf16[128,7168]{1,0:T(8,128)(2,1)S(1)}, bf16[128,7168]{1,0:T(8,128)(2,1)}, u32[]{:S(2)}) %copy-start.2) | copy-done | bytes 1835032
  1.5 0.0 copy-start.4
  1.5 0.7 copy-done.4
  2.2 0.0 copy-start.5
  2.3 0.7 copy-done.5
  2.9 0.0 copy-start.6
  2.9 0.7 copy-done.6
  3.6 1.5 %prepare.1 = (bf16[16,7168]{1,0:T(8,128)(2,1)S(1)}, bf16[16,7168]{1,0:T(8,128)(2,1)S(1)}, bf16[16,7168]{1,0:T(8,128)(2,1)S(1)}, bf16[16,7168]{1,0:T(8,128)(2,1)S...) custom-call(bf16[128,7168]{1,0:T(8,128)(2,1)S(1)} %copy-done.2, ...), custom_call_target="tpu_custom_call" | custom-call | flops 234881024 | bytes 3670016 | tf_op jit(solution)/shard_map/prepare/pallas_call | solution.py:87
  5.0 4.1 %collective-permute-start = (bf16[16,7168]{1,0:T(8,128)(2,1)S(1)}, bf16[16,7168]{1,0:T(8,128)(2,1)S(1)}, u32[]{:S(2)}, u32[]{:S(2)}) collective-permute-start(bf16[16,7168]{1,0:T(8,128)(2,1)S(1)} %get-tuple-element.34), channel_id=1, source_target_pairs={{0,8},{1,9},{2,10},{3,11},{4,12},{5,13},{6,14},{7,15},{8,0},{9,1},... | collective-permute-start | bytes 688136 | tf_op jit(solution)/shard_map/ppermute | solution.py:365
  9.1 1.3 %collective-permute-start.1 = (bf16[16,7168]{1,0:T(8,128)(2,1)S(1)}, bf16[16,7168]{1,0:T(8,128)(2,1)S(1)}, u32[]{:S(2)}, u32[]{:S(2)}) collective-permute-start(bf16[16,7168]{1,0:T(8,128)(2,1)S(1)} %get-tuple-element.35), channel_id=1, source_target_pairs={{0,12},{1,13},{2,14},{3,15},{4,8},{5,9},{6,10},{7,11},{8,4},{9,5},... | collective-permute-start | bytes 688136 | tf_op jit(solution)/shard_map/ppermute | solution.py:365
  10.5 1.5 %collective-permute-start.2 = (bf16[16,7168]{1,0:T(8,128)(2,1)S(1)}, bf16[16,7168]{1,0:T(8,128)(2,1)S(1)}, u32[]{:S(2)}, u32[]{:S(2)}) collective-permute-start(bf16[16,7168]{1,0:T(8,128)(2,1)S(1)} %get-tuple-element.37), channel_id=1, source_target_pairs={{0,2},{1,3},{2,0},{3,1},{4,6},{5,7},{6,4},{7,5},{8,10},{9,11},{10,... | collective-permute-start | bytes 688136 | tf_op jit(solution)/shard_map/ppermute | solution.py:365
  12.0 0.2 collective-permute-start.3
  12.2 13.2 %collective-permute-done.refs_0_.refs_3_ = bf16[16,7168]{1,0:T(8,128)(2,1)S(1)} collective-permute-done((bf16[16,7168]{1,0:T(8,128)(2,1)S(1)}, bf16[16,7168]{1,0:T(8,128)(2,1)S(1)}, u32[]{:S(2)}, u32[]{:S(2)}) %collective-permute-start) | collective-permute-done | bytes 229408 | tf_op jit(solution)/shard_map/ppermute | solution.py:365
  25.5 0.0 collective-permute-done.1.refs_1_
  25.5 0.0 collective-permute-done.2.refs_3_
  25.5 1.7 %collective-permute-done.3.refs_4_ = bf16[16,7168]{1,0:T(8,128)(2,1)S(1)} collective-permute-done((bf16[16,7168]{1,0:T(8,128)(2,1)S(1)}, bf16[16,7168]{1,0:T(8,128)(2,1)S(1)}, u32[]{:S(2)}, u32[]{:S(2)}) %collective-permute-start.3) | collective-permute-done | bytes 229408 | tf_op jit(solution)/shard_map/ppermute | solution.py:365
  27.2 0.1 collective-permute-start.4
  27.4 6.0 %collective-permute-start.5 = (bf16[16,7168]{1,0:T(8,128)(2,1)S(1)}, bf16[16,7168]{1,0:T(8,128)(2,1)S(1)}, u32[]{:S(2)}, u32[]{:S(2)}) collective-permute-start(bf16[16,7168]{1,0:T(8,128)(2,1)S(1)} %get-tuple-element.44), channel_id=1, source_target_pairs={{0,10},{1,11},{2,8},{3,9},{4,14},{5,15},{6,12},{7,13},{8,2},{9,3},... | collective-permute-start | bytes 688136 | tf_op jit(solution)/shard_map/ppermute | solution.py:365
  33.4 0.4 collective-permute-start.6
  33.8 0.2 collective-permute-start.7
  34.0 0.0 collective-permute-done.4.refs_5_
  34.0 0.0 copy-start
  34.0 5.2 %copy-done = bf16[7168,1024]{1,0:T(8,128)(2,1)S(1)} copy-done((bf16[7168,1024]{1,0:T(8,128)(2,1)S(1)}, bf16[7168,1024]{1,0:T(8,128)(2,1)}, u32[]{:S(2)}) %copy-start) | copy-done | bytes 14680088
  39.2 0.0 copy-start.1
  39.2 14.6 %ffn.2 = (bf16[40,7168]{1,0:T(8,128)(2,1)S(1)}, bf16[40,7168]{1,0:T(8,128)(2,1)S(1)}) custom-call(bf16[7168,1024]{1,0:T(8,128)(2,1)S(1)} %copy-done, bf16[7168,1024]{1,0:T(8,128)(2,1)} %up_hbm.3, bf16[1024,7168]{1,0:T(8,128)(2,1)} %down_hbm.3, bf16[16,7168]{1,0:T(8,128)(2,1)S(1)} %collective-permute-done.refs_0_.refs_3_, ...), custom_call_target="tpu_custom_call" | custom-call | flops 3523215360 | bytes 46333952 | tf_op jit(solution)/shard_map/ffn/pallas_call | solution.py:285
  53.7 0.0 collective-permute-done.5.refs_1_.refs_0_
  53.7 0.0 collective-permute-done.6.refs_2_.refs_1_
  53.8 0.0 collective-permute-done.7.refs_3_.refs_2_
  53.8 0.1 collective-permute-start.8
  53.9 0.6 collective-permute-start.9
  54.5 1.4 %collective-permute-done.8.lower_ref = bf16[40,7168]{1,0:T(8,128)(2,1)S(1)} collective-permute-done((bf16[40,7168]{1,0:T(8,128)(2,1)S(1)}, bf16[40,7168]{1,0:T(8,128)(2,1)S(1)}, u32[]{:S(2)}, u32[]{:S(2)}) %collective-permute-start.8) | collective-permute-done | bytes 573472 | tf_op jit(solution)/shard_map/ppermute | solution.py:365
  55.9 0.1 zipped.2
  55.9 4.7 %collective-permute-start.10 = (bf16[16,7168]{1,0:T(8,128)(2,1)S(1)}, bf16[16,7168]{1,0:T(8,128)(2,1)S(1)}, u32[]{:S(2)}, u32[]{:S(2)}) collective-permute-start(bf16[16,7168]{1,0:T(8,128)(2,1)S(1)} %get-tuple-element.52), channel_id=1, source_target_pairs={{0,8},{1,9},{2,10},{3,11},{4,12},{5,13},{6,14},{7,15},{8,0},{9,1},... | collective-permute-start | bytes 688136 | tf_op jit(solution)/shard_map/ppermute | solution.py:365
  60.7 0.0 copy-start.3
  60.7 0.4 collective-permute-start.11
  61.1 0.0 collective-permute-done.9.refs_3_
  61.1 0.0 copy-done.1
  61.1 13.7 %ffn.3 = (bf16[24,7168]{1,0:T(8,128)(2,1)S(1)}, bf16[24,7168]{1,0:T(8,128)(2,1)S(1)}) custom-call(bf16[7168,1024]{1,0:T(8,128)(2,1)S(1)} %copy-done.1, bf16[7168,1024]{1,0:T(8,128)(2,1)} %up_hbm.3, bf16[1024,7168]{1,0:T(8,128)(2,1)} %down_hbm.3, bf16[16,7168]{1,0:T(8,128)(2,1)S(1)} %collective-permute-done.5.refs_1_.refs_0_, ...), custom_call_target="tpu_custom_call" | custom-call | flops 2113929216 | bytes 45416448 | tf_op jit(solution)/shard_map/ffn/pallas_call | solution.py:285
  74.9 1.8 %collective-permute-done.10.refs_1_.refs_4_ = bf16[16,7168]{1,0:T(8,128)(2,1)S(1)} collective-permute-done((bf16[16,7168]{1,0:T(8,128)(2,1)S(1)}, bf16[16,7168]{1,0:T(8,128)(2,1)S(1)}, u32[]{:S(2)}, u32[]{:S(2)}) %collective-permute-start.10) | collective-permute-done | bytes 229408 | tf_op jit(solution)/shard_map/ppermute | solution.py:365
  76.7 0.0 collective-permute-done.11.refs_2_.refs_6_
  76.7 0.1 collective-permute-start.12
  76.8 1.6 %collective-permute-done.12.lower_ref = bf16[24,7168]{1,0:T(8,128)(2,1)S(1)} collective-permute-done((bf16[24,7168]{1,0:T(8,128)(2,1)S(1)}, bf16[24,7168]{1,0:T(8,128)(2,1)S(1)}, u32[]{:S(2)}, u32[]{:S(2)}) %collective-permute-start.12) | collective-permute-done | bytes 344096 | tf_op jit(solution)/shard_map/ppermute | solution.py:365
  78.5 5.9 %collective-permute-start.16 = (bf16[16,7168]{1,0:T(8,128)(2,1)S(1)}, bf16[16,7168]{1,0:T(8,128)(2,1)S(1)}, u32[]{:S(2)}, u32[]{:S(2)}) collective-permute-start(bf16[16,7168]{1,0:T(8,128)(2,1)S(1)} %get-tuple-element.54.refs_2_), channel_id=1, source_target_pairs={{0,10},{1,11},{2,8},{3,9},{4,14},{5,15},{6,12},{7,13},{8,2},{9,3},... | collective-permute-start | bytes 688136 | tf_op jit(solution)/shard_map/ppermute | solution.py:365
  84.4 0.6 collective-permute-start.13
  85.0 0.0 collective-permute-start.14
  85.0 2.9 %collective-permute-start.15 = (bf16[16,7168]{1,0:T(8,128)(2,1)S(1)}, bf16[16,7168]{1,0:T(8,128)(2,1)S(1)}, u32[]{:S(2)}, u32[]{:S(2)}) collective-permute-start(bf16[16,7168]{1,0:T(8,128)(2,1)S(1)} %get-tuple-element.57), channel_id=1, source_target_pairs={{0,6},{1,7},{2,4},{3,5},{4,2},{5,3},{6,0},{7,1},{8,14},{9,15},{10,... | collective-permute-start | bytes 688136 | tf_op jit(solution)/shard_map/ppermute | solution.py:365
  88.0 2.6 %collective-permute-start.17 = (bf16[16,7168]{1,0:T(8,128)(2,1)S(1)}, bf16[16,7168]{1,0:T(8,128)(2,1)S(1)}, u32[]{:S(2)}, u32[]{:S(2)}) collective-permute-start(bf16[16,7168]{1,0:T(8,128)(2,1)S(1)} %get-tuple-element.58), channel_id=1, source_target_pairs={{0,14},{1,15},{2,12},{3,13},{4,10},{5,11},{6,8},{7,9},{8,6},{9,7},... | collective-permute-start | bytes 688136 | tf_op jit(solution)/shard_map/ppermute | solution.py:365
  90.6 5.8 %collective-permute-done.13.refs_1_ = bf16[16,7168]{1,0:T(8,128)(2,1)S(1)} collective-permute-done((bf16[16,7168]{1,0:T(8,128)(2,1)S(1)}, bf16[16,7168]{1,0:T(8,128)(2,1)S(1)}, u32[]{:S(2)}, u32[]{:S(2)}) %collective-permute-start.13) | collective-permute-done | bytes 229408 | tf_op jit(solution)/shard_map/ppermute | solution.py:365
  96.4 0.0 collective-permute-done.14.refs_2_
  96.4 6.6 %collective-permute-done.15.refs_3_ = bf16[16,7168]{1,0:T(8,128)(2,1)S(1)} collective-permute-done((bf16[16,7168]{1,0:T(8,128)(2,1)S(1)}, bf16[16,7168]{1,0:T(8,128)(2,1)S(1)}, u32[]{:S(2)}, u32[]{:S(2)}) %collective-permute-start.15) | collective-permute-done | bytes 229408 | tf_op jit(solution)/shard_map/ppermute | solution.py:365
  103.0 0.0 collective-permute-done.16.refs_5_
  103.0 7.2 %collective-permute-done.17.refs_7_ = bf16[16,7168]{1,0:T(8,128)(2,1)S(1)} collective-permute-done((bf16[16,7168]{1,0:T(8,128)(2,1)S(1)}, bf16[16,7168]{1,0:T(8,128)(2,1)S(1)}, u32[]{:S(2)}, u32[]{:S(2)}) %collective-permute-start.17) | collective-permute-done | bytes 229408 | tf_op jit(solution)/shard_map/ppermute | solution.py:365
  110.2 0.0 copy-done.3
  110.2 1.6 %combine.1 = bf16[128,7168]{1,0:T(8,128)(2,1)} custom-call(bf16[128,7168]{1,0:T(8,128)(2,1)S(1)} %copy-done.3, s32[8,128]{1,0:T(8,128)S(1)} %get-tuple-element.32.slot_ref, f32[8,128]{1,0:T(8,128)S(1)} %get-tuple-element.33.gates_ref, bf16[16,7168]{1,0:T(8,128)(2,1)S(1)} %get-tuple-element.47.refs_0_, bf16[16,7168]{1,0:T(8,128)(2,1)S(1)} %collective-permute-done.13.refs_1_, ...), custom_call_target="tpu_custom_call" | custom-call | flops 234881024 | bytes 5505024 | tf_op jit(solution)/shard_map/combine/pallas_call | solution.py:337
  (7 shorter events, 0.2 us)
Async XLA Ops:
  0.0 1.5 %copy-start.2 = (bf16[128,7168]{1,0:T(8,128)(2,1)S(1)}, bf16[128,7168]{1,0:T(8,128)(2,1)}, u32[]{:S(2)}) copy-start(bf16[128,7168]{1,0:T(8,128)(2,1)} %tokens_ref.1) | copy-start | bytes 5505028
  1.5 0.7 copy-start.4
  2.2 0.7 copy-start.5
  2.9 0.7 copy-start.6
  5.0 20.4 %collective-permute-start = (bf16[16,7168]{1,0:T(8,128)(2,1)S(1)}, bf16[16,7168]{1,0:T(8,128)(2,1)S(1)}, u32[]{:S(2)}, u32[]{:S(2)}) collective-permute-start(bf16[16,7168]{1,0:T(8,128)(2,1)S(1)} %get-tuple-element.34), channel_id=1, source_target_pairs={{0,8},{1,9},{2,10},{3,11},{4,12},{5,13},{6,14},{7,15},{8,0},{9,1},... | collective-permute-start | bytes 688136 | tf_op jit(solution)/shard_map/ppermute | solution.py:365
  9.1 16.3 %collective-permute-start.1 = (bf16[16,7168]{1,0:T(8,128)(2,1)S(1)}, bf16[16,7168]{1,0:T(8,128)(2,1)S(1)}, u32[]{:S(2)}, u32[]{:S(2)}) collective-permute-start(bf16[16,7168]{1,0:T(8,128)(2,1)S(1)} %get-tuple-element.35), channel_id=1, source_target_pairs={{0,12},{1,13},{2,14},{3,15},{4,8},{5,9},{6,10},{7,11},{8,4},{9,5},... | collective-permute-start | bytes 688136 | tf_op jit(solution)/shard_map/ppermute | solution.py:365
  10.5 15.0 %collective-permute-start.2 = (bf16[16,7168]{1,0:T(8,128)(2,1)S(1)}, bf16[16,7168]{1,0:T(8,128)(2,1)S(1)}, u32[]{:S(2)}, u32[]{:S(2)}) collective-permute-start(bf16[16,7168]{1,0:T(8,128)(2,1)S(1)} %get-tuple-element.37), channel_id=1, source_target_pairs={{0,2},{1,3},{2,0},{3,1},{4,6},{5,7},{6,4},{7,5},{8,10},{9,11},{10,... | collective-permute-start | bytes 688136 | tf_op jit(solution)/shard_map/ppermute | solution.py:365
  12.0 15.2 %collective-permute-start.3 = (bf16[16,7168]{1,0:T(8,128)(2,1)S(1)}, bf16[16,7168]{1,0:T(8,128)(2,1)S(1)}, u32[]{:S(2)}, u32[]{:S(2)}) collective-permute-start(bf16[16,7168]{1,0:T(8,128)(2,1)S(1)} %get-tuple-element.38), channel_id=1, source_target_pairs={{0,4},{1,5},{2,6},{3,7},{4,0},{5,1},{6,2},{7,3},{8,12},{9,13},{10,... | collective-permute-start | bytes 688136 | tf_op jit(solution)/shard_map/ppermute | solution.py:365
  27.2 6.8 %collective-permute-start.4 = (bf16[40,7168]{1,0:T(8,128)(2,1)S(1)}, bf16[40,7168]{1,0:T(8,128)(2,1)S(1)}, u32[]{:S(2)}, u32[]{:S(2)}) collective-permute-start(bf16[40,7168]{1,0:T(8,128)(2,1)S(1)} %second_halves.2), channel_id=1, source_target_pairs={{0,1},{1,0},{2,3},{3,2},{4,5},{5,4},{6,7},{7,6},{8,9},{9,8},{10,11... | collective-permute-start | bytes 1720328 | tf_op jit(solution)/shard_map/ppermute | solution.py:365
  27.4 26.4 %collective-permute-start.5 = (bf16[16,7168]{1,0:T(8,128)(2,1)S(1)}, bf16[16,7168]{1,0:T(8,128)(2,1)S(1)}, u32[]{:S(2)}, u32[]{:S(2)}) collective-permute-start(bf16[16,7168]{1,0:T(8,128)(2,1)S(1)} %get-tuple-element.44), channel_id=1, source_target_pairs={{0,10},{1,11},{2,8},{3,9},{4,14},{5,15},{6,12},{7,13},{8,2},{9,3},... | collective-permute-start | bytes 688136 | tf_op jit(solution)/shard_map/ppermute | solution.py:365
  33.4 20.4 %collective-permute-start.6 = (bf16[16,7168]{1,0:T(8,128)(2,1)S(1)}, bf16[16,7168]{1,0:T(8,128)(2,1)S(1)}, u32[]{:S(2)}, u32[]{:S(2)}) collective-permute-start(bf16[16,7168]{1,0:T(8,128)(2,1)S(1)} %get-tuple-element.45), channel_id=1, source_target_pairs={{0,14},{1,15},{2,12},{3,13},{4,10},{5,11},{6,8},{7,9},{8,6},{9,7},... | collective-permute-start | bytes 688136 | tf_op jit(solution)/shard_map/ppermute | solution.py:365
  33.8 20.0 %collective-permute-start.7 = (bf16[16,7168]{1,0:T(8,128)(2,1)S(1)}, bf16[16,7168]{1,0:T(8,128)(2,1)S(1)}, u32[]{:S(2)}, u32[]{:S(2)}) collective-permute-start(bf16[16,7168]{1,0:T(8,128)(2,1)S(1)} %get-tuple-element.46), channel_id=1, source_target_pairs={{0,6},{1,7},{2,4},{3,5},{4,2},{5,3},{6,0},{7,1},{8,14},{9,15},{10,... | collective-permute-start | bytes 688136 | tf_op jit(solution)/shard_map/ppermute | solution.py:365
  34.0 5.2 %copy-start = (bf16[7168,1024]{1,0:T(8,128)(2,1)S(1)}, bf16[7168,1024]{1,0:T(8,128)(2,1)}, u32[]{:S(2)}) copy-start(bf16[7168,1024]{1,0:T(8,128)(2,1)} %gate_hbm.3) | copy-start | bytes 44040196
  39.2 22.0 %copy-start.1 = (bf16[7168,1024]{1,0:T(8,128)(2,1)S(1)}, bf16[7168,1024]{1,0:T(8,128)(2,1)}, u32[]{:S(2)}) copy-start(bf16[7168,1024]{1,0:T(8,128)(2,1)} %gate_hbm.3) | copy-start | bytes 44040196
  53.8 2.0 %collective-permute-start.8 = (bf16[40,7168]{1,0:T(8,128)(2,1)S(1)}, bf16[40,7168]{1,0:T(8,128)(2,1)S(1)}, u32[]{:S(2)}, u32[]{:S(2)}) collective-permute-start(bf16[40,7168]{1,0:T(8,128)(2,1)S(1)} %after.5), channel_id=1, source_target_pairs={{0,1},{1,0},{2,3},{3,2},{4,5},{5,4},{6,7},{7,6},{8,9},{9,8},{10,11... | collective-permute-start | bytes 1720328 | tf_op jit(solution)/shard_map/ppermute | solution.py:365
  53.9 7.2 %collective-permute-start.9 = (bf16[24,7168]{1,0:T(8,128)(2,1)S(1)}, bf16[24,7168]{1,0:T(8,128)(2,1)S(1)}, u32[]{:S(2)}, u32[]{:S(2)}) collective-permute-start(bf16[24,7168]{1,0:T(8,128)(2,1)S(1)} %second_halves.3), channel_id=1, source_target_pairs={{0,1},{1,0},{2,3},{3,2},{4,5},{5,4},{6,7},{7,6},{8,9},{9,8},{10,11... | collective-permute-start | bytes 1032200 | tf_op jit(solution)/shard_map/ppermute | solution.py:365
  55.9 20.7 %collective-permute-start.10 = (bf16[16,7168]{1,0:T(8,128)(2,1)S(1)}, bf16[16,7168]{1,0:T(8,128)(2,1)S(1)}, u32[]{:S(2)}, u32[]{:S(2)}) collective-permute-start(bf16[16,7168]{1,0:T(8,128)(2,1)S(1)} %get-tuple-element.52), channel_id=1, source_target_pairs={{0,8},{1,9},{2,10},{3,11},{4,12},{5,13},{6,14},{7,15},{8,0},{9,1},... | collective-permute-start | bytes 688136 | tf_op jit(solution)/shard_map/ppermute | solution.py:365
  60.7 49.5 %copy-start.3 = (bf16[128,7168]{1,0:T(8,128)(2,1)S(1)}, bf16[128,7168]{1,0:T(8,128)(2,1)}, u32[]{:S(2)}) copy-start(bf16[128,7168]{1,0:T(8,128)(2,1)} %tokens_ref.1) | copy-start | bytes 5505028
  60.7 16.0 %collective-permute-start.11 = (bf16[16,7168]{1,0:T(8,128)(2,1)S(1)}, bf16[16,7168]{1,0:T(8,128)(2,1)S(1)}, u32[]{:S(2)}, u32[]{:S(2)}) collective-permute-start(bf16[16,7168]{1,0:T(8,128)(2,1)S(1)} %get-tuple-element.53), channel_id=1, source_target_pairs={{0,12},{1,13},{2,14},{3,15},{4,8},{5,9},{6,10},{7,11},{8,4},{9,5},... | collective-permute-start | bytes 688136 | tf_op jit(solution)/shard_map/ppermute | solution.py:365
  76.7 1.7 %collective-permute-start.12 = (bf16[24,7168]{1,0:T(8,128)(2,1)S(1)}, bf16[24,7168]{1,0:T(8,128)(2,1)S(1)}, u32[]{:S(2)}, u32[]{:S(2)}) collective-permute-start(bf16[24,7168]{1,0:T(8,128)(2,1)S(1)} %after.6), channel_id=1, source_target_pairs={{0,1},{1,0},{2,3},{3,2},{4,5},{5,4},{6,7},{7,6},{8,9},{9,8},{10,11... | collective-permute-start | bytes 1032200 | tf_op jit(solution)/shard_map/ppermute | solution.py:365
  78.5 24.5 %collective-permute-start.16 = (bf16[16,7168]{1,0:T(8,128)(2,1)S(1)}, bf16[16,7168]{1,0:T(8,128)(2,1)S(1)}, u32[]{:S(2)}, u32[]{:S(2)}) collective-permute-start(bf16[16,7168]{1,0:T(8,128)(2,1)S(1)} %get-tuple-element.54.refs_2_), channel_id=1, source_target_pairs={{0,10},{1,11},{2,8},{3,9},{4,14},{5,15},{6,12},{7,13},{8,2},{9,3},... | collective-permute-start | bytes 688136 | tf_op jit(solution)/shard_map/ppermute | solution.py:365
  84.4 12.0 %collective-permute-start.13 = (bf16[16,7168]{1,0:T(8,128)(2,1)S(1)}, bf16[16,7168]{1,0:T(8,128)(2,1)S(1)}, u32[]{:S(2)}, u32[]{:S(2)}) collective-permute-start(bf16[16,7168]{1,0:T(8,128)(2,1)S(1)} %get-tuple-element.55), channel_id=1, source_target_pairs={{0,2},{1,3},{2,0},{3,1},{4,6},{5,7},{6,4},{7,5},{8,10},{9,11},{10,... | collective-permute-start | bytes 688136 | tf_op jit(solution)/shard_map/ppermute | solution.py:365
  85.0 11.4 %collective-permute-start.14 = (bf16[16,7168]{1,0:T(8,128)(2,1)S(1)}, bf16[16,7168]{1,0:T(8,128)(2,1)S(1)}, u32[]{:S(2)}, u32[]{:S(2)}) collective-permute-start(bf16[16,7168]{1,0:T(8,128)(2,1)S(1)} %get-tuple-element.56), channel_id=1, source_target_pairs={{0,4},{1,5},{2,6},{3,7},{4,0},{5,1},{6,2},{7,3},{8,12},{9,13},{10,... | collective-permute-start | bytes 688136 | tf_op jit(solution)/shard_map/ppermute | solution.py:365
  85.0 18.0 %collective-permute-start.15 = (bf16[16,7168]{1,0:T(8,128)(2,1)S(1)}, bf16[16,7168]{1,0:T(8,128)(2,1)S(1)}, u32[]{:S(2)}, u32[]{:S(2)}) collective-permute-start(bf16[16,7168]{1,0:T(8,128)(2,1)S(1)} %get-tuple-element.57), channel_id=1, source_target_pairs={{0,6},{1,7},{2,4},{3,5},{4,2},{5,3},{6,0},{7,1},{8,14},{9,15},{10,... | collective-permute-start | bytes 688136 | tf_op jit(solution)/shard_map/ppermute | solution.py:365
  88.0 22.3 %collective-permute-start.17 = (bf16[16,7168]{1,0:T(8,128)(2,1)S(1)}, bf16[16,7168]{1,0:T(8,128)(2,1)S(1)}, u32[]{:S(2)}, u32[]{:S(2)}) collective-permute-start(bf16[16,7168]{1,0:T(8,128)(2,1)S(1)} %get-tuple-element.58), channel_id=1, source_target_pairs={{0,14},{1,15},{2,12},{3,13},{4,10},{5,11},{6,8},{7,9},{8,6},{9,7},... | collective-permute-start | bytes 688136 | tf_op jit(solution)/shard_map/ppermute | solution.py:365

commit v2 on v1

--- a/solution.py
+++ b/solution.py
@@ -10,7 +10,14 @@
 EXPERTS = 16
 CAP = 8
 PAIRS = EXPERTS // 2
-GROUPS = ((4, 6, 0, 1, 2), (5, 7, 3))
+PAIRED = ((4, 2, 1, 0), (5, 3))
+SINGLE = ((12, 13), (14, 15))
+BLOCKS = sorted(
+    [(2 * m, 2, ("p", m)) for group in PAIRED for m in group]
+    + [(k, 1, ("s", k)) for group in SINGLE for k in group]
+)
+FORWARD = (("p", 5), ("p", 3), ("s", 14), ("s", 15))
+RETURN = (("p", 2), ("s", 12), ("p", 4))
 RING = 3
 SPLIT = 2
 PREP_VMEM = 12 * 2**20
@@ -43,8 +50,8 @@
 
 
 def prep_kernel(shards, tokens_hbm, gain_hbm, ids_hbm, gates_hbm, *refs):
-    out_refs = refs[:PAIRS]
-    slot_ref, gate_ref, tokens_ref, gain_ref, ids_ref, gates_ref, sems = refs[PAIRS:]
+    out_refs = refs[: len(BLOCKS)]
+    slot_ref, gate_ref, tokens_ref, gain_ref, ids_ref, gates_ref, sems = refs[len(BLOCKS) :]
     count, width = tokens_ref.shape
     chunk = tile_of(width, 1024)
     starts = list(range(0, width, chunk))
@@ -77,9 +84,9 @@
         part = slice(first, first + chunk)
         wide = tokens_ref[:, part].astype(jnp.float32)
         normed = (wide * scale * gain_ref[:, part]).astype(jnp.bfloat16)
-        rows = jnp.dot(pick, normed, preferred_element_type=jnp.float32).astype(jnp.bfloat16)
-        for k, out_ref in enumerate(out_refs):
-            out_ref[:, part] = rows[k * 2 * CAP : (k + 1) * 2 * CAP]
+        rows = jnp.dot(pick, normed, preferred_element_type=jnp.float32)
+        for (k, size, _), out_ref in zip(BLOCKS, out_refs):
+            out_ref[:, part] = rows[k * CAP : (k + size) * CAP].astype(jnp.bfloat16)
 
 
 def prepare(tokens, gain, ids, gates, shards):
@@ -87,7 +94,9 @@
     return pl.pallas_call(
         functools.partial(prep_kernel, shards),
         in_specs=[HBM] * 4,
-        out_shape=[jax.ShapeDtypeStruct((2 * CAP, width), jnp.bfloat16)] * PAIRS
+        out_shape=[
+            jax.ShapeDtypeStruct((size * CAP, width), jnp.bfloat16) for _, size, _ in BLOCKS
+        ]
         + [
             jax.ShapeDtypeStruct((8, count), jnp.int32),
             jax.ShapeDtypeStruct((8, count), jnp.float32),
@@ -297,7 +306,7 @@
             pltpu.VMEM((RING, units, columns), jnp.bfloat16),
             pltpu.SemaphoreType.DMA((3, RING, SPLIT)),
         ],
-        compiler_params=pltpu.CompilerParams(vmem_limit_bytes=8 * 2**20 + 6 * RING * depth * units + 8 * total * width),
+        compiler_params=pltpu.CompilerParams(vmem_limit_bytes=50 * 2**20),
         cost_estimate=pl.CostEstimate(
             flops=6 * total * width * units,
             bytes_accessed=6 * width * units + 4 * total * width,
@@ -318,7 +327,9 @@
     copies = []
     for i, first in enumerate(range(0, width, chunk)):
         part = slice(first, first + chunk)
-        back = jnp.concatenate([ref[:, part] for ref in back_refs], axis=0)
+        back = jnp.concatenate(
+            [ref[:, part].astype(jnp.float32) for ref in back_refs], axis=0
+        ).astype(jnp.bfloat16)
         summed = jnp.dot(table, back, preferred_element_type=jnp.float32)
         wide = tokens_ref[:, part].astype(jnp.float32)
         staged[:, part] = (wide + gates * summed).astype(jnp.bfloat16)
@@ -364,45 +375,55 @@
         pairs = [(d, (d // shards ^ k) * shards + d % shards) for d in range(devices)]
         return lax.ppermute(block, "ep", pairs)
 
-    def expert(blocks, swapped):
+    def expert(pairs, swapped, singles):
         half = swapped.shape[0]
-        takes = [CAP] * len(blocks) + [half]
+        x_list = pairs + [swapped] + singles
+        takes = [CAP] * len(pairs) + [half] + [CAP] * len(singles)
+        out_rows = [half, half] + [CAP] * len(singles)
         if shards == 1:
-            return ffn(blocks + [swapped], takes, [half, half], *weights)
-        rows = jnp.concatenate([block[:CAP] for block in blocks] + [swapped], axis=0)
+            return ffn(x_list, takes, out_rows, *weights)
+        rows = jnp.concatenate([x[:take] for x, take in zip(x_list, takes)], axis=0)
         rows = lax.all_gather(rows, "ep", axis_index_groups=holders, tiled=True)
         (part,) = ffn([rows], [rows.shape[0]], [rows.shape[0]], *weights)
         part = lax.all_to_all(part, "ep", 0, 0, axis_index_groups=holders, tiled=True)
-        part = part.reshape(shards, 2 * half, width).astype(jnp.float32)
+        part = part.reshape(shards, -1, width).astype(jnp.float32)
         part = jnp.sum(part, axis=0).astype(jnp.bfloat16)
-        return part[:half], part[half:]
+        return jnp.split(part, [sum(out_rows[: i + 1]) for i in range(len(out_rows) - 1)], axis=0)
 
     ids_row = route_ids.reshape(1, count)
     gates_row = route_gates.reshape(1, count)
     *sent, slot_row, gates_row = prepare(
         tokens, norm_gain.reshape(1, width), ids_row, gates_row, shards
     )
-    early, late = GROUPS
-    held = {m: across(sent[m], 2 * m) for m in early}
-    later = after([sent[m] for m in late], [held[early[0]]])
-    held.update({m: across(block, 2 * m) for m, block in zip(late, later)})
+    sent = {name: block for (_, _, name), block in zip(BLOCKS, sent)}
+
+    def move(name, block):
+        return across(block, 2 * name[1] if name[0] == "p" else name[1])
+
+    early, late = (
+        [("p", m) for m in pairs] + [("s", k) for k in singles]
+        for pairs, singles in zip(PAIRED, SINGLE)
+    )
+    held = {name: move(name, sent[name]) for name in early}
+    later = after([sent[name] for name in late], [held[early[0]]])
+    held.update({name: move(name, block) for name, block in zip(late, later)})
     back = {}
-    for group in GROUPS:
-        blocks = [held[m] for m in group]
-        swapped = across(second_halves(blocks), 1)
-        own, other = expert(blocks, swapped)
-        waits = [held[m] for m in late] if group is early else [back[m] for m in early[:2]]
-        (other,) = after([other], waits)
-        blocks = dict(zip(group, zipped(own, across(other, 1))))
+    for group in (early, late):
+        pairs = [name for name in group if name[0] == "p"]
+        singles = [name for name in group if name[0] == "s"]
+        blocks = [held[name] for name in pairs]
+        first = [held[name] for name in singles] if group is early else []
+        swapped = across(second_halves(blocks, first), 1)
+        own, other, *results = expert(blocks, swapped, [held[name] for name in singles])
+        waits = [held[name] for name in FORWARD] if group is early else [back[name] for name in RETURN]
         if group is early:
-            last = {m: blocks.pop(m) for m in early[2:]}
+            (other,) = after([other], waits)
         else:
-            near = [m for m in last if m]
-            moved = after([last[m] for m in near], [blocks[late[0]]])
-            blocks.update(zip(near, moved))
-            blocks.update({m: block for m, block in last.items() if not m})
-        back.update({m: across(block, 2 * m) for m, block in blocks.items()})
-    return combine(tokens, slot_row, gates_row, [back[m] for m in range(PAIRS)])
+            other, *results = after([other] + results, waits)
+        blocks = dict(zip(singles, results))
+        blocks.update(zip(pairs, zipped(own, across(other, 1))))
+        back.update({name: move(name, blocks[name]) for name in group})
+    return combine(tokens, slot_row, gates_row, [back[name] for _, _, name in BLOCKS])
 
 
 def solution(mesh):

time: 112 us -> 105 us (0.938)
  the two profiles are of different devices: /device:TPU:0 before, /device:TPU:9 now
where the time goes in v2:
time: 105 us
  Pallas kernels  37.2 us (35%)
  waiting for transfers between devices  35.9 us (34%)
  starting transfers between devices  28.2 us (27%)
  local copies, waits for them, and re-layouts  3.56 us (3%)
    ppermute x22, waiting for transfers between devices, across(): return lax.ppermute(block, 'ep', pairs)  35.9 us
    pallas_call x2, Pallas kernels, ffn(): pl.pallas_call(functools.partial(ffn_kernel, takes, len(out_rows)), in_sp...  33.9 us
    ppermute x22, starting transfers between devices, across(): return lax.ppermute(block, 'ep', pairs)  28.2 us
    unnamed x10, local copies, waits for them, and re-layouts  3.56 us
  transfers between devices with their start and end apart: 22, of which 7 were waited for; matrix products, arithmetic and copies ran while one was open for 0% of the time, Pallas kernels for 32%

profile of v2, /device:TPU:9, one launch (start us, length us, event | category | flops | bytes accessed | tf_op | source)
XLA Modules:
  0.0 105.0 jit_solution(13545734875723515372)
XLA Ops:
  0.0 0.0 copy-start
  0.0 1.5 %copy-done = bf16[128,7168]{1,0:T(8,128)(2,1)S(1)} copy-done((bf16[128,7168]{1,0:T(8,128)(2,1)S(1)}, bf16[128,7168]{1,0:T(8,128)(2,1)}, u32[]{:S(2)}) %copy-start) | copy-done | bytes 1835032
  1.5 0.0 copy-start.2
  1.5 0.7 copy-done.2
  2.2 0.0 copy-start.3
  2.3 0.7 copy-done.3
  2.9 0.0 copy-start.4
  2.9 0.7 copy-done.4
  3.6 1.5 %prepare.1 = (bf16[16,7168]{1,0:T(8,128)(2,1)S(1)}, bf16[16,7168]{1,0:T(8,128)(2,1)S(1)}, bf16[16,7168]{1,0:T(8,128)(2,1)S(1)}, bf16[16,7168]{1,0:T(8,128)(2,1)S...) custom-call(bf16[128,7168]{1,0:T(8,128)(2,1)S(1)} %copy-done, ...), custom_call_target="tpu_custom_call" | custom-call | flops 234881024 | bytes 3670016 | tf_op jit(solution)/shard_map/prepare/pallas_call | solution.py:94
  5.0 2.4 %collective-permute-start = (bf16[16,7168]{1,0:T(8,128)(2,1)S(1)}, bf16[16,7168]{1,0:T(8,128)(2,1)S(1)}, u32[]{:S(2)}, u32[]{:S(2)}) collective-permute-start(bf16[16,7168]{1,0:T(8,128)(2,1)S(1)} %get-tuple-element.40), channel_id=1, source_target_pairs={{0,8},{1,9},{2,10},{3,11},{4,12},{5,13},{6,14},{7,15},{8,0},{9,1},... | collective-permute-start | bytes 688136 | tf_op jit(solution)/shard_map/ppermute | solution.py:376
  7.4 0.2 collective-permute-start.1
  7.6 1.2 %collective-permute-start.2 = (bf16[16,7168]{1,0:T(8,128)(2,1)S(1)}, bf16[16,7168]{1,0:T(8,128)(2,1)S(1)}, u32[]{:S(2)}, u32[]{:S(2)}) collective-permute-start(bf16[16,7168]{1,0:T(8,128)(2,1)S(1)} %get-tuple-element.42), channel_id=1, source_target_pairs={{0,2},{1,3},{2,0},{3,1},{4,6},{5,7},{6,4},{7,5},{8,10},{9,11},{10,... | collective-permute-start | bytes 688136 | tf_op jit(solution)/shard_map/ppermute | solution.py:376
  8.8 0.2 collective-permute-start.3
  9.0 3.0 %collective-permute-start.4 = (bf16[8,7168]{1,0:T(8,128)(2,1)S(1)}, bf16[8,7168]{1,0:T(8,128)(2,1)S(1)}, u32[]{:S(2)}, u32[]{:S(2)}) collective-permute-start(bf16[8,7168]{1,0:T(8,128)(2,1)S(1)} %get-tuple-element.45), channel_id=1, source_target_pairs={{0,13},{1,12},{2,15},{3,14},{4,9},{5,8},{6,11},{7,10},{8,5},{9,4},... | collective-permute-start | bytes 344072 | tf_op jit(solution)/shard_map/ppermute | solution.py:376
  11.9 13.0 %collective-permute-done.3.refs_4_.refs_5_ = bf16[8,7168]{1,0:T(8,128)(2,1)S(1)} collective-permute-done((bf16[8,7168]{1,0:T(8,128)(2,1)S(1)}, bf16[8,7168]{1,0:T(8,128)(2,1)S(1)}, u32[]{:S(2)}, u32[]{:S(2)}) %collective-permute-start.3) | collective-permute-done | bytes 114720 | tf_op jit(solution)/shard_map/ppermute | solution.py:376
  24.9 2.5 %collective-permute-done.4.refs_5_.refs_6_ = bf16[8,7168]{1,0:T(8,128)(2,1)S(1)} collective-permute-done((bf16[8,7168]{1,0:T(8,128)(2,1)S(1)}, bf16[8,7168]{1,0:T(8,128)(2,1)S(1)}, u32[]{:S(2)}, u32[]{:S(2)}) %collective-permute-start.4) | collective-permute-done | bytes 114720 | tf_op jit(solution)/shard_map/ppermute | solution.py:376
  27.4 0.0 collective-permute-done.refs_0_.refs_4_
  27.4 0.0 collective-permute-done.1.refs_1_
  27.4 0.0 collective-permute-done.2.refs_2_
  27.4 0.6 collective-permute-start.5
  28.0 0.1 collective-permute-start.6
  28.1 4.2 %collective-permute-start.7 = (bf16[16,7168]{1,0:T(8,128)(2,1)S(1)}, bf16[16,7168]{1,0:T(8,128)(2,1)S(1)}, u32[]{:S(2)}, u32[]{:S(2)}) collective-permute-start(bf16[16,7168]{1,0:T(8,128)(2,1)S(1)} %get-tuple-element.53), channel_id=1, source_target_pairs={{0,6},{1,7},{2,4},{3,5},{4,2},{5,3},{6,0},{7,1},{8,14},{9,15},{10,... | collective-permute-start | bytes 688136 | tf_op jit(solution)/shard_map/ppermute | solution.py:376
  32.3 0.3 collective-permute-start.8
  32.6 3.0 %collective-permute-start.9 = (bf16[8,7168]{1,0:T(8,128)(2,1)S(1)}, bf16[8,7168]{1,0:T(8,128)(2,1)S(1)}, u32[]{:S(2)}, u32[]{:S(2)}) collective-permute-start(bf16[8,7168]{1,0:T(8,128)(2,1)S(1)} %get-tuple-element.55), channel_id=1, source_target_pairs={{0,15},{1,14},{2,13},{3,12},{4,11},{5,10},{6,9},{7,8},{8,7},{9,6},... | collective-permute-start | bytes 344072 | tf_op jit(solution)/shard_map/ppermute | solution.py:376
  35.5 0.0 collective-permute-done.5.refs_4_
  35.5 17.0 %ffn.2 = (bf16[32,7168]{1,0:T(8,128)(2,1)S(1)}, bf16[32,7168]{1,0:T(8,128)(2,1)S(1)}, bf16[8,7168]{1,0:T(8,128)(2,1)S(1)}, bf16[8,7168]{1,0:T(8,128)(2,1)S(1)}) custom-call(bf16[7168,1024]{1,0:T(8,128)(2,1)} %gate_hbm.3, bf16[7168,1024]{1,0:T(8,128)(2,1)} %up_hbm.3, bf16[1024,7168]{1,0:T(8,128)(2,1)} %down_hbm.3, ...), custom_call_target="tpu_custom_call" | custom-call | flops 3523215360 | bytes 46333952 | tf_op jit(solution)/shard_map/ffn/pallas_call | solution.py:294
  52.5 0.0 collective-permute-done.8.refs_3_
  52.5 0.3 collective-permute-done.9.refs_4_
  52.8 0.0 collective-permute-done.6.refs_1_.refs_0_
  52.8 0.0 collective-permute-done.7.refs_2_.refs_1_
  52.9 0.5 collective-permute-start.10
  53.3 0.2 collective-permute-start.13
  53.5 1.2 %collective-permute-done.10.lower_ref = bf16[32,7168]{1,0:T(8,128)(2,1)S(1)} collective-permute-done((bf16[32,7168]{1,0:T(8,128)(2,1)S(1)}, bf16[32,7168]{1,0:T(8,128)(2,1)S(1)}, u32[]{:S(2)}, u32[]{:S(2)}) %collective-permute-start.10) | collective-permute-done | bytes 458784 | tf_op jit(solution)/shard_map/ppermute | solution.py:376
  54.8 0.1 zipped.2
  54.8 1.3 %collective-permute-start.12 = (bf16[16,7168]{1,0:T(8,128)(2,1)S(1)}, bf16[16,7168]{1,0:T(8,128)(2,1)S(1)}, u32[]{:S(2)}, u32[]{:S(2)}) collective-permute-start(bf16[16,7168]{1,0:T(8,128)(2,1)S(1)} %get-tuple-element.58), channel_id=1, source_target_pairs={{0,4},{1,5},{2,6},{3,7},{4,0},{5,1},{6,2},{7,3},{8,12},{9,13},{10,... | collective-permute-start | bytes 688136 | tf_op jit(solution)/shard_map/ppermute | solution.py:376
  56.1 0.2 collective-permute-start.15
  56.3 0.0 copy-start.1
  56.3 1.2 %collective-permute-start.14 = (bf16[8,7168]{1,0:T(8,128)(2,1)S(1)}, bf16[8,7168]{1,0:T(8,128)(2,1)S(1)}, u32[]{:S(2)}, u32[]{:S(2)}) collective-permute-start(bf16[8,7168]{1,0:T(8,128)(2,1)S(1)} %get-tuple-element.63), channel_id=1, source_target_pairs={{0,12},{1,13},{2,14},{3,15},{4,8},{5,9},{6,10},{7,11},{8,4},{9,5},... | collective-permute-start | bytes 344072 | tf_op jit(solution)/shard_map/ppermute | solution.py:376
  57.5 0.0 collective-permute-done.13.refs_2_
  57.6 16.9 %ffn.3 = (bf16[16,7168]{1,0:T(8,128)(2,1)S(1)}, bf16[16,7168]{1,0:T(8,128)(2,1)S(1)}, bf16[8,7168]{1,0:T(8,128)(2,1)S(1)}, bf16[8,7168]{1,0:T(8,128)(2,1)S(1)}) custom-call(bf16[7168,1024]{1,0:T(8,128)(2,1)} %gate_hbm.3, bf16[7168,1024]{1,0:T(8,128)(2,1)} %up_hbm.3, bf16[1024,7168]{1,0:T(8,128)(2,1)} %down_hbm.3, ...), custom_call_target="tpu_custom_call" | custom-call | flops 2113929216 | bytes 45416448 | tf_op jit(solution)/shard_map/ffn/pallas_call | solution.py:294
  74.5 0.0 collective-permute-done.14.refs_4_.refs_6_
  74.5 0.0 collective-permute-done.12.refs_3_.refs_2_
  74.5 0.0 collective-permute-done.15.refs_5_.refs_4_
  74.5 1.3 %collective-permute-start.16 = (bf16[16,7168]{1,0:T(8,128)(2,1)S(1)}, bf16[16,7168]{1,0:T(8,128)(2,1)S(1)}, u32[]{:S(2)}, u32[]{:S(2)}) collective-permute-start(bf16[16,7168]{1,0:T(8,128)(2,1)S(1)} %get-tuple-element.65), channel_id=1, source_target_pairs={{0,1},{1,0},{2,3},{3,2},{4,5},{5,4},{6,7},{7,6},{8,9},{9,8},{10,11... | collective-permute-start | bytes 688136 | tf_op jit(solution)/shard_map/ppermute | solution.py:376
  75.8 0.0 collective-permute-start.19
  75.8 0.9 collective-permute-start.11
  76.7 0.2 collective-permute-done.16.lower_ref
  77.0 3.3 %collective-permute-start.17 = (bf16[16,7168]{1,0:T(8,128)(2,1)S(1)}, bf16[16,7168]{1,0:T(8,128)(2,1)S(1)}, u32[]{:S(2)}, u32[]{:S(2)}) collective-permute-start(bf16[16,7168]{1,0:T(8,128)(2,1)S(1)} %get-tuple-element.66), channel_id=1, source_target_pairs={{0,6},{1,7},{2,4},{3,5},{4,2},{5,3},{6,0},{7,1},{8,14},{9,15},{10,... | collective-permute-start | bytes 688136 | tf_op jit(solution)/shard_map/ppermute | solution.py:376
  80.3 0.9 collective-permute-start.18
  81.2 0.3 collective-permute-start.20
  81.5 0.0 collective-permute-done.19.refs_7_
  81.5 3.2 %collective-permute-start.21 = (bf16[8,7168]{1,0:T(8,128)(2,1)S(1)}, bf16[8,7168]{1,0:T(8,128)(2,1)S(1)}, u32[]{:S(2)}, u32[]{:S(2)}) collective-permute-start(bf16[8,7168]{1,0:T(8,128)(2,1)S(1)} %get-tuple-element.70), channel_id=1, source_target_pairs={{0,15},{1,14},{2,13},{3,12},{4,11},{5,10},{6,9},{7,8},{8,7},{9,6},... | collective-permute-start | bytes 344072 | tf_op jit(solution)/shard_map/ppermute | solution.py:376
  84.7 0.0 collective-permute-done.11.refs_1_
  84.7 16.1 %collective-permute-done.20.refs_8_ = bf16[8,7168]{1,0:T(8,128)(2,1)S(1)} collective-permute-done((bf16[8,7168]{1,0:T(8,128)(2,1)S(1)}, bf16[8,7168]{1,0:T(8,128)(2,1)S(1)}, u32[]{:S(2)}, u32[]{:S(2)}) %collective-permute-start.20) | collective-permute-done | bytes 114720 | tf_op jit(solution)/shard_map/ppermute | solution.py:376
  100.8 2.6 %collective-permute-done.21.refs_9_ = bf16[8,7168]{1,0:T(8,128)(2,1)S(1)} collective-permute-done((bf16[8,7168]{1,0:T(8,128)(2,1)S(1)}, bf16[8,7168]{1,0:T(8,128)(2,1)S(1)}, u32[]{:S(2)}, u32[]{:S(2)}) %collective-permute-start.21) | collective-permute-done | bytes 114720 | tf_op jit(solution)/shard_map/ppermute | solution.py:376
  103.4 0.0 collective-permute-done.17.refs_3_
  103.4 0.0 collective-permute-done.18.refs_5_
  103.4 0.0 copy-done.1
  103.4 1.6 %combine.1 = bf16[128,7168]{1,0:T(8,128)(2,1)} custom-call(bf16[128,7168]{1,0:T(8,128)(2,1)S(1)} %copy-done.1, s32[8,128]{1,0:T(8,128)S(1)} %get-tuple-element.38.slot_ref, f32[8,128]{1,0:T(8,128)S(1)} %get-tuple-element.39.gates_ref, bf16[16,7168]{1,0:T(8,128)(2,1)S(1)} %get-tuple-element.56.refs_0_, bf16[16,7168]{1,0:T(8,128)(2,1)S(1)} %collective-permute-done.11.refs_1_, ...), custom_call_target="tpu_custom_call" | custom-call | flops 234881024 | bytes 5505024 | tf_op jit(solution)/shard_map/combine/pallas_call | solution.py:348
  (6 shorter events, 0.2 us)
Async XLA Ops:
  0.0 1.5 %copy-start = (bf16[128,7168]{1,0:T(8,128)(2,1)S(1)}, bf16[128,7168]{1,0:T(8,128)(2,1)}, u32[]{:S(2)}) copy-start(bf16[128,7168]{1,0:T(8,128)(2,1)} %tokens_ref.1) | copy-start | bytes 5505028
  1.5 0.7 copy-start.2
  2.2 0.7 copy-start.3
  2.9 0.7 copy-start.4
  5.0 22.3 %collective-permute-start = (bf16[16,7168]{1,0:T(8,128)(2,1)S(1)}, bf16[16,7168]{1,0:T(8,128)(2,1)S(1)}, u32[]{:S(2)}, u32[]{:S(2)}) collective-permute-start(bf16[16,7168]{1,0:T(8,128)(2,1)S(1)} %get-tuple-element.40), channel_id=1, source_target_pairs={{0,8},{1,9},{2,10},{3,11},{4,12},{5,13},{6,14},{7,15},{8,0},{9,1},... | collective-permute-start | bytes 688136 | tf_op jit(solution)/shard_map/ppermute | solution.py:376
  7.4 20.0 %collective-permute-start.1 = (bf16[16,7168]{1,0:T(8,128)(2,1)S(1)}, bf16[16,7168]{1,0:T(8,128)(2,1)S(1)}, u32[]{:S(2)}, u32[]{:S(2)}) collective-permute-start(bf16[16,7168]{1,0:T(8,128)(2,1)S(1)} %get-tuple-element.41), channel_id=1, source_target_pairs={{0,4},{1,5},{2,6},{3,7},{4,0},{5,1},{6,2},{7,3},{8,12},{9,13},{10,... | collective-permute-start | bytes 688136 | tf_op jit(solution)/shard_map/ppermute | solution.py:376
  7.6 19.8 %collective-permute-start.2 = (bf16[16,7168]{1,0:T(8,128)(2,1)S(1)}, bf16[16,7168]{1,0:T(8,128)(2,1)S(1)}, u32[]{:S(2)}, u32[]{:S(2)}) collective-permute-start(bf16[16,7168]{1,0:T(8,128)(2,1)S(1)} %get-tuple-element.42), channel_id=1, source_target_pairs={{0,2},{1,3},{2,0},{3,1},{4,6},{5,7},{6,4},{7,5},{8,10},{9,11},{10,... | collective-permute-start | bytes 688136 | tf_op jit(solution)/shard_map/ppermute | solution.py:376
  8.8 16.1 %collective-permute-start.3 = (bf16[8,7168]{1,0:T(8,128)(2,1)S(1)}, bf16[8,7168]{1,0:T(8,128)(2,1)S(1)}, u32[]{:S(2)}, u32[]{:S(2)}) collective-permute-start(bf16[8,7168]{1,0:T(8,128)(2,1)S(1)} %get-tuple-element.44), channel_id=1, source_target_pairs={{0,12},{1,13},{2,14},{3,15},{4,8},{5,9},{6,10},{7,11},{8,4},{9,5},... | collective-permute-start | bytes 344072 | tf_op jit(solution)/shard_map/ppermute | solution.py:376
  9.0 18.4 %collective-permute-start.4 = (bf16[8,7168]{1,0:T(8,128)(2,1)S(1)}, bf16[8,7168]{1,0:T(8,128)(2,1)S(1)}, u32[]{:S(2)}, u32[]{:S(2)}) collective-permute-start(bf16[8,7168]{1,0:T(8,128)(2,1)S(1)} %get-tuple-element.45), channel_id=1, source_target_pairs={{0,13},{1,12},{2,15},{3,14},{4,9},{5,8},{6,11},{7,10},{8,5},{9,4},... | collective-permute-start | bytes 344072 | tf_op jit(solution)/shard_map/ppermute | solution.py:376
  27.4 8.1 %collective-permute-start.5 = (bf16[32,7168]{1,0:T(8,128)(2,1)S(1)}, bf16[32,7168]{1,0:T(8,128)(2,1)S(1)}, u32[]{:S(2)}, u32[]{:S(2)}) collective-permute-start(bf16[32,7168]{1,0:T(8,128)(2,1)S(1)} %second_halves.2), channel_id=1, source_target_pairs={{0,1},{1,0},{2,3},{3,2},{4,5},{5,4},{6,7},{7,6},{8,9},{9,8},{10,11... | collective-permute-start | bytes 1376264 | tf_op jit(solution)/shard_map/ppermute | solution.py:376
  28.0 24.8 %collective-permute-start.6 = (bf16[16,7168]{1,0:T(8,128)(2,1)S(1)}, bf16[16,7168]{1,0:T(8,128)(2,1)S(1)}, u32[]{:S(2)}, u32[]{:S(2)}) collective-permute-start(bf16[16,7168]{1,0:T(8,128)(2,1)S(1)} %get-tuple-element.52), channel_id=1, source_target_pairs={{0,10},{1,11},{2,8},{3,9},{4,14},{5,15},{6,12},{7,13},{8,2},{9,3},... | collective-permute-start | bytes 688136 | tf_op jit(solution)/shard_map/ppermute | solution.py:376
  28.1 24.7 %collective-permute-start.7 = (bf16[16,7168]{1,0:T(8,128)(2,1)S(1)}, bf16[16,7168]{1,0:T(8,128)(2,1)S(1)}, u32[]{:S(2)}, u32[]{:S(2)}) collective-permute-start(bf16[16,7168]{1,0:T(8,128)(2,1)S(1)} %get-tuple-element.53), channel_id=1, source_target_pairs={{0,6},{1,7},{2,4},{3,5},{4,2},{5,3},{6,0},{7,1},{8,14},{9,15},{10,... | collective-permute-start | bytes 688136 | tf_op jit(solution)/shard_map/ppermute | solution.py:376
  32.3 20.2 %collective-permute-start.8 = (bf16[8,7168]{1,0:T(8,128)(2,1)S(1)}, bf16[8,7168]{1,0:T(8,128)(2,1)S(1)}, u32[]{:S(2)}, u32[]{:S(2)}) collective-permute-start(bf16[8,7168]{1,0:T(8,128)(2,1)S(1)} %get-tuple-element.54), channel_id=1, source_target_pairs={{0,14},{1,15},{2,12},{3,13},{4,10},{5,11},{6,8},{7,9},{8,6},{9,7},... | collective-permute-start | bytes 344072 | tf_op jit(solution)/shard_map/ppermute | solution.py:376
  32.6 20.2 %collective-permute-start.9 = (bf16[8,7168]{1,0:T(8,128)(2,1)S(1)}, bf16[8,7168]{1,0:T(8,128)(2,1)S(1)}, u32[]{:S(2)}, u32[]{:S(2)}) collective-permute-start(bf16[8,7168]{1,0:T(8,128)(2,1)S(1)} %get-tuple-element.55), channel_id=1, source_target_pairs={{0,15},{1,14},{2,13},{3,12},{4,11},{5,10},{6,9},{7,8},{8,7},{9,6},... | collective-permute-start | bytes 344072 | tf_op jit(solution)/shard_map/ppermute | solution.py:376
  52.9 1.9 %collective-permute-start.10 = (bf16[32,7168]{1,0:T(8,128)(2,1)S(1)}, bf16[32,7168]{1,0:T(8,128)(2,1)S(1)}, u32[]{:S(2)}, u32[]{:S(2)}) collective-permute-start(bf16[32,7168]{1,0:T(8,128)(2,1)S(1)} %after.4), channel_id=1, source_target_pairs={{0,1},{1,0},{2,3},{3,2},{4,5},{5,4},{6,7},{7,6},{8,9},{9,8},{10,11... | collective-permute-start | bytes 1376264 | tf_op jit(solution)/shard_map/ppermute | solution.py:376
  53.3 4.2 %collective-permute-start.13 = (bf16[16,7168]{1,0:T(8,128)(2,1)S(1)}, bf16[16,7168]{1,0:T(8,128)(2,1)S(1)}, u32[]{:S(2)}, u32[]{:S(2)}) collective-permute-start(bf16[16,7168]{1,0:T(8,128)(2,1)S(1)} %second_halves.3), channel_id=1, source_target_pairs={{0,1},{1,0},{2,3},{3,2},{4,5},{5,4},{6,7},{7,6},{8,9},{9,8},{10,11... | collective-permute-start | bytes 688136 | tf_op jit(solution)/shard_map/ppermute | solution.py:376
  54.8 19.7 %collective-permute-start.12 = (bf16[16,7168]{1,0:T(8,128)(2,1)S(1)}, bf16[16,7168]{1,0:T(8,128)(2,1)S(1)}, u32[]{:S(2)}, u32[]{:S(2)}) collective-permute-start(bf16[16,7168]{1,0:T(8,128)(2,1)S(1)} %get-tuple-element.58), channel_id=1, source_target_pairs={{0,4},{1,5},{2,6},{3,7},{4,0},{5,1},{6,2},{7,3},{8,12},{9,13},{10,... | collective-permute-start | bytes 688136 | tf_op jit(solution)/shard_map/ppermute | solution.py:376
  56.1 18.3 %collective-permute-start.15 = (bf16[16,7168]{1,0:T(8,128)(2,1)S(1)}, bf16[16,7168]{1,0:T(8,128)(2,1)S(1)}, u32[]{:S(2)}, u32[]{:S(2)}) collective-permute-start(bf16[16,7168]{1,0:T(8,128)(2,1)S(1)} %get-tuple-element.64), channel_id=1, source_target_pairs={{0,8},{1,9},{2,10},{3,11},{4,12},{5,13},{6,14},{7,15},{8,0},{9,1},... | collective-permute-start | bytes 688136 | tf_op jit(solution)/shard_map/ppermute | solution.py:376
  56.3 47.1 %copy-start.1 = (bf16[128,7168]{1,0:T(8,128)(2,1)S(1)}, bf16[128,7168]{1,0:T(8,128)(2,1)}, u32[]{:S(2)}) copy-start(bf16[128,7168]{1,0:T(8,128)(2,1)} %tokens_ref.1) | copy-start | bytes 5505028
  56.3 18.2 %collective-permute-start.14 = (bf16[8,7168]{1,0:T(8,128)(2,1)S(1)}, bf16[8,7168]{1,0:T(8,128)(2,1)S(1)}, u32[]{:S(2)}, u32[]{:S(2)}) collective-permute-start(bf16[8,7168]{1,0:T(8,128)(2,1)S(1)} %get-tuple-element.63), channel_id=1, source_target_pairs={{0,12},{1,13},{2,14},{3,15},{4,8},{5,9},{6,10},{7,11},{8,4},{9,5},... | collective-permute-start | bytes 344072 | tf_op jit(solution)/shard_map/ppermute | solution.py:376
  74.5 2.4 %collective-permute-start.16 = (bf16[16,7168]{1,0:T(8,128)(2,1)S(1)}, bf16[16,7168]{1,0:T(8,128)(2,1)S(1)}, u32[]{:S(2)}, u32[]{:S(2)}) collective-permute-start(bf16[16,7168]{1,0:T(8,128)(2,1)S(1)} %get-tuple-element.65), channel_id=1, source_target_pairs={{0,1},{1,0},{2,3},{3,2},{4,5},{5,4},{6,7},{7,6},{8,9},{9,8},{10,11... | collective-permute-start | bytes 688136 | tf_op jit(solution)/shard_map/ppermute | solution.py:376
  75.8 5.7 %collective-permute-start.19 = (bf16[8,7168]{1,0:T(8,128)(2,1)S(1)}, bf16[8,7168]{1,0:T(8,128)(2,1)S(1)}, u32[]{:S(2)}, u32[]{:S(2)}) collective-permute-start(bf16[8,7168]{1,0:T(8,128)(2,1)S(1)} %get-tuple-element.68), channel_id=1, source_target_pairs={{0,13},{1,12},{2,15},{3,14},{4,9},{5,8},{6,11},{7,10},{8,5},{9,4},... | collective-permute-start | bytes 344072 | tf_op jit(solution)/shard_map/ppermute | solution.py:376
  75.8 8.9 %collective-permute-start.11 = (bf16[16,7168]{1,0:T(8,128)(2,1)S(1)}, bf16[16,7168]{1,0:T(8,128)(2,1)S(1)}, u32[]{:S(2)}, u32[]{:S(2)}) collective-permute-start(bf16[16,7168]{1,0:T(8,128)(2,1)S(1)} %get-tuple-element.57), channel_id=1, source_target_pairs={{0,2},{1,3},{2,0},{3,1},{4,6},{5,7},{6,4},{7,5},{8,10},{9,11},{10,... | collective-permute-start | bytes 688136 | tf_op jit(solution)/shard_map/ppermute | solution.py:376
  77.0 26.4 %collective-permute-start.17 = (bf16[16,7168]{1,0:T(8,128)(2,1)S(1)}, bf16[16,7168]{1,0:T(8,128)(2,1)S(1)}, u32[]{:S(2)}, u32[]{:S(2)}) collective-permute-start(bf16[16,7168]{1,0:T(8,128)(2,1)S(1)} %get-tuple-element.66), channel_id=1, source_target_pairs={{0,6},{1,7},{2,4},{3,5},{4,2},{5,3},{6,0},{7,1},{8,14},{9,15},{10,... | collective-permute-start | bytes 688136 | tf_op jit(solution)/shard_map/ppermute | solution.py:376
  80.3 23.2 %collective-permute-start.18 = (bf16[16,7168]{1,0:T(8,128)(2,1)S(1)}, bf16[16,7168]{1,0:T(8,128)(2,1)S(1)}, u32[]{:S(2)}, u32[]{:S(2)}) collective-permute-start(bf16[16,7168]{1,0:T(8,128)(2,1)S(1)} %get-tuple-element.67), channel_id=1, source_target_pairs={{0,10},{1,11},{2,8},{3,9},{4,14},{5,15},{6,12},{7,13},{8,2},{9,3},... | collective-permute-start | bytes 688136 | tf_op jit(solution)/shard_map/ppermute | solution.py:376
  81.2 19.7 %collective-permute-start.20 = (bf16[8,7168]{1,0:T(8,128)(2,1)S(1)}, bf16[8,7168]{1,0:T(8,128)(2,1)S(1)}, u32[]{:S(2)}, u32[]{:S(2)}) collective-permute-start(bf16[8,7168]{1,0:T(8,128)(2,1)S(1)} %get-tuple-element.69), channel_id=1, source_target_pairs={{0,14},{1,15},{2,12},{3,13},{4,10},{5,11},{6,8},{7,9},{8,6},{9,7},... | collective-permute-start | bytes 344072 | tf_op jit(solution)/shard_map/ppermute | solution.py:376
  81.5 21.9 %collective-permute-start.21 = (bf16[8,7168]{1,0:T(8,128)(2,1)S(1)}, bf16[8,7168]{1,0:T(8,128)(2,1)S(1)}, u32[]{:S(2)}, u32[]{:S(2)}) collective-permute-start(bf16[8,7168]{1,0:T(8,128)(2,1)S(1)} %get-tuple-element.70), channel_id=1, source_target_pairs={{0,15},{1,14},{2,13},{3,12},{4,11},{5,10},{6,9},{7,8},{8,7},{9,6},... | collective-permute-start | bytes 344072 | tf_op jit(solution)/shard_map/ppermute | solution.py:376

commit v3 on v2

--- a/solution.py
+++ b/solution.py
@@ -20,7 +20,7 @@
 RETURN = (("p", 2), ("s", 12), ("p", 4))
 RING = 3
 SPLIT = 2
-PREP_VMEM = 12 * 2**20
+PREP_VMEM = 51 * 2**20
 HBM = pl.BlockSpec(memory_space=pltpu.HBM)
 VMEM = pl.BlockSpec(memory_space=pltpu.VMEM)
 
@@ -49,51 +49,49 @@
     return jnp.sum(jnp.where(same & before, 1.0, 0.0), axis=axis, keepdims=True)
 
 
-def prep_kernel(shards, tokens_hbm, gain_hbm, ids_hbm, gates_hbm, *refs):
+def prep_kernel(shards, tokens_hbm, vectors_ref, *refs):
     out_refs = refs[: len(BLOCKS)]
-    slot_ref, gate_ref, tokens_ref, gain_ref, ids_ref, gates_ref, sems = refs[len(BLOCKS) :]
+    slot_ref, gate_ref, tokens_ref, sems = refs[len(BLOCKS) :]
     count, width = tokens_ref.shape
     chunk = tile_of(width, 1024)
     starts = list(range(0, width, chunk))
-    pairs = [(ids_hbm, ids_ref), (gates_hbm, gates_ref), (gain_hbm, gain_ref)]
-    pairs += [(tokens_hbm.at[:, pl.ds(at, chunk)], tokens_ref.at[:, pl.ds(at, chunk)]) for at in starts]
     copies = [
-        pltpu.make_async_copy(source, target, sems.at[i]) for i, (source, target) in enumerate(pairs)
+        pltpu.make_async_copy(
+            tokens_hbm.at[:, pl.ds(at, chunk)], tokens_ref.at[:, pl.ds(at, chunk)], sems.at[i]
+        )
+        for i, at in enumerate(starts)
     ]
     for copy in copies:
         copy.start()
     mine = lax.axis_index("ep") // shards
-    copies[0].wait()
-    ids_row = ids_ref[...]
+    ids_row = vectors_ref[:, width : width + count].astype(jnp.int32)
     rank_row = ranks(ids_row.astype(jnp.float32), 0).astype(jnp.int32)
     slot_row = (ids_row ^ mine) * CAP + rank_row
     slots = EXPERTS * CAP
     pick = (lax.broadcasted_iota(jnp.int32, (slots, count), 0) == slot_row).astype(jnp.bfloat16)
     slot_ref[...] = jnp.broadcast_to(slot_row, slot_ref.shape)
-    copies[1].wait()
-    gate_ref[...] = jnp.broadcast_to(gates_ref[...], gate_ref.shape)
+    gate_ref[...] = jnp.broadcast_to(vectors_ref[:, width + count :], gate_ref.shape)
     square_sum = jnp.zeros((count, 128), jnp.float32)
-    for first, copy in zip(starts, copies[3:]):
+    for first, copy in zip(starts, copies):
         copy.wait()
         for lane in range(first, first + chunk, 128):
             wide = tokens_ref[:, lane : lane + 128].astype(jnp.float32)
             square_sum = square_sum + wide * wide
     scale = lax.rsqrt(jnp.sum(square_sum, axis=1, keepdims=True) / width + 1e-05)
-    copies[2].wait()
     for first in starts:
         part = slice(first, first + chunk)
         wide = tokens_ref[:, part].astype(jnp.float32)
-        normed = (wide * scale * gain_ref[:, part]).astype(jnp.bfloat16)
+        normed = (wide * scale * vectors_ref[:, part]).astype(jnp.bfloat16)
         rows = jnp.dot(pick, normed, preferred_element_type=jnp.float32)
         for (k, size, _), out_ref in zip(BLOCKS, out_refs):
             out_ref[:, part] = rows[k * CAP : (k + size) * CAP].astype(jnp.bfloat16)
 
 
-def prepare(tokens, gain, ids, gates, shards):
+def prepare(tokens, vectors, shards):
     count, width = tokens.shape
     return pl.pallas_call(
         functools.partial(prep_kernel, shards),
-        in_specs=[HBM] * 4,
+        in_specs=[HBM, VMEM],
         out_shape=[
             jax.ShapeDtypeStruct((size * CAP, width), jnp.bfloat16) for _, size, _ in BLOCKS
         ]
@@ -103,17 +101,14 @@
         ],
         scratch_shapes=[
             pltpu.VMEM((count, width), jnp.bfloat16),
-            pltpu.VMEM((1, width), jnp.float32),
-            pltpu.VMEM((1, count), jnp.int32),
-            pltpu.VMEM((1, count), jnp.float32),
-            pltpu.SemaphoreType.DMA((width // tile_of(width, 1024) + 3,)),
+            pltpu.SemaphoreType.DMA((width // tile_of(width, 1024),)),
         ],
         compiler_params=pltpu.CompilerParams(vmem_limit_bytes=PREP_VMEM),
         cost_estimate=pl.CostEstimate(
             flops=2 * count * count * width, bytes_accessed=4 * count * width, transcendentals=0
         ),
         name="prepare",
-    )(tokens, gain, ids, gates)
+    )(tokens, vectors)
 
 
 def halves_kernel(count, *refs):
@@ -390,11 +385,10 @@
         part = jnp.sum(part, axis=0).astype(jnp.bfloat16)
         return jnp.split(part, [sum(out_rows[: i + 1]) for i in range(len(out_rows) - 1)], axis=0)
 
-    ids_row = route_ids.reshape(1, count)
-    gates_row = route_gates.reshape(1, count)
-    *sent, slot_row, gates_row = prepare(
-        tokens, norm_gain.reshape(1, width), ids_row, gates_row, shards
-    )
+    vectors = jnp.concatenate(
+        [norm_gain, route_ids.reshape(count).astype(jnp.float32), route_gates.reshape(count)]
+    ).reshape(1, -1)
+    *sent, slot_row, gates_row = prepare(tokens, vectors, shards)
     sent = {name: block for (_, _, name), block in zip(BLOCKS, sent)}
 
     def move(name, block):

time: 105 us -> 104 us (level)
  local copies, waits for them, and re-layouts: 3.56 us -> 0.02 us
  other arithmetic: 0 us -> 1.43 us
    unnamed x10 -> x2, local copies, waits for them, and re-layouts: 3.56 us -> 0.01 us
  transfers between devices with their start and end apart: 22 -> 22, of which waited for: 7 -> 7; matrix products, arithmetic and copies ran while one was open for 0% -> 0% of each run, Pallas kernels for 32% -> 33%
where the time goes in v3:
time: 104 us
  Pallas kernels  38 us (37%)
  waiting for transfers between devices  35.9 us (35%)
  starting transfers between devices  28.2 us (27%)
  other arithmetic  1.43 us (1%)
    ppermute x22, waiting for transfers between devices, across(): return lax.ppermute(block, 'ep', pairs)  35.9 us
    pallas_call x2, Pallas kernels, ffn(): pl.pallas_call(functools.partial(ffn_kernel, takes, len(out_rows)), in_sp...  33.9 us
    ppermute x22, starting transfers between devices, across(): return lax.ppermute(block, 'ep', pairs)  28.2 us
    pallas_call x1, Pallas kernels, prepare(): pl.pallas_call(functools.partial(prep_kernel, shards), in_specs=[HBM, VME...  2.26 us
  transfers between devices with their start and end apart: 22, of which 7 were waited for; matrix products, arithmetic and copies ran while one was open for 0% of the time, Pallas kernels for 33%

profile of v3, /device:TPU:9, one launch (start us, length us, event | category | flops | bytes accessed | tf_op | source)
XLA Modules:
  0.0 103.7 jit_solution(850910791107409509)
XLA Ops:
  0.0 0.7 convert_bitcast_fusion
  0.7 0.8 pad_maximum_fusion
  1.5 2.3 %prepare.1 = (bf16[16,7168]{1,0:T(8,128)(2,1)S(1)}, bf16[16,7168]{1,0:T(8,128)(2,1)S(1)}, bf16[16,7168]{1,0:T(8,128)(2,1)S(1)}, bf16[16,7168]{1,0:T(8,128)(2,1)S...) custom-call(bf16[128,7168]{1,0:T(8,128)(2,1)} %tokens_ref.1, ...), custom_call_target="tpu_custom_call" | custom-call | flops 234881024 | bytes 3670016 | tf_op jit(solution)/shard_map/prepare/pallas_call | solution.py:92
  3.7 2.4 %collective-permute-start = (bf16[16,7168]{1,0:T(8,128)(2,1)S(1)}, bf16[16,7168]{1,0:T(8,128)(2,1)S(1)}, u32[]{:S(2)}, u32[]{:S(2)}) collective-permute-start(bf16[16,7168]{1,0:T(8,128)(2,1)S(1)} %get-tuple-element.40), channel_id=1, source_target_pairs={{0,8},{1,9},{2,10},{3,11},{4,12},{5,13},{6,14},{7,15},{8,0},{9,1},... | collective-permute-start | bytes 688136 | tf_op jit(solution)/shard_map/ppermute | solution.py:371
  6.1 0.2 collective-permute-start.1
  6.3 1.2 %collective-permute-start.2 = (bf16[16,7168]{1,0:T(8,128)(2,1)S(1)}, bf16[16,7168]{1,0:T(8,128)(2,1)S(1)}, u32[]{:S(2)}, u32[]{:S(2)}) collective-permute-start(bf16[16,7168]{1,0:T(8,128)(2,1)S(1)} %get-tuple-element.42), channel_id=1, source_target_pairs={{0,2},{1,3},{2,0},{3,1},{4,6},{5,7},{6,4},{7,5},{8,10},{9,11},{10,... | collective-permute-start | bytes 688136 | tf_op jit(solution)/shard_map/ppermute | solution.py:371
  7.5 0.2 collective-permute-start.3
  7.7 3.0 %collective-permute-start.4 = (bf16[8,7168]{1,0:T(8,128)(2,1)S(1)}, bf16[8,7168]{1,0:T(8,128)(2,1)S(1)}, u32[]{:S(2)}, u32[]{:S(2)}) collective-permute-start(bf16[8,7168]{1,0:T(8,128)(2,1)S(1)} %get-tuple-element.45), channel_id=1, source_target_pairs={{0,13},{1,12},{2,15},{3,14},{4,9},{5,8},{6,11},{7,10},{8,5},{9,4},... | collective-permute-start | bytes 344072 | tf_op jit(solution)/shard_map/ppermute | solution.py:371
  10.6 13.0 %collective-permute-done.3.refs_4_.refs_5_ = bf16[8,7168]{1,0:T(8,128)(2,1)S(1)} collective-permute-done((bf16[8,7168]{1,0:T(8,128)(2,1)S(1)}, bf16[8,7168]{1,0:T(8,128)(2,1)S(1)}, u32[]{:S(2)}, u32[]{:S(2)}) %collective-permute-start.3) | collective-permute-done | bytes 114720 | tf_op jit(solution)/shard_map/ppermute | solution.py:371
  23.6 2.5 %collective-permute-done.4.refs_5_.refs_6_ = bf16[8,7168]{1,0:T(8,128)(2,1)S(1)} collective-permute-done((bf16[8,7168]{1,0:T(8,128)(2,1)S(1)}, bf16[8,7168]{1,0:T(8,128)(2,1)S(1)}, u32[]{:S(2)}, u32[]{:S(2)}) %collective-permute-start.4) | collective-permute-done | bytes 114720 | tf_op jit(solution)/shard_map/ppermute | solution.py:371
  26.1 0.0 collective-permute-done.refs_0_.refs_4_
  26.1 0.0 collective-permute-done.1.refs_1_
  26.1 0.0 collective-permute-done.2.refs_2_
  26.1 0.6 collective-permute-start.5
  26.7 0.1 collective-permute-start.6
  26.8 4.2 %collective-permute-start.7 = (bf16[16,7168]{1,0:T(8,128)(2,1)S(1)}, bf16[16,7168]{1,0:T(8,128)(2,1)S(1)}, u32[]{:S(2)}, u32[]{:S(2)}) collective-permute-start(bf16[16,7168]{1,0:T(8,128)(2,1)S(1)} %get-tuple-element.53), channel_id=1, source_target_pairs={{0,6},{1,7},{2,4},{3,5},{4,2},{5,3},{6,0},{7,1},{8,14},{9,15},{10,... | collective-permute-start | bytes 688136 | tf_op jit(solution)/shard_map/ppermute | solution.py:371
  31.0 0.3 collective-permute-start.8
  31.3 2.9 %collective-permute-start.9 = (bf16[8,7168]{1,0:T(8,128)(2,1)S(1)}, bf16[8,7168]{1,0:T(8,128)(2,1)S(1)}, u32[]{:S(2)}, u32[]{:S(2)}) collective-permute-start(bf16[8,7168]{1,0:T(8,128)(2,1)S(1)} %get-tuple-element.55), channel_id=1, source_target_pairs={{0,15},{1,14},{2,13},{3,12},{4,11},{5,10},{6,9},{7,8},{8,7},{9,6},... | collective-permute-start | bytes 344072 | tf_op jit(solution)/shard_map/ppermute | solution.py:371
  34.2 0.0 collective-permute-done.5.refs_4_
  34.2 17.0 %ffn.2 = (bf16[32,7168]{1,0:T(8,128)(2,1)S(1)}, bf16[32,7168]{1,0:T(8,128)(2,1)S(1)}, bf16[8,7168]{1,0:T(8,128)(2,1)S(1)}, bf16[8,7168]{1,0:T(8,128)(2,1)S(1)}) custom-call(bf16[7168,1024]{1,0:T(8,128)(2,1)} %gate_hbm.3, bf16[7168,1024]{1,0:T(8,128)(2,1)} %up_hbm.3, bf16[1024,7168]{1,0:T(8,128)(2,1)} %down_hbm.3, ...), custom_call_target="tpu_custom_call" | custom-call | flops 3523215360 | bytes 46333952 | tf_op jit(solution)/shard_map/ffn/pallas_call | solution.py:289
  51.2 0.0 collective-permute-done.8.refs_3_
  51.2 0.3 collective-permute-done.9.refs_4_
  51.5 0.0 collective-permute-done.6.refs_1_.refs_0_
  51.5 0.0 collective-permute-done.7.refs_2_.refs_1_
  51.5 0.5 collective-permute-start.10
  52.0 0.2 collective-permute-start.13
  52.2 1.2 %collective-permute-done.10.lower_ref = bf16[32,7168]{1,0:T(8,128)(2,1)S(1)} collective-permute-done((bf16[32,7168]{1,0:T(8,128)(2,1)S(1)}, bf16[32,7168]{1,0:T(8,128)(2,1)S(1)}, u32[]{:S(2)}, u32[]{:S(2)}) %collective-permute-start.10) | collective-permute-done | bytes 458784 | tf_op jit(solution)/shard_map/ppermute | solution.py:371
  53.4 0.1 zipped.2
  53.5 1.3 %collective-permute-start.12 = (bf16[16,7168]{1,0:T(8,128)(2,1)S(1)}, bf16[16,7168]{1,0:T(8,128)(2,1)S(1)}, u32[]{:S(2)}, u32[]{:S(2)}) collective-permute-start(bf16[16,7168]{1,0:T(8,128)(2,1)S(1)} %get-tuple-element.58), channel_id=1, source_target_pairs={{0,4},{1,5},{2,6},{3,7},{4,0},{5,1},{6,2},{7,3},{8,12},{9,13},{10,... | collective-permute-start | bytes 688136 | tf_op jit(solution)/shard_map/ppermute | solution.py:371
  54.8 0.1 collective-permute-start.15
  55.0 0.0 copy-start
  55.0 1.2 %collective-permute-start.14 = (bf16[8,7168]{1,0:T(8,128)(2,1)S(1)}, bf16[8,7168]{1,0:T(8,128)(2,1)S(1)}, u32[]{:S(2)}, u32[]{:S(2)}) collective-permute-start(bf16[8,7168]{1,0:T(8,128)(2,1)S(1)} %get-tuple-element.63), channel_id=1, source_target_pairs={{0,12},{1,13},{2,14},{3,15},{4,8},{5,9},{6,10},{7,11},{8,4},{9,5},... | collective-permute-start | bytes 344072 | tf_op jit(solution)/shard_map/ppermute | solution.py:371
  56.2 0.0 collective-permute-done.13.refs_2_
  56.2 16.9 %ffn.3 = (bf16[16,7168]{1,0:T(8,128)(2,1)S(1)}, bf16[16,7168]{1,0:T(8,128)(2,1)S(1)}, bf16[8,7168]{1,0:T(8,128)(2,1)S(1)}, bf16[8,7168]{1,0:T(8,128)(2,1)S(1)}) custom-call(bf16[7168,1024]{1,0:T(8,128)(2,1)} %gate_hbm.3, bf16[7168,1024]{1,0:T(8,128)(2,1)} %up_hbm.3, bf16[1024,7168]{1,0:T(8,128)(2,1)} %down_hbm.3, ...), custom_call_target="tpu_custom_call" | custom-call | flops 2113929216 | bytes 45416448 | tf_op jit(solution)/shard_map/ffn/pallas_call | solution.py:289
  73.1 0.0 collective-permute-done.14.refs_4_.refs_6_
  73.2 0.0 collective-permute-done.12.refs_3_.refs_2_
  73.2 0.0 collective-permute-done.15.refs_5_.refs_4_
  73.2 1.3 %collective-permute-start.16 = (bf16[16,7168]{1,0:T(8,128)(2,1)S(1)}, bf16[16,7168]{1,0:T(8,128)(2,1)S(1)}, u32[]{:S(2)}, u32[]{:S(2)}) collective-permute-start(bf16[16,7168]{1,0:T(8,128)(2,1)S(1)} %get-tuple-element.65), channel_id=1, source_target_pairs={{0,1},{1,0},{2,3},{3,2},{4,5},{5,4},{6,7},{7,6},{8,9},{9,8},{10,11... | collective-permute-start | bytes 688136 | tf_op jit(solution)/shard_map/ppermute | solution.py:371
  74.5 0.0 collective-permute-start.19
  74.5 0.9 collective-permute-start.11
  75.4 0.2 collective-permute-done.16.lower_ref
  75.6 3.3 %collective-permute-start.17 = (bf16[16,7168]{1,0:T(8,128)(2,1)S(1)}, bf16[16,7168]{1,0:T(8,128)(2,1)S(1)}, u32[]{:S(2)}, u32[]{:S(2)}) collective-permute-start(bf16[16,7168]{1,0:T(8,128)(2,1)S(1)} %get-tuple-element.66), channel_id=1, source_target_pairs={{0,6},{1,7},{2,4},{3,5},{4,2},{5,3},{6,0},{7,1},{8,14},{9,15},{10,... | collective-permute-start | bytes 688136 | tf_op jit(solution)/shard_map/ppermute | solution.py:371
  78.9 0.9 collective-permute-start.18
  79.8 0.3 collective-permute-start.20
  80.2 0.0 collective-permute-done.19.refs_7_
  80.2 3.2 %collective-permute-start.21 = (bf16[8,7168]{1,0:T(8,128)(2,1)S(1)}, bf16[8,7168]{1,0:T(8,128)(2,1)S(1)}, u32[]{:S(2)}, u32[]{:S(2)}) collective-permute-start(bf16[8,7168]{1,0:T(8,128)(2,1)S(1)} %get-tuple-element.70), channel_id=1, source_target_pairs={{0,15},{1,14},{2,13},{3,12},{4,11},{5,10},{6,9},{7,8},{8,7},{9,6},... | collective-permute-start | bytes 344072 | tf_op jit(solution)/shard_map/ppermute | solution.py:371
  83.4 0.0 collective-permute-done.11.refs_1_
  83.4 16.1 %collective-permute-done.20.refs_8_ = bf16[8,7168]{1,0:T(8,128)(2,1)S(1)} collective-permute-done((bf16[8,7168]{1,0:T(8,128)(2,1)S(1)}, bf16[8,7168]{1,0:T(8,128)(2,1)S(1)}, u32[]{:S(2)}, u32[]{:S(2)}) %collective-permute-start.20) | collective-permute-done | bytes 114720 | tf_op jit(solution)/shard_map/ppermute | solution.py:371
  99.5 2.6 %collective-permute-done.21.refs_9_ = bf16[8,7168]{1,0:T(8,128)(2,1)S(1)} collective-permute-done((bf16[8,7168]{1,0:T(8,128)(2,1)S(1)}, bf16[8,7168]{1,0:T(8,128)(2,1)S(1)}, u32[]{:S(2)}, u32[]{:S(2)}) %collective-permute-start.21) | collective-permute-done | bytes 114720 | tf_op jit(solution)/shard_map/ppermute | solution.py:371
  102.1 0.0 collective-permute-done.17.refs_3_
  102.1 0.0 collective-permute-done.18.refs_5_
  102.1 0.0 copy-done
  102.1 1.6 %combine.1 = bf16[128,7168]{1,0:T(8,128)(2,1)} custom-call(bf16[128,7168]{1,0:T(8,128)(2,1)S(1)} %copy-done, s32[8,128]{1,0:T(8,128)S(1)} %get-tuple-element.38.slot_ref, f32[8,128]{1,0:T(8,128)S(1)} %get-tuple-element.39.gates_ref, bf16[16,7168]{1,0:T(8,128)(2,1)S(1)} %get-tuple-element.56.refs_0_, bf16[16,7168]{1,0:T(8,128)(2,1)S(1)} %collective-permute-done.11.refs_1_, ...), custom_call_target="tpu_custom_call" | custom-call | flops 234881024 | bytes 5505024 | tf_op jit(solution)/shard_map/combine/pallas_call | solution.py:343
  (7 shorter events, 0.2 us)
Async XLA Ops:
  3.7 22.3 %collective-permute-start = (bf16[16,7168]{1,0:T(8,128)(2,1)S(1)}, bf16[16,7168]{1,0:T(8,128)(2,1)S(1)}, u32[]{:S(2)}, u32[]{:S(2)}) collective-permute-start(bf16[16,7168]{1,0:T(8,128)(2,1)S(1)} %get-tuple-element.40), channel_id=1, source_target_pairs={{0,8},{1,9},{2,10},{3,11},{4,12},{5,13},{6,14},{7,15},{8,0},{9,1},... | collective-permute-start | bytes 688136 | tf_op jit(solution)/shard_map/ppermute | solution.py:371
  6.1 20.0 %collective-permute-start.1 = (bf16[16,7168]{1,0:T(8,128)(2,1)S(1)}, bf16[16,7168]{1,0:T(8,128)(2,1)S(1)}, u32[]{:S(2)}, u32[]{:S(2)}) collective-permute-start(bf16[16,7168]{1,0:T(8,128)(2,1)S(1)} %get-tuple-element.41), channel_id=1, source_target_pairs={{0,4},{1,5},{2,6},{3,7},{4,0},{5,1},{6,2},{7,3},{8,12},{9,13},{10,... | collective-permute-start | bytes 688136 | tf_op jit(solution)/shard_map/ppermute | solution.py:371
  6.3 19.8 %collective-permute-start.2 = (bf16[16,7168]{1,0:T(8,128)(2,1)S(1)}, bf16[16,7168]{1,0:T(8,128)(2,1)S(1)}, u32[]{:S(2)}, u32[]{:S(2)}) collective-permute-start(bf16[16,7168]{1,0:T(8,128)(2,1)S(1)} %get-tuple-element.42), channel_id=1, source_target_pairs={{0,2},{1,3},{2,0},{3,1},{4,6},{5,7},{6,4},{7,5},{8,10},{9,11},{10,... | collective-permute-start | bytes 688136 | tf_op jit(solution)/shard_map/ppermute | solution.py:371
  7.5 16.1 %collective-permute-start.3 = (bf16[8,7168]{1,0:T(8,128)(2,1)S(1)}, bf16[8,7168]{1,0:T(8,128)(2,1)S(1)}, u32[]{:S(2)}, u32[]{:S(2)}) collective-permute-start(bf16[8,7168]{1,0:T(8,128)(2,1)S(1)} %get-tuple-element.44), channel_id=1, source_target_pairs={{0,12},{1,13},{2,14},{3,15},{4,8},{5,9},{6,10},{7,11},{8,4},{9,5},... | collective-permute-start | bytes 344072 | tf_op jit(solution)/shard_map/ppermute | solution.py:371
  7.7 18.4 %collective-permute-start.4 = (bf16[8,7168]{1,0:T(8,128)(2,1)S(1)}, bf16[8,7168]{1,0:T(8,128)(2,1)S(1)}, u32[]{:S(2)}, u32[]{:S(2)}) collective-permute-start(bf16[8,7168]{1,0:T(8,128)(2,1)S(1)} %get-tuple-element.45), channel_id=1, source_target_pairs={{0,13},{1,12},{2,15},{3,14},{4,9},{5,8},{6,11},{7,10},{8,5},{9,4},... | collective-permute-start | bytes 344072 | tf_op jit(solution)/shard_map/ppermute | solution.py:371
  26.1 8.1 %collective-permute-start.5 = (bf16[32,7168]{1,0:T(8,128)(2,1)S(1)}, bf16[32,7168]{1,0:T(8,128)(2,1)S(1)}, u32[]{:S(2)}, u32[]{:S(2)}) collective-permute-start(bf16[32,7168]{1,0:T(8,128)(2,1)S(1)} %second_halves.2), channel_id=1, source_target_pairs={{0,1},{1,0},{2,3},{3,2},{4,5},{5,4},{6,7},{7,6},{8,9},{9,8},{10,11... | collective-permute-start | bytes 1376264 | tf_op jit(solution)/shard_map/ppermute | solution.py:371
  26.7 24.8 %collective-permute-start.6 = (bf16[16,7168]{1,0:T(8,128)(2,1)S(1)}, bf16[16,7168]{1,0:T(8,128)(2,1)S(1)}, u32[]{:S(2)}, u32[]{:S(2)}) collective-permute-start(bf16[16,7168]{1,0:T(8,128)(2,1)S(1)} %get-tuple-element.52), channel_id=1, source_target_pairs={{0,10},{1,11},{2,8},{3,9},{4,14},{5,15},{6,12},{7,13},{8,2},{9,3},... | collective-permute-start | bytes 688136 | tf_op jit(solution)/shard_map/ppermute | solution.py:371
  26.8 24.7 %collective-permute-start.7 = (bf16[16,7168]{1,0:T(8,128)(2,1)S(1)}, bf16[16,7168]{1,0:T(8,128)(2,1)S(1)}, u32[]{:S(2)}, u32[]{:S(2)}) collective-permute-start(bf16[16,7168]{1,0:T(8,128)(2,1)S(1)} %get-tuple-element.53), channel_id=1, source_target_pairs={{0,6},{1,7},{2,4},{3,5},{4,2},{5,3},{6,0},{7,1},{8,14},{9,15},{10,... | collective-permute-start | bytes 688136 | tf_op jit(solution)/shard_map/ppermute | solution.py:371
  31.0 20.2 %collective-permute-start.8 = (bf16[8,7168]{1,0:T(8,128)(2,1)S(1)}, bf16[8,7168]{1,0:T(8,128)(2,1)S(1)}, u32[]{:S(2)}, u32[]{:S(2)}) collective-permute-start(bf16[8,7168]{1,0:T(8,128)(2,1)S(1)} %get-tuple-element.54), channel_id=1, source_target_pairs={{0,14},{1,15},{2,12},{3,13},{4,10},{5,11},{6,8},{7,9},{8,6},{9,7},... | collective-permute-start | bytes 344072 | tf_op jit(solution)/shard_map/ppermute | solution.py:371
  31.3 20.2 %collective-permute-start.9 = (bf16[8,7168]{1,0:T(8,128)(2,1)S(1)}, bf16[8,7168]{1,0:T(8,128)(2,1)S(1)}, u32[]{:S(2)}, u32[]{:S(2)}) collective-permute-start(bf16[8,7168]{1,0:T(8,128)(2,1)S(1)} %get-tuple-element.55), channel_id=1, source_target_pairs={{0,15},{1,14},{2,13},{3,12},{4,11},{5,10},{6,9},{7,8},{8,7},{9,6},... | collective-permute-start | bytes 344072 | tf_op jit(solution)/shard_map/ppermute | solution.py:371
  51.5 1.9 %collective-permute-start.10 = (bf16[32,7168]{1,0:T(8,128)(2,1)S(1)}, bf16[32,7168]{1,0:T(8,128)(2,1)S(1)}, u32[]{:S(2)}, u32[]{:S(2)}) collective-permute-start(bf16[32,7168]{1,0:T(8,128)(2,1)S(1)} %after.4), channel_id=1, source_target_pairs={{0,1},{1,0},{2,3},{3,2},{4,5},{5,4},{6,7},{7,6},{8,9},{9,8},{10,11... | collective-permute-start | bytes 1376264 | tf_op jit(solution)/shard_map/ppermute | solution.py:371
  52.0 4.2 %collective-permute-start.13 = (bf16[16,7168]{1,0:T(8,128)(2,1)S(1)}, bf16[16,7168]{1,0:T(8,128)(2,1)S(1)}, u32[]{:S(2)}, u32[]{:S(2)}) collective-permute-start(bf16[16,7168]{1,0:T(8,128)(2,1)S(1)} %second_halves.3), channel_id=1, source_target_pairs={{0,1},{1,0},{2,3},{3,2},{4,5},{5,4},{6,7},{7,6},{8,9},{9,8},{10,11... | collective-permute-start | bytes 688136 | tf_op jit(solution)/shard_map/ppermute | solution.py:371
  53.5 19.6 %collective-permute-start.12 = (bf16[16,7168]{1,0:T(8,128)(2,1)S(1)}, bf16[16,7168]{1,0:T(8,128)(2,1)S(1)}, u32[]{:S(2)}, u32[]{:S(2)}) collective-permute-start(bf16[16,7168]{1,0:T(8,128)(2,1)S(1)} %get-tuple-element.58), channel_id=1, source_target_pairs={{0,4},{1,5},{2,6},{3,7},{4,0},{5,1},{6,2},{7,3},{8,12},{9,13},{10,... | collective-permute-start | bytes 688136 | tf_op jit(solution)/shard_map/ppermute | solution.py:371
  54.8 18.3 %collective-permute-start.15 = (bf16[16,7168]{1,0:T(8,128)(2,1)S(1)}, bf16[16,7168]{1,0:T(8,128)(2,1)S(1)}, u32[]{:S(2)}, u32[]{:S(2)}) collective-permute-start(bf16[16,7168]{1,0:T(8,128)(2,1)S(1)} %get-tuple-element.64), channel_id=1, source_target_pairs={{0,8},{1,9},{2,10},{3,11},{4,12},{5,13},{6,14},{7,15},{8,0},{9,1},... | collective-permute-start | bytes 688136 | tf_op jit(solution)/shard_map/ppermute | solution.py:371
  55.0 47.1 %copy-start = (bf16[128,7168]{1,0:T(8,128)(2,1)S(1)}, bf16[128,7168]{1,0:T(8,128)(2,1)}, u32[]{:S(2)}) copy-start(bf16[128,7168]{1,0:T(8,128)(2,1)} %tokens_ref.1) | copy-start | bytes 5505028
  55.0 18.2 %collective-permute-start.14 = (bf16[8,7168]{1,0:T(8,128)(2,1)S(1)}, bf16[8,7168]{1,0:T(8,128)(2,1)S(1)}, u32[]{:S(2)}, u32[]{:S(2)}) collective-permute-start(bf16[8,7168]{1,0:T(8,128)(2,1)S(1)} %get-tuple-element.63), channel_id=1, source_target_pairs={{0,12},{1,13},{2,14},{3,15},{4,8},{5,9},{6,10},{7,11},{8,4},{9,5},... | collective-permute-start | bytes 344072 | tf_op jit(solution)/shard_map/ppermute | solution.py:371
  73.2 2.4 %collective-permute-start.16 = (bf16[16,7168]{1,0:T(8,128)(2,1)S(1)}, bf16[16,7168]{1,0:T(8,128)(2,1)S(1)}, u32[]{:S(2)}, u32[]{:S(2)}) collective-permute-start(bf16[16,7168]{1,0:T(8,128)(2,1)S(1)} %get-tuple-element.65), channel_id=1, source_target_pairs={{0,1},{1,0},{2,3},{3,2},{4,5},{5,4},{6,7},{7,6},{8,9},{9,8},{10,11... | collective-permute-start | bytes 688136 | tf_op jit(solution)/shard_map/ppermute | solution.py:371
  74.5 5.7 %collective-permute-start.19 = (bf16[8,7168]{1,0:T(8,128)(2,1)S(1)}, bf16[8,7168]{1,0:T(8,128)(2,1)S(1)}, u32[]{:S(2)}, u32[]{:S(2)}) collective-permute-start(bf16[8,7168]{1,0:T(8,128)(2,1)S(1)} %get-tuple-element.68), channel_id=1, source_target_pairs={{0,13},{1,12},{2,15},{3,14},{4,9},{5,8},{6,11},{7,10},{8,5},{9,4},... | collective-permute-start | bytes 344072 | tf_op jit(solution)/shard_map/ppermute | solution.py:371
  74.5 8.9 %collective-permute-start.11 = (bf16[16,7168]{1,0:T(8,128)(2,1)S(1)}, bf16[16,7168]{1,0:T(8,128)(2,1)S(1)}, u32[]{:S(2)}, u32[]{:S(2)}) collective-permute-start(bf16[16,7168]{1,0:T(8,128)(2,1)S(1)} %get-tuple-element.57), channel_id=1, source_target_pairs={{0,2},{1,3},{2,0},{3,1},{4,6},{5,7},{6,4},{7,5},{8,10},{9,11},{10,... | collective-permute-start | bytes 688136 | tf_op jit(solution)/shard_map/ppermute | solution.py:371
  75.6 26.4 %collective-permute-start.17 = (bf16[16,7168]{1,0:T(8,128)(2,1)S(1)}, bf16[16,7168]{1,0:T(8,128)(2,1)S(1)}, u32[]{:S(2)}, u32[]{:S(2)}) collective-permute-start(bf16[16,7168]{1,0:T(8,128)(2,1)S(1)} %get-tuple-element.66), channel_id=1, source_target_pairs={{0,6},{1,7},{2,4},{3,5},{4,2},{5,3},{6,0},{7,1},{8,14},{9,15},{10,... | collective-permute-start | bytes 688136 | tf_op jit(solution)/shard_map/ppermute | solution.py:371
  78.9 23.2 %collective-permute-start.18 = (bf16[16,7168]{1,0:T(8,128)(2,1)S(1)}, bf16[16,7168]{1,0:T(8,128)(2,1)S(1)}, u32[]{:S(2)}, u32[]{:S(2)}) collective-permute-start(bf16[16,7168]{1,0:T(8,128)(2,1)S(1)} %get-tuple-element.67), channel_id=1, source_target_pairs={{0,10},{1,11},{2,8},{3,9},{4,14},{5,15},{6,12},{7,13},{8,2},{9,3},... | collective-permute-start | bytes 688136 | tf_op jit(solution)/shard_map/ppermute | solution.py:371
  79.8 19.7 %collective-permute-start.20 = (bf16[8,7168]{1,0:T(8,128)(2,1)S(1)}, bf16[8,7168]{1,0:T(8,128)(2,1)S(1)}, u32[]{:S(2)}, u32[]{:S(2)}) collective-permute-start(bf16[8,7168]{1,0:T(8,128)(2,1)S(1)} %get-tuple-element.69), channel_id=1, source_target_pairs={{0,14},{1,15},{2,12},{3,13},{4,10},{5,11},{6,8},{7,9},{8,6},{9,7},... | collective-permute-start | bytes 344072 | tf_op jit(solution)/shard_map/ppermute | solution.py:371
  80.2 21.9 %collective-permute-start.21 = (bf16[8,7168]{1,0:T(8,128)(2,1)S(1)}, bf16[8,7168]{1,0:T(8,128)(2,1)S(1)}, u32[]{:S(2)}, u32[]{:S(2)}) collective-permute-start(bf16[8,7168]{1,0:T(8,128)(2,1)S(1)} %get-tuple-element.70), channel_id=1, source_target_pairs={{0,15},{1,14},{2,13},{3,12},{4,11},{5,10},{6,9},{7,8},{8,7},{9,6},... | collective-permute-start | bytes 344072 | tf_op jit(solution)/shard_map/ppermute | solution.py:371

commit v4 on v3

--- a/solution.py
+++ b/solution.py
@@ -10,13 +10,13 @@
 EXPERTS = 16
 CAP = 8
 PAIRS = EXPERTS // 2
-PAIRED = ((4, 2, 1, 0), (5, 3))
+PAIRED = ((4, 2, 3, 0), (5, 1))
 SINGLE = ((12, 13), (14, 15))
 BLOCKS = sorted(
     [(2 * m, 2, ("p", m)) for group in PAIRED for m in group]
     + [(k, 1, ("s", k)) for group in SINGLE for k in group]
 )
-FORWARD = (("p", 5), ("p", 3), ("s", 14), ("s", 15))
+FORWARD = (("p", 5), ("p", 1), ("s", 14), ("s", 15))
 RETURN = (("p", 2), ("s", 12), ("p", 4))
 RING = 3
 SPLIT = 2
@@ -385,9 +385,13 @@
         part = jnp.sum(part, axis=0).astype(jnp.bfloat16)
         return jnp.split(part, [sum(out_rows[: i + 1]) for i in range(len(out_rows) - 1)], axis=0)
 
-    vectors = jnp.concatenate(
-        [norm_gain, route_ids.reshape(count).astype(jnp.float32), route_gates.reshape(count)]
-    ).reshape(1, -1)
+    parts = (norm_gain.reshape(1, width), route_ids.reshape(1, count), route_gates.reshape(1, count))
+    at = lax.broadcasted_iota(jnp.int32, (1, width + 2 * count), 1)
+    gain, ids, gates = (
+        jnp.pad(part, ((0, 0), (low, width + 2 * count - low - part.shape[1])))
+        for part, low in zip(parts, (0, width, width + count))
+    )
+    vectors = jnp.where(at < width, gain, jnp.where(at < width + count, ids.astype(jnp.float32), gates))
     *sent, slot_row, gates_row = prepare(tokens, vectors, shards)
     sent = {name: block for (_, _, name), block in zip(BLOCKS, sent)}
 

time: 104 us -> 103 us (level)
  waiting for transfers between devices: 35.9 us -> 32.7 us
  starting transfers between devices: 28.2 us -> 31 us
    ppermute x22, waiting for transfers between devices: 35.9 us -> 32.7 us  [across(): return lax.ppermute(block, 'ep', pairs)]
    ppermute x22, starting transfers between devices: 28.2 us -> 31 us  [across(): return lax.ppermute(block, 'ep', pairs)]
  transfers between devices with their start and end apart: 22 -> 22, of which waited for: 7 -> 8; matrix products, arithmetic and copies ran while one was open for 0% -> 0% of each run, Pallas kernels for 33% -> 33%
where the time goes in v4:
time: 103 us
  Pallas kernels  38 us (37%)
  waiting for transfers between devices  32.7 us (32%)
  starting transfers between devices  31 us (30%)
    pallas_call x2, Pallas kernels, ffn(): pl.pallas_call(functools.partial(ffn_kernel, takes, len(out_rows)), in_sp...  33.9 us
    ppermute x22, waiting for transfers between devices, across(): return lax.ppermute(block, 'ep', pairs)  32.7 us
    ppermute x22, starting transfers between devices, across(): return lax.ppermute(block, 'ep', pairs)  31 us
    pallas_call x1, Pallas kernels, prepare(): pl.pallas_call(functools.partial(prep_kernel, shards), in_specs=[HBM, VME...  2.26 us
  transfers between devices with their start and end apart: 22, of which 8 were waited for; matrix products, arithmetic and copies ran while one was open for 0% of the time, Pallas kernels for 33%

profile of v4, /device:TPU:9, one launch (start us, length us, event | category | flops | bytes accessed | tf_op | source)
XLA Modules:
  0.0 102.6 jit_solution(5792499765080889662)
XLA Ops:
  0.0 0.8 compare_select_fusion.1.vectors_ref
  0.8 2.3 %prepare.1 = (bf16[16,7168]{1,0:T(8,128)(2,1)S(1)}, bf16[16,7168]{1,0:T(8,128)(2,1)S(1)}, bf16[16,7168]{1,0:T(8,128)(2,1)S(1)}, bf16[16,7168]{1,0:T(8,128)(2,1)S...) custom-call(bf16[128,7168]{1,0:T(8,128)(2,1)} %tokens_ref.1, ...), custom_call_target="tpu_custom_call" | custom-call | flops 234881024 | bytes 3670016 | tf_op jit(solution)/shard_map/prepare/pallas_call | solution.py:92
  3.1 2.4 %collective-permute-start = (bf16[16,7168]{1,0:T(8,128)(2,1)S(1)}, bf16[16,7168]{1,0:T(8,128)(2,1)S(1)}, u32[]{:S(2)}, u32[]{:S(2)}) collective-permute-start(bf16[16,7168]{1,0:T(8,128)(2,1)S(1)} %get-tuple-element.40), channel_id=1, source_target_pairs={{0,8},{1,9},{2,10},{3,11},{4,12},{5,13},{6,14},{7,15},{8,0},{9,1},... | collective-permute-start | bytes 688136 | tf_op jit(solution)/shard_map/ppermute | solution.py:371
  5.4 0.2 collective-permute-start.1
  5.6 2.2 %collective-permute-start.2 = (bf16[16,7168]{1,0:T(8,128)(2,1)S(1)}, bf16[16,7168]{1,0:T(8,128)(2,1)S(1)}, u32[]{:S(2)}, u32[]{:S(2)}) collective-permute-start(bf16[16,7168]{1,0:T(8,128)(2,1)S(1)} %get-tuple-element.42), channel_id=1, source_target_pairs={{0,6},{1,7},{2,4},{3,5},{4,2},{5,3},{6,0},{7,1},{8,14},{9,15},{10,... | collective-permute-start | bytes 688136 | tf_op jit(solution)/shard_map/ppermute | solution.py:371
  7.8 0.0 collective-permute-start.3
  7.8 3.1 %collective-permute-start.4 = (bf16[8,7168]{1,0:T(8,128)(2,1)S(1)}, bf16[8,7168]{1,0:T(8,128)(2,1)S(1)}, u32[]{:S(2)}, u32[]{:S(2)}) collective-permute-start(bf16[8,7168]{1,0:T(8,128)(2,1)S(1)} %get-tuple-element.45), channel_id=1, source_target_pairs={{0,13},{1,12},{2,15},{3,14},{4,9},{5,8},{6,11},{7,10},{8,5},{9,4},... | collective-permute-start | bytes 344072 | tf_op jit(solution)/shard_map/ppermute | solution.py:371
  11.0 7.1 %collective-permute-done.3.refs_4_.refs_5_ = bf16[8,7168]{1,0:T(8,128)(2,1)S(1)} collective-permute-done((bf16[8,7168]{1,0:T(8,128)(2,1)S(1)}, bf16[8,7168]{1,0:T(8,128)(2,1)S(1)}, u32[]{:S(2)}, u32[]{:S(2)}) %collective-permute-start.3) | collective-permute-done | bytes 114720 | tf_op jit(solution)/shard_map/ppermute | solution.py:371
  18.1 3.0 %collective-permute-done.4.refs_5_.refs_6_ = bf16[8,7168]{1,0:T(8,128)(2,1)S(1)} collective-permute-done((bf16[8,7168]{1,0:T(8,128)(2,1)S(1)}, bf16[8,7168]{1,0:T(8,128)(2,1)S(1)}, u32[]{:S(2)}, u32[]{:S(2)}) %collective-permute-start.4) | collective-permute-done | bytes 114720 | tf_op jit(solution)/shard_map/ppermute | solution.py:371
  21.1 0.0 collective-permute-done.refs_0_.refs_4_
  21.1 0.0 collective-permute-done.1.refs_1_
  21.1 0.3 collective-permute-done.2.refs_2_
  21.4 2.8 %collective-permute-start.5 = (bf16[32,7168]{1,0:T(8,128)(2,1)S(1)}, bf16[32,7168]{1,0:T(8,128)(2,1)S(1)}, u32[]{:S(2)}, u32[]{:S(2)}) collective-permute-start(bf16[32,7168]{1,0:T(8,128)(2,1)S(1)} %second_halves.2), channel_id=1, source_target_pairs={{0,1},{1,0},{2,3},{3,2},{4,5},{5,4},{6,7},{7,6},{8,9},{9,8},{10,11... | collective-permute-start | bytes 1376264 | tf_op jit(solution)/shard_map/ppermute | solution.py:371
  24.3 5.3 %collective-permute-start.6 = (bf16[16,7168]{1,0:T(8,128)(2,1)S(1)}, bf16[16,7168]{1,0:T(8,128)(2,1)S(1)}, u32[]{:S(2)}, u32[]{:S(2)}) collective-permute-start(bf16[16,7168]{1,0:T(8,128)(2,1)S(1)} %get-tuple-element.52), channel_id=1, source_target_pairs={{0,10},{1,11},{2,8},{3,9},{4,14},{5,15},{6,12},{7,13},{8,2},{9,3},... | collective-permute-start | bytes 688136 | tf_op jit(solution)/shard_map/ppermute | solution.py:371
  29.5 0.3 collective-permute-start.7
  29.8 1.1 %collective-permute-start.8 = (bf16[8,7168]{1,0:T(8,128)(2,1)S(1)}, bf16[8,7168]{1,0:T(8,128)(2,1)S(1)}, u32[]{:S(2)}, u32[]{:S(2)}) collective-permute-start(bf16[8,7168]{1,0:T(8,128)(2,1)S(1)} %get-tuple-element.54), channel_id=1, source_target_pairs={{0,14},{1,15},{2,12},{3,13},{4,10},{5,11},{6,8},{7,9},{8,6},{9,7},... | collective-permute-start | bytes 344072 | tf_op jit(solution)/shard_map/ppermute | solution.py:371
  30.9 2.5 %collective-permute-start.9 = (bf16[8,7168]{1,0:T(8,128)(2,1)S(1)}, bf16[8,7168]{1,0:T(8,128)(2,1)S(1)}, u32[]{:S(2)}, u32[]{:S(2)}) collective-permute-start(bf16[8,7168]{1,0:T(8,128)(2,1)S(1)} %get-tuple-element.55), channel_id=1, source_target_pairs={{0,15},{1,14},{2,13},{3,12},{4,11},{5,10},{6,9},{7,8},{8,7},{9,6},... | collective-permute-start | bytes 344072 | tf_op jit(solution)/shard_map/ppermute | solution.py:371
  33.4 0.0 collective-permute-done.5.refs_4_
  33.4 17.0 %ffn.2 = (bf16[32,7168]{1,0:T(8,128)(2,1)S(1)}, bf16[32,7168]{1,0:T(8,128)(2,1)S(1)}, bf16[8,7168]{1,0:T(8,128)(2,1)S(1)}, bf16[8,7168]{1,0:T(8,128)(2,1)S(1)}) custom-call(bf16[7168,1024]{1,0:T(8,128)(2,1)} %gate_hbm.3, bf16[7168,1024]{1,0:T(8,128)(2,1)} %up_hbm.3, bf16[1024,7168]{1,0:T(8,128)(2,1)} %down_hbm.3, ...), custom_call_target="tpu_custom_call" | custom-call | flops 3523215360 | bytes 46333952 | tf_op jit(solution)/shard_map/ffn/pallas_call | solution.py:289
  50.3 0.0 collective-permute-done.8.refs_3_
  50.3 0.0 collective-permute-done.9.refs_4_
  50.4 0.0 collective-permute-done.6.refs_1_.refs_0_
  50.4 0.0 collective-permute-done.7.refs_2_.refs_1_
  50.4 0.4 collective-permute-start.10
  50.9 0.2 collective-permute-start.11
  51.1 1.2 %collective-permute-done.10.lower_ref = bf16[32,7168]{1,0:T(8,128)(2,1)S(1)} collective-permute-done((bf16[32,7168]{1,0:T(8,128)(2,1)S(1)}, bf16[32,7168]{1,0:T(8,128)(2,1)S(1)}, u32[]{:S(2)}, u32[]{:S(2)}) %collective-permute-start.10) | collective-permute-done | bytes 458784 | tf_op jit(solution)/shard_map/ppermute | solution.py:371
  52.3 0.1 zipped.2
  52.4 0.7 collective-permute-start.12
  53.0 1.1 %collective-permute-start.14 = (bf16[16,7168]{1,0:T(8,128)(2,1)S(1)}, bf16[16,7168]{1,0:T(8,128)(2,1)S(1)}, u32[]{:S(2)}, u32[]{:S(2)}) collective-permute-start(bf16[16,7168]{1,0:T(8,128)(2,1)S(1)} %get-tuple-element.63), channel_id=1, source_target_pairs={{0,8},{1,9},{2,10},{3,11},{4,12},{5,13},{6,14},{7,15},{8,0},{9,1},... | collective-permute-start | bytes 688136 | tf_op jit(solution)/shard_map/ppermute | solution.py:371
  54.1 0.0 copy-start
  54.1 0.9 collective-permute-start.13
  55.1 0.0 collective-permute-done.11.refs_2_
  55.1 16.9 %ffn.3 = (bf16[16,7168]{1,0:T(8,128)(2,1)S(1)}, bf16[16,7168]{1,0:T(8,128)(2,1)S(1)}, bf16[8,7168]{1,0:T(8,128)(2,1)S(1)}, bf16[8,7168]{1,0:T(8,128)(2,1)S(1)}) custom-call(bf16[7168,1024]{1,0:T(8,128)(2,1)} %gate_hbm.3, bf16[7168,1024]{1,0:T(8,128)(2,1)} %up_hbm.3, bf16[1024,7168]{1,0:T(8,128)(2,1)} %down_hbm.3, ...), custom_call_target="tpu_custom_call" | custom-call | flops 2113929216 | bytes 45416448 | tf_op jit(solution)/shard_map/ffn/pallas_call | solution.py:289
  72.0 0.0 collective-permute-done.13.refs_4_.refs_6_
  72.0 0.0 collective-permute-done.12.refs_3_.refs_2_
  72.0 0.0 collective-permute-done.14.refs_5_.refs_4_
  72.1 1.3 %collective-permute-start.15 = (bf16[16,7168]{1,0:T(8,128)(2,1)S(1)}, bf16[16,7168]{1,0:T(8,128)(2,1)S(1)}, u32[]{:S(2)}, u32[]{:S(2)}) collective-permute-start(bf16[16,7168]{1,0:T(8,128)(2,1)S(1)} %get-tuple-element.64), channel_id=1, source_target_pairs={{0,1},{1,0},{2,3},{3,2},{4,5},{5,4},{6,7},{7,6},{8,9},{9,8},{10,11... | collective-permute-start | bytes 688136 | tf_op jit(solution)/shard_map/ppermute | solution.py:371
  73.3 0.2 collective-permute-start.19
  73.6 3.2 %collective-permute-start.17 = (bf16[16,7168]{1,0:T(8,128)(2,1)S(1)}, bf16[16,7168]{1,0:T(8,128)(2,1)S(1)}, u32[]{:S(2)}, u32[]{:S(2)}) collective-permute-start(bf16[16,7168]{1,0:T(8,128)(2,1)S(1)} %get-tuple-element.66), channel_id=1, source_target_pairs={{0,6},{1,7},{2,4},{3,5},{4,2},{5,3},{6,0},{7,1},{8,14},{9,15},{10,... | collective-permute-start | bytes 688136 | tf_op jit(solution)/shard_map/ppermute | solution.py:371
  76.8 0.0 collective-permute-done.15.lower_ref
  76.8 1.3 %collective-permute-start.16 = (bf16[16,7168]{1,0:T(8,128)(2,1)S(1)}, bf16[16,7168]{1,0:T(8,128)(2,1)S(1)}, u32[]{:S(2)}, u32[]{:S(2)}) collective-permute-start(bf16[16,7168]{1,0:T(8,128)(2,1)S(1)} %get-tuple-element.65), channel_id=1, source_target_pairs={{0,2},{1,3},{2,0},{3,1},{4,6},{5,7},{6,4},{7,5},{8,10},{9,11},{10,... | collective-permute-start | bytes 688136 | tf_op jit(solution)/shard_map/ppermute | solution.py:371
  78.1 0.0 collective-permute-start.18
  78.1 1.2 %collective-permute-start.20 = (bf16[8,7168]{1,0:T(8,128)(2,1)S(1)}, bf16[8,7168]{1,0:T(8,128)(2,1)S(1)}, u32[]{:S(2)}, u32[]{:S(2)}) collective-permute-start(bf16[8,7168]{1,0:T(8,128)(2,1)S(1)} %get-tuple-element.69), channel_id=1, source_target_pairs={{0,14},{1,15},{2,12},{3,13},{4,10},{5,11},{6,8},{7,9},{8,6},{9,7},... | collective-permute-start | bytes 344072 | tf_op jit(solution)/shard_map/ppermute | solution.py:371
  79.2 1.8 %collective-permute-done.19.refs_7_ = bf16[8,7168]{1,0:T(8,128)(2,1)S(1)} collective-permute-done((bf16[8,7168]{1,0:T(8,128)(2,1)S(1)}, bf16[8,7168]{1,0:T(8,128)(2,1)S(1)}, u32[]{:S(2)}, u32[]{:S(2)}) %collective-permute-start.19) | collective-permute-done | bytes 114720 | tf_op jit(solution)/shard_map/ppermute | solution.py:371
  81.0 0.7 collective-permute-start.21
  81.8 6.9 %collective-permute-done.17.refs_3_ = bf16[16,7168]{1,0:T(8,128)(2,1)S(1)} collective-permute-done((bf16[16,7168]{1,0:T(8,128)(2,1)S(1)}, bf16[16,7168]{1,0:T(8,128)(2,1)S(1)}, u32[]{:S(2)}, u32[]{:S(2)}) %collective-permute-start.17) | collective-permute-done | bytes 229408 | tf_op jit(solution)/shard_map/ppermute | solution.py:371
  88.7 9.6 %collective-permute-done.20.refs_8_ = bf16[8,7168]{1,0:T(8,128)(2,1)S(1)} collective-permute-done((bf16[8,7168]{1,0:T(8,128)(2,1)S(1)}, bf16[8,7168]{1,0:T(8,128)(2,1)S(1)}, u32[]{:S(2)}, u32[]{:S(2)}) %collective-permute-start.20) | collective-permute-done | bytes 114720 | tf_op jit(solution)/shard_map/ppermute | solution.py:371
  98.3 2.7 %collective-permute-done.21.refs_9_ = bf16[8,7168]{1,0:T(8,128)(2,1)S(1)} collective-permute-done((bf16[8,7168]{1,0:T(8,128)(2,1)S(1)}, bf16[8,7168]{1,0:T(8,128)(2,1)S(1)}, u32[]{:S(2)}, u32[]{:S(2)}) %collective-permute-start.21) | collective-permute-done | bytes 114720 | tf_op jit(solution)/shard_map/ppermute | solution.py:371
  101.0 0.0 collective-permute-done.16.refs_1_
  101.0 0.0 collective-permute-done.18.refs_5_
  101.0 0.0 copy-done
  101.0 1.6 %combine.1 = bf16[128,7168]{1,0:T(8,128)(2,1)} custom-call(bf16[128,7168]{1,0:T(8,128)(2,1)S(1)} %copy-done, s32[8,128]{1,0:T(8,128)S(1)} %get-tuple-element.38.slot_ref, f32[8,128]{1,0:T(8,128)S(1)} %get-tuple-element.39.gates_ref, bf16[16,7168]{1,0:T(8,128)(2,1)S(1)} %get-tuple-element.56.refs_0_, bf16[16,7168]{1,0:T(8,128)(2,1)S(1)} %collective-permute-done.16.refs_1_, ...), custom_call_target="tpu_custom_call" | custom-call | flops 234881024 | bytes 5505024 | tf_op jit(solution)/shard_map/combine/pallas_call | solution.py:343
  (6 shorter events, 0.2 us)
Async XLA Ops:
  3.1 18.0 %collective-permute-start = (bf16[16,7168]{1,0:T(8,128)(2,1)S(1)}, bf16[16,7168]{1,0:T(8,128)(2,1)S(1)}, u32[]{:S(2)}, u32[]{:S(2)}) collective-permute-start(bf16[16,7168]{1,0:T(8,128)(2,1)S(1)} %get-tuple-element.40), channel_id=1, source_target_pairs={{0,8},{1,9},{2,10},{3,11},{4,12},{5,13},{6,14},{7,15},{8,0},{9,1},... | collective-permute-start | bytes 688136 | tf_op jit(solution)/shard_map/ppermute | solution.py:371
  5.4 15.6 %collective-permute-start.1 = (bf16[16,7168]{1,0:T(8,128)(2,1)S(1)}, bf16[16,7168]{1,0:T(8,128)(2,1)S(1)}, u32[]{:S(2)}, u32[]{:S(2)}) collective-permute-start(bf16[16,7168]{1,0:T(8,128)(2,1)S(1)} %get-tuple-element.41), channel_id=1, source_target_pairs={{0,4},{1,5},{2,6},{3,7},{4,0},{5,1},{6,2},{7,3},{8,12},{9,13},{10,... | collective-permute-start | bytes 688136 | tf_op jit(solution)/shard_map/ppermute | solution.py:371
  5.6 15.8 %collective-permute-start.2 = (bf16[16,7168]{1,0:T(8,128)(2,1)S(1)}, bf16[16,7168]{1,0:T(8,128)(2,1)S(1)}, u32[]{:S(2)}, u32[]{:S(2)}) collective-permute-start(bf16[16,7168]{1,0:T(8,128)(2,1)S(1)} %get-tuple-element.42), channel_id=1, source_target_pairs={{0,6},{1,7},{2,4},{3,5},{4,2},{5,3},{6,0},{7,1},{8,14},{9,15},{10,... | collective-permute-start | bytes 688136 | tf_op jit(solution)/shard_map/ppermute | solution.py:371
  7.8 10.2 %collective-permute-start.3 = (bf16[8,7168]{1,0:T(8,128)(2,1)S(1)}, bf16[8,7168]{1,0:T(8,128)(2,1)S(1)}, u32[]{:S(2)}, u32[]{:S(2)}) collective-permute-start(bf16[8,7168]{1,0:T(8,128)(2,1)S(1)} %get-tuple-element.44), channel_id=1, source_target_pairs={{0,12},{1,13},{2,14},{3,15},{4,8},{5,9},{6,10},{7,11},{8,4},{9,5},... | collective-permute-start | bytes 344072 | tf_op jit(solution)/shard_map/ppermute | solution.py:371
  7.8 13.2 %collective-permute-start.4 = (bf16[8,7168]{1,0:T(8,128)(2,1)S(1)}, bf16[8,7168]{1,0:T(8,128)(2,1)S(1)}, u32[]{:S(2)}, u32[]{:S(2)}) collective-permute-start(bf16[8,7168]{1,0:T(8,128)(2,1)S(1)} %get-tuple-element.45), channel_id=1, source_target_pairs={{0,13},{1,12},{2,15},{3,14},{4,9},{5,8},{6,11},{7,10},{8,5},{9,4},... | collective-permute-start | bytes 344072 | tf_op jit(solution)/shard_map/ppermute | solution.py:371
  21.4 11.9 %collective-permute-start.5 = (bf16[32,7168]{1,0:T(8,128)(2,1)S(1)}, bf16[32,7168]{1,0:T(8,128)(2,1)S(1)}, u32[]{:S(2)}, u32[]{:S(2)}) collective-permute-start(bf16[32,7168]{1,0:T(8,128)(2,1)S(1)} %second_halves.2), channel_id=1, source_target_pairs={{0,1},{1,0},{2,3},{3,2},{4,5},{5,4},{6,7},{7,6},{8,9},{9,8},{10,11... | collective-permute-start | bytes 1376264 | tf_op jit(solution)/shard_map/ppermute | solution.py:371
  24.3 26.1 %collective-permute-start.6 = (bf16[16,7168]{1,0:T(8,128)(2,1)S(1)}, bf16[16,7168]{1,0:T(8,128)(2,1)S(1)}, u32[]{:S(2)}, u32[]{:S(2)}) collective-permute-start(bf16[16,7168]{1,0:T(8,128)(2,1)S(1)} %get-tuple-element.52), channel_id=1, source_target_pairs={{0,10},{1,11},{2,8},{3,9},{4,14},{5,15},{6,12},{7,13},{8,2},{9,3},... | collective-permute-start | bytes 688136 | tf_op jit(solution)/shard_map/ppermute | solution.py:371
  29.5 20.8 %collective-permute-start.7 = (bf16[16,7168]{1,0:T(8,128)(2,1)S(1)}, bf16[16,7168]{1,0:T(8,128)(2,1)S(1)}, u32[]{:S(2)}, u32[]{:S(2)}) collective-permute-start(bf16[16,7168]{1,0:T(8,128)(2,1)S(1)} %get-tuple-element.53), channel_id=1, source_target_pairs={{0,2},{1,3},{2,0},{3,1},{4,6},{5,7},{6,4},{7,5},{8,10},{9,11},{10,... | collective-permute-start | bytes 688136 | tf_op jit(solution)/shard_map/ppermute | solution.py:371
  29.8 20.6 %collective-permute-start.8 = (bf16[8,7168]{1,0:T(8,128)(2,1)S(1)}, bf16[8,7168]{1,0:T(8,128)(2,1)S(1)}, u32[]{:S(2)}, u32[]{:S(2)}) collective-permute-start(bf16[8,7168]{1,0:T(8,128)(2,1)S(1)} %get-tuple-element.54), channel_id=1, source_target_pairs={{0,14},{1,15},{2,12},{3,13},{4,10},{5,11},{6,8},{7,9},{8,6},{9,7},... | collective-permute-start | bytes 344072 | tf_op jit(solution)/shard_map/ppermute | solution.py:371
  30.9 19.5 %collective-permute-start.9 = (bf16[8,7168]{1,0:T(8,128)(2,1)S(1)}, bf16[8,7168]{1,0:T(8,128)(2,1)S(1)}, u32[]{:S(2)}, u32[]{:S(2)}) collective-permute-start(bf16[8,7168]{1,0:T(8,128)(2,1)S(1)} %get-tuple-element.55), channel_id=1, source_target_pairs={{0,15},{1,14},{2,13},{3,12},{4,11},{5,10},{6,9},{7,8},{8,7},{9,6},... | collective-permute-start | bytes 344072 | tf_op jit(solution)/shard_map/ppermute | solution.py:371
  50.4 1.9 %collective-permute-start.10 = (bf16[32,7168]{1,0:T(8,128)(2,1)S(1)}, bf16[32,7168]{1,0:T(8,128)(2,1)S(1)}, u32[]{:S(2)}, u32[]{:S(2)}) collective-permute-start(bf16[32,7168]{1,0:T(8,128)(2,1)S(1)} %after.4), channel_id=1, source_target_pairs={{0,1},{1,0},{2,3},{3,2},{4,5},{5,4},{6,7},{7,6},{8,9},{9,8},{10,11... | collective-permute-start | bytes 1376264 | tf_op jit(solution)/shard_map/ppermute | solution.py:371
  50.9 4.2 %collective-permute-start.11 = (bf16[16,7168]{1,0:T(8,128)(2,1)S(1)}, bf16[16,7168]{1,0:T(8,128)(2,1)S(1)}, u32[]{:S(2)}, u32[]{:S(2)}) collective-permute-start(bf16[16,7168]{1,0:T(8,128)(2,1)S(1)} %second_halves.3), channel_id=1, source_target_pairs={{0,1},{1,0},{2,3},{3,2},{4,5},{5,4},{6,7},{7,6},{8,9},{9,8},{10,11... | collective-permute-start | bytes 688136 | tf_op jit(solution)/shard_map/ppermute | solution.py:371
  52.4 19.6 %collective-permute-start.12 = (bf16[16,7168]{1,0:T(8,128)(2,1)S(1)}, bf16[16,7168]{1,0:T(8,128)(2,1)S(1)}, u32[]{:S(2)}, u32[]{:S(2)}) collective-permute-start(bf16[16,7168]{1,0:T(8,128)(2,1)S(1)} %get-tuple-element.61), channel_id=1, source_target_pairs={{0,4},{1,5},{2,6},{3,7},{4,0},{5,1},{6,2},{7,3},{8,12},{9,13},{10,... | collective-permute-start | bytes 688136 | tf_op jit(solution)/shard_map/ppermute | solution.py:371
  53.0 19.0 %collective-permute-start.14 = (bf16[16,7168]{1,0:T(8,128)(2,1)S(1)}, bf16[16,7168]{1,0:T(8,128)(2,1)S(1)}, u32[]{:S(2)}, u32[]{:S(2)}) collective-permute-start(bf16[16,7168]{1,0:T(8,128)(2,1)S(1)} %get-tuple-element.63), channel_id=1, source_target_pairs={{0,8},{1,9},{2,10},{3,11},{4,12},{5,13},{6,14},{7,15},{8,0},{9,1},... | collective-permute-start | bytes 688136 | tf_op jit(solution)/shard_map/ppermute | solution.py:371
  54.1 46.9 %copy-start = (bf16[128,7168]{1,0:T(8,128)(2,1)S(1)}, bf16[128,7168]{1,0:T(8,128)(2,1)}, u32[]{:S(2)}) copy-start(bf16[128,7168]{1,0:T(8,128)(2,1)} %tokens_ref.1) | copy-start | bytes 5505028
  54.1 17.9 %collective-permute-start.13 = (bf16[8,7168]{1,0:T(8,128)(2,1)S(1)}, bf16[8,7168]{1,0:T(8,128)(2,1)S(1)}, u32[]{:S(2)}, u32[]{:S(2)}) collective-permute-start(bf16[8,7168]{1,0:T(8,128)(2,1)S(1)} %get-tuple-element.62), channel_id=1, source_target_pairs={{0,12},{1,13},{2,14},{3,15},{4,8},{5,9},{6,10},{7,11},{8,4},{9,5},... | collective-permute-start | bytes 344072 | tf_op jit(solution)/shard_map/ppermute | solution.py:371
  72.1 4.7 %collective-permute-start.15 = (bf16[16,7168]{1,0:T(8,128)(2,1)S(1)}, bf16[16,7168]{1,0:T(8,128)(2,1)S(1)}, u32[]{:S(2)}, u32[]{:S(2)}) collective-permute-start(bf16[16,7168]{1,0:T(8,128)(2,1)S(1)} %get-tuple-element.64), channel_id=1, source_target_pairs={{0,1},{1,0},{2,3},{3,2},{4,5},{5,4},{6,7},{7,6},{8,9},{9,8},{10,11... | collective-permute-start | bytes 688136 | tf_op jit(solution)/shard_map/ppermute | solution.py:371
  73.3 7.7 %collective-permute-start.19 = (bf16[8,7168]{1,0:T(8,128)(2,1)S(1)}, bf16[8,7168]{1,0:T(8,128)(2,1)S(1)}, u32[]{:S(2)}, u32[]{:S(2)}) collective-permute-start(bf16[8,7168]{1,0:T(8,128)(2,1)S(1)} %get-tuple-element.68), channel_id=1, source_target_pairs={{0,13},{1,12},{2,15},{3,14},{4,9},{5,8},{6,11},{7,10},{8,5},{9,4},... | collective-permute-start | bytes 344072 | tf_op jit(solution)/shard_map/ppermute | solution.py:371
  73.6 15.1 %collective-permute-start.17 = (bf16[16,7168]{1,0:T(8,128)(2,1)S(1)}, bf16[16,7168]{1,0:T(8,128)(2,1)S(1)}, u32[]{:S(2)}, u32[]{:S(2)}) collective-permute-start(bf16[16,7168]{1,0:T(8,128)(2,1)S(1)} %get-tuple-element.66), channel_id=1, source_target_pairs={{0,6},{1,7},{2,4},{3,5},{4,2},{5,3},{6,0},{7,1},{8,14},{9,15},{10,... | collective-permute-start | bytes 688136 | tf_op jit(solution)/shard_map/ppermute | solution.py:371
  76.8 24.2 %collective-permute-start.16 = (bf16[16,7168]{1,0:T(8,128)(2,1)S(1)}, bf16[16,7168]{1,0:T(8,128)(2,1)S(1)}, u32[]{:S(2)}, u32[]{:S(2)}) collective-permute-start(bf16[16,7168]{1,0:T(8,128)(2,1)S(1)} %get-tuple-element.65), channel_id=1, source_target_pairs={{0,2},{1,3},{2,0},{3,1},{4,6},{5,7},{6,4},{7,5},{8,10},{9,11},{10,... | collective-permute-start | bytes 688136 | tf_op jit(solution)/shard_map/ppermute | solution.py:371
  78.1 22.9 %collective-permute-start.18 = (bf16[16,7168]{1,0:T(8,128)(2,1)S(1)}, bf16[16,7168]{1,0:T(8,128)(2,1)S(1)}, u32[]{:S(2)}, u32[]{:S(2)}) collective-permute-start(bf16[16,7168]{1,0:T(8,128)(2,1)S(1)} %get-tuple-element.67), channel_id=1, source_target_pairs={{0,10},{1,11},{2,8},{3,9},{4,14},{5,15},{6,12},{7,13},{8,2},{9,3},... | collective-permute-start | bytes 688136 | tf_op jit(solution)/shard_map/ppermute | solution.py:371
  78.1 20.2 %collective-permute-start.20 = (bf16[8,7168]{1,0:T(8,128)(2,1)S(1)}, bf16[8,7168]{1,0:T(8,128)(2,1)S(1)}, u32[]{:S(2)}, u32[]{:S(2)}) collective-permute-start(bf16[8,7168]{1,0:T(8,128)(2,1)S(1)} %get-tuple-element.69), channel_id=1, source_target_pairs={{0,14},{1,15},{2,12},{3,13},{4,10},{5,11},{6,8},{7,9},{8,6},{9,7},... | collective-permute-start | bytes 344072 | tf_op jit(solution)/shard_map/ppermute | solution.py:371
  81.0 20.0 %collective-permute-start.21 = (bf16[8,7168]{1,0:T(8,128)(2,1)S(1)}, bf16[8,7168]{1,0:T(8,128)(2,1)S(1)}, u32[]{:S(2)}, u32[]{:S(2)}) collective-permute-start(bf16[8,7168]{1,0:T(8,128)(2,1)S(1)} %get-tuple-element.70), channel_id=1, source_target_pairs={{0,15},{1,14},{2,13},{3,12},{4,11},{5,10},{6,9},{7,8},{8,7},{9,6},... | collective-permute-start | bytes 344072 | tf_op jit(solution)/shard_map/ppermute | solution.py:371

commit v5 on v4

--- a/solution.py
+++ b/solution.py
@@ -18,8 +18,8 @@
 )
 FORWARD = (("p", 5), ("p", 1), ("s", 14), ("s", 15))
 RETURN = (("p", 2), ("s", 12), ("p", 4))
-RING = 3
-SPLIT = 2
+RING = 6
+SPLIT = 1
 PREP_VMEM = 51 * 2**20
 HBM = pl.BlockSpec(memory_space=pltpu.HBM)
 VMEM = pl.BlockSpec(memory_space=pltpu.VMEM)
@@ -283,8 +283,8 @@
     parts = len(x_list)
     width = x_list[0].shape[1]
     units = gate.shape[1]
-    depth = tile_of(width, 1024)
-    columns = tile_of(width, 1024)
+    depth = tile_of(width, 512)
+    columns = tile_of(width, 512)
     total = sum(takes)
     return pl.pallas_call(
         functools.partial(ffn_kernel, takes, len(out_rows)),

time: 103 us -> 102 us (level)
  starting transfers between devices: 31 us -> 29.7 us
  Pallas kernels: 38 us -> 36.7 us
  waiting for transfers between devices: 32.7 us -> 34 us
    ppermute x22, waiting for transfers between devices: 32.7 us -> 34 us  [across(): return lax.ppermute(block, 'ep', pairs)]
    ppermute x22, starting transfers between devices: 31 us -> 29.7 us  [across(): return lax.ppermute(block, 'ep', pairs)]
    pallas_call x2, Pallas kernels: 33.9 us -> 32.6 us  [ffn(): pl.pallas_call(functools.partial(ffn_kernel, takes, len(out_rows)), in_sp...]
  transfers between devices with their start and end apart: 22 -> 22, of which waited for: 8 -> 9; matrix products, arithmetic and copies ran while one was open for 0% -> 0% of each run, Pallas kernels for 33% -> 32%
where the time goes in v5:
time: 102 us; the launch traced here: 101 us
  Pallas kernels  36.7 us (36%)
  waiting for transfers between devices  34 us (33%)
  starting transfers between devices  29.7 us (29%)
    ppermute x22, waiting for transfers between devices, across(): return lax.ppermute(block, 'ep', pairs)  34 us
    pallas_call x2, Pallas kernels, ffn(): pl.pallas_call(functools.partial(ffn_kernel, takes, len(out_rows)), in_sp...  32.6 us
    ppermute x22, starting transfers between devices, across(): return lax.ppermute(block, 'ep', pairs)  29.7 us
    pallas_call x1, Pallas kernels, prepare(): pl.pallas_call(functools.partial(prep_kernel, shards), in_specs=[HBM, VME...  2.26 us
  transfers between devices with their start and end apart: 22, of which 9 were waited for; matrix products, arithmetic and copies ran while one was open for 0% of the time, Pallas kernels for 32%

profile of v5, /device:TPU:9, one launch (start us, length us, event | category | flops | bytes accessed | tf_op | source)
XLA Modules:
  0.0 101.4 jit_solution(8062227947143095991)
XLA Ops:
  0.0 0.8 compare_select_fusion.1.vectors_ref
  0.8 2.3 %prepare.1 = (bf16[16,7168]{1,0:T(8,128)(2,1)S(1)}, bf16[16,7168]{1,0:T(8,128)(2,1)S(1)}, bf16[16,7168]{1,0:T(8,128)(2,1)S(1)}, bf16[16,7168]{1,0:T(8,128)(2,1)S...) custom-call(bf16[128,7168]{1,0:T(8,128)(2,1)} %tokens_ref.1, ...), custom_call_target="tpu_custom_call" | custom-call | flops 234881024 | bytes 3670016 | tf_op jit(solution)/shard_map/prepare/pallas_call | solution.py:92
  3.1 2.4 %collective-permute-start = (bf16[16,7168]{1,0:T(8,128)(2,1)S(1)}, bf16[16,7168]{1,0:T(8,128)(2,1)S(1)}, u32[]{:S(2)}, u32[]{:S(2)}) collective-permute-start(bf16[16,7168]{1,0:T(8,128)(2,1)S(1)} %get-tuple-element.40), channel_id=1, source_target_pairs={{0,8},{1,9},{2,10},{3,11},{4,12},{5,13},{6,14},{7,15},{8,0},{9,1},... | collective-permute-start | bytes 688136 | tf_op jit(solution)/shard_map/ppermute | solution.py:371
  5.4 0.2 collective-permute-start.1
  5.6 2.2 %collective-permute-start.2 = (bf16[16,7168]{1,0:T(8,128)(2,1)S(1)}, bf16[16,7168]{1,0:T(8,128)(2,1)S(1)}, u32[]{:S(2)}, u32[]{:S(2)}) collective-permute-start(bf16[16,7168]{1,0:T(8,128)(2,1)S(1)} %get-tuple-element.42), channel_id=1, source_target_pairs={{0,6},{1,7},{2,4},{3,5},{4,2},{5,3},{6,0},{7,1},{8,14},{9,15},{10,... | collective-permute-start | bytes 688136 | tf_op jit(solution)/shard_map/ppermute | solution.py:371
  7.8 0.0 collective-permute-start.3
  7.8 3.1 %collective-permute-start.4 = (bf16[8,7168]{1,0:T(8,128)(2,1)S(1)}, bf16[8,7168]{1,0:T(8,128)(2,1)S(1)}, u32[]{:S(2)}, u32[]{:S(2)}) collective-permute-start(bf16[8,7168]{1,0:T(8,128)(2,1)S(1)} %get-tuple-element.45), channel_id=1, source_target_pairs={{0,13},{1,12},{2,15},{3,14},{4,9},{5,8},{6,11},{7,10},{8,5},{9,4},... | collective-permute-start | bytes 344072 | tf_op jit(solution)/shard_map/ppermute | solution.py:371
  11.0 7.1 %collective-permute-done.3.refs_4_.refs_5_ = bf16[8,7168]{1,0:T(8,128)(2,1)S(1)} collective-permute-done((bf16[8,7168]{1,0:T(8,128)(2,1)S(1)}, bf16[8,7168]{1,0:T(8,128)(2,1)S(1)}, u32[]{:S(2)}, u32[]{:S(2)}) %collective-permute-start.3) | collective-permute-done | bytes 114720 | tf_op jit(solution)/shard_map/ppermute | solution.py:371
  18.1 3.0 %collective-permute-done.4.refs_5_.refs_6_ = bf16[8,7168]{1,0:T(8,128)(2,1)S(1)} collective-permute-done((bf16[8,7168]{1,0:T(8,128)(2,1)S(1)}, bf16[8,7168]{1,0:T(8,128)(2,1)S(1)}, u32[]{:S(2)}, u32[]{:S(2)}) %collective-permute-start.4) | collective-permute-done | bytes 114720 | tf_op jit(solution)/shard_map/ppermute | solution.py:371
  21.1 0.0 collective-permute-done.refs_0_.refs_4_
  21.1 0.0 collective-permute-done.1.refs_1_
  21.1 0.3 collective-permute-done.2.refs_2_
  21.4 2.8 %collective-permute-start.5 = (bf16[32,7168]{1,0:T(8,128)(2,1)S(1)}, bf16[32,7168]{1,0:T(8,128)(2,1)S(1)}, u32[]{:S(2)}, u32[]{:S(2)}) collective-permute-start(bf16[32,7168]{1,0:T(8,128)(2,1)S(1)} %second_halves.2), channel_id=1, source_target_pairs={{0,1},{1,0},{2,3},{3,2},{4,5},{5,4},{6,7},{7,6},{8,9},{9,8},{10,11... | collective-permute-start | bytes 1376264 | tf_op jit(solution)/shard_map/ppermute | solution.py:371
  24.3 5.3 %collective-permute-start.6 = (bf16[16,7168]{1,0:T(8,128)(2,1)S(1)}, bf16[16,7168]{1,0:T(8,128)(2,1)S(1)}, u32[]{:S(2)}, u32[]{:S(2)}) collective-permute-start(bf16[16,7168]{1,0:T(8,128)(2,1)S(1)} %get-tuple-element.52), channel_id=1, source_target_pairs={{0,10},{1,11},{2,8},{3,9},{4,14},{5,15},{6,12},{7,13},{8,2},{9,3},... | collective-permute-start | bytes 688136 | tf_op jit(solution)/shard_map/ppermute | solution.py:371
  29.5 0.3 collective-permute-start.7
  29.8 1.1 %collective-permute-start.8 = (bf16[8,7168]{1,0:T(8,128)(2,1)S(1)}, bf16[8,7168]{1,0:T(8,128)(2,1)S(1)}, u32[]{:S(2)}, u32[]{:S(2)}) collective-permute-start(bf16[8,7168]{1,0:T(8,128)(2,1)S(1)} %get-tuple-element.54), channel_id=1, source_target_pairs={{0,14},{1,15},{2,12},{3,13},{4,10},{5,11},{6,8},{7,9},{8,6},{9,7},... | collective-permute-start | bytes 344072 | tf_op jit(solution)/shard_map/ppermute | solution.py:371
  30.9 2.5 %collective-permute-start.9 = (bf16[8,7168]{1,0:T(8,128)(2,1)S(1)}, bf16[8,7168]{1,0:T(8,128)(2,1)S(1)}, u32[]{:S(2)}, u32[]{:S(2)}) collective-permute-start(bf16[8,7168]{1,0:T(8,128)(2,1)S(1)} %get-tuple-element.55), channel_id=1, source_target_pairs={{0,15},{1,14},{2,13},{3,12},{4,11},{5,10},{6,9},{7,8},{8,7},{9,6},... | collective-permute-start | bytes 344072 | tf_op jit(solution)/shard_map/ppermute | solution.py:371
  33.4 0.0 collective-permute-done.5.refs_4_
  33.4 16.4 %ffn.2 = (bf16[32,7168]{1,0:T(8,128)(2,1)S(1)}, bf16[32,7168]{1,0:T(8,128)(2,1)S(1)}, bf16[8,7168]{1,0:T(8,128)(2,1)S(1)}, bf16[8,7168]{1,0:T(8,128)(2,1)S(1)}) custom-call(bf16[7168,1024]{1,0:T(8,128)(2,1)} %gate_hbm.3, bf16[7168,1024]{1,0:T(8,128)(2,1)} %up_hbm.3, bf16[1024,7168]{1,0:T(8,128)(2,1)} %down_hbm.3, ...), custom_call_target="tpu_custom_call" | custom-call | flops 3523215360 | bytes 46333952 | tf_op jit(solution)/shard_map/ffn/pallas_call | solution.py:289
  49.8 0.0 collective-permute-done.8.refs_3_
  49.8 0.5 collective-permute-done.9.refs_4_
  50.3 0.0 collective-permute-done.6.refs_1_.refs_0_
  50.3 0.0 collective-permute-done.7.refs_2_.refs_1_
  50.4 0.5 collective-permute-start.10
  50.9 0.2 collective-permute-start.11
  51.0 1.2 %collective-permute-done.10.lower_ref = bf16[32,7168]{1,0:T(8,128)(2,1)S(1)} collective-permute-done((bf16[32,7168]{1,0:T(8,128)(2,1)S(1)}, bf16[32,7168]{1,0:T(8,128)(2,1)S(1)}, u32[]{:S(2)}, u32[]{:S(2)}) %collective-permute-start.10) | collective-permute-done | bytes 458784 | tf_op jit(solution)/shard_map/ppermute | solution.py:371
  52.3 0.1 zipped.2
  52.3 0.1 collective-permute-start.12
  52.5 1.3 %collective-permute-start.14 = (bf16[16,7168]{1,0:T(8,128)(2,1)S(1)}, bf16[16,7168]{1,0:T(8,128)(2,1)S(1)}, u32[]{:S(2)}, u32[]{:S(2)}) collective-permute-start(bf16[16,7168]{1,0:T(8,128)(2,1)S(1)} %get-tuple-element.63), channel_id=1, source_target_pairs={{0,8},{1,9},{2,10},{3,11},{4,12},{5,13},{6,14},{7,15},{8,0},{9,1},... | collective-permute-start | bytes 688136 | tf_op jit(solution)/shard_map/ppermute | solution.py:371
  53.8 0.0 copy-start
  53.8 1.3 %collective-permute-start.13 = (bf16[8,7168]{1,0:T(8,128)(2,1)S(1)}, bf16[8,7168]{1,0:T(8,128)(2,1)S(1)}, u32[]{:S(2)}, u32[]{:S(2)}) collective-permute-start(bf16[8,7168]{1,0:T(8,128)(2,1)S(1)} %get-tuple-element.62), channel_id=1, source_target_pairs={{0,12},{1,13},{2,14},{3,15},{4,8},{5,9},{6,10},{7,11},{8,4},{9,5},... | collective-permute-start | bytes 344072 | tf_op jit(solution)/shard_map/ppermute | solution.py:371
  55.1 0.0 collective-permute-done.11.refs_2_
  55.1 16.2 %ffn.3 = (bf16[16,7168]{1,0:T(8,128)(2,1)S(1)}, bf16[16,7168]{1,0:T(8,128)(2,1)S(1)}, bf16[8,7168]{1,0:T(8,128)(2,1)S(1)}, bf16[8,7168]{1,0:T(8,128)(2,1)S(1)}) custom-call(bf16[7168,1024]{1,0:T(8,128)(2,1)} %gate_hbm.3, bf16[7168,1024]{1,0:T(8,128)(2,1)} %up_hbm.3, bf16[1024,7168]{1,0:T(8,128)(2,1)} %down_hbm.3, ...), custom_call_target="tpu_custom_call" | custom-call | flops 2113929216 | bytes 45416448 | tf_op jit(solution)/shard_map/ffn/pallas_call | solution.py:289
  71.3 0.0 collective-permute-done.13.refs_4_.refs_6_
  71.3 0.0 collective-permute-done.12.refs_3_.refs_2_
  71.3 0.0 collective-permute-done.14.refs_5_.refs_4_
  71.4 1.3 %collective-permute-start.15 = (bf16[16,7168]{1,0:T(8,128)(2,1)S(1)}, bf16[16,7168]{1,0:T(8,128)(2,1)S(1)}, u32[]{:S(2)}, u32[]{:S(2)}) collective-permute-start(bf16[16,7168]{1,0:T(8,128)(2,1)S(1)} %get-tuple-element.64), channel_id=1, source_target_pairs={{0,1},{1,0},{2,3},{3,2},{4,5},{5,4},{6,7},{7,6},{8,9},{9,8},{10,11... | collective-permute-start | bytes 688136 | tf_op jit(solution)/shard_map/ppermute | solution.py:371
  72.7 0.2 collective-permute-start.19
  72.9 2.6 %collective-permute-start.17 = (bf16[16,7168]{1,0:T(8,128)(2,1)S(1)}, bf16[16,7168]{1,0:T(8,128)(2,1)S(1)}, u32[]{:S(2)}, u32[]{:S(2)}) collective-permute-start(bf16[16,7168]{1,0:T(8,128)(2,1)S(1)} %get-tuple-element.66), channel_id=1, source_target_pairs={{0,6},{1,7},{2,4},{3,5},{4,2},{5,3},{6,0},{7,1},{8,14},{9,15},{10,... | collective-permute-start | bytes 688136 | tf_op jit(solution)/shard_map/ppermute | solution.py:371
  75.5 0.0 collective-permute-done.15.lower_ref
  75.6 1.3 %collective-permute-start.16 = (bf16[16,7168]{1,0:T(8,128)(2,1)S(1)}, bf16[16,7168]{1,0:T(8,128)(2,1)S(1)}, u32[]{:S(2)}, u32[]{:S(2)}) collective-permute-start(bf16[16,7168]{1,0:T(8,128)(2,1)S(1)} %get-tuple-element.65), channel_id=1, source_target_pairs={{0,2},{1,3},{2,0},{3,1},{4,6},{5,7},{6,4},{7,5},{8,10},{9,11},{10,... | collective-permute-start | bytes 688136 | tf_op jit(solution)/shard_map/ppermute | solution.py:371
  76.8 0.0 collective-permute-start.18
  76.9 1.2 %collective-permute-start.20 = (bf16[8,7168]{1,0:T(8,128)(2,1)S(1)}, bf16[8,7168]{1,0:T(8,128)(2,1)S(1)}, u32[]{:S(2)}, u32[]{:S(2)}) collective-permute-start(bf16[8,7168]{1,0:T(8,128)(2,1)S(1)} %get-tuple-element.69), channel_id=1, source_target_pairs={{0,14},{1,15},{2,12},{3,13},{4,10},{5,11},{6,8},{7,9},{8,6},{9,7},... | collective-permute-start | bytes 344072 | tf_op jit(solution)/shard_map/ppermute | solution.py:371
  78.0 2.8 %collective-permute-done.19.refs_7_ = bf16[8,7168]{1,0:T(8,128)(2,1)S(1)} collective-permute-done((bf16[8,7168]{1,0:T(8,128)(2,1)S(1)}, bf16[8,7168]{1,0:T(8,128)(2,1)S(1)}, u32[]{:S(2)}, u32[]{:S(2)}) %collective-permute-start.19) | collective-permute-done | bytes 114720 | tf_op jit(solution)/shard_map/ppermute | solution.py:371
  80.8 0.0 collective-permute-start.21
  80.8 6.3 %collective-permute-done.17.refs_3_ = bf16[16,7168]{1,0:T(8,128)(2,1)S(1)} collective-permute-done((bf16[16,7168]{1,0:T(8,128)(2,1)S(1)}, bf16[16,7168]{1,0:T(8,128)(2,1)S(1)}, u32[]{:S(2)}, u32[]{:S(2)}) %collective-permute-start.17) | collective-permute-done | bytes 229408 | tf_op jit(solution)/shard_map/ppermute | solution.py:371
  87.1 9.9 %collective-permute-done.20.refs_8_ = bf16[8,7168]{1,0:T(8,128)(2,1)S(1)} collective-permute-done((bf16[8,7168]{1,0:T(8,128)(2,1)S(1)}, bf16[8,7168]{1,0:T(8,128)(2,1)S(1)}, u32[]{:S(2)}, u32[]{:S(2)}) %collective-permute-start.20) | collective-permute-done | bytes 114720 | tf_op jit(solution)/shard_map/ppermute | solution.py:371
  97.0 2.7 %collective-permute-done.21.refs_9_ = bf16[8,7168]{1,0:T(8,128)(2,1)S(1)} collective-permute-done((bf16[8,7168]{1,0:T(8,128)(2,1)S(1)}, bf16[8,7168]{1,0:T(8,128)(2,1)S(1)}, u32[]{:S(2)}, u32[]{:S(2)}) %collective-permute-start.21) | collective-permute-done | bytes 114720 | tf_op jit(solution)/shard_map/ppermute | solution.py:371
  99.8 0.0 collective-permute-done.16.refs_1_
  99.8 0.0 collective-permute-done.18.refs_5_
  99.8 0.0 copy-done
  99.8 1.6 %combine.1 = bf16[128,7168]{1,0:T(8,128)(2,1)} custom-call(bf16[128,7168]{1,0:T(8,128)(2,1)S(1)} %copy-done, s32[8,128]{1,0:T(8,128)S(1)} %get-tuple-element.38.slot_ref, f32[8,128]{1,0:T(8,128)S(1)} %get-tuple-element.39.gates_ref, bf16[16,7168]{1,0:T(8,128)(2,1)S(1)} %get-tuple-element.56.refs_0_, bf16[16,7168]{1,0:T(8,128)(2,1)S(1)} %collective-permute-done.16.refs_1_, ...), custom_call_target="tpu_custom_call" | custom-call | flops 234881024 | bytes 5505024 | tf_op jit(solution)/shard_map/combine/pallas_call | solution.py:343
  (6 shorter events, 0.2 us)
Async XLA Ops:
  3.1 18.0 %collective-permute-start = (bf16[16,7168]{1,0:T(8,128)(2,1)S(1)}, bf16[16,7168]{1,0:T(8,128)(2,1)S(1)}, u32[]{:S(2)}, u32[]{:S(2)}) collective-permute-start(bf16[16,7168]{1,0:T(8,128)(2,1)S(1)} %get-tuple-element.40), channel_id=1, source_target_pairs={{0,8},{1,9},{2,10},{3,11},{4,12},{5,13},{6,14},{7,15},{8,0},{9,1},... | collective-permute-start | bytes 688136 | tf_op jit(solution)/shard_map/ppermute | solution.py:371
  5.4 15.6 %collective-permute-start.1 = (bf16[16,7168]{1,0:T(8,128)(2,1)S(1)}, bf16[16,7168]{1,0:T(8,128)(2,1)S(1)}, u32[]{:S(2)}, u32[]{:S(2)}) collective-permute-start(bf16[16,7168]{1,0:T(8,128)(2,1)S(1)} %get-tuple-element.41), channel_id=1, source_target_pairs={{0,4},{1,5},{2,6},{3,7},{4,0},{5,1},{6,2},{7,3},{8,12},{9,13},{10,... | collective-permute-start | bytes 688136 | tf_op jit(solution)/shard_map/ppermute | solution.py:371
  5.6 15.8 %collective-permute-start.2 = (bf16[16,7168]{1,0:T(8,128)(2,1)S(1)}, bf16[16,7168]{1,0:T(8,128)(2,1)S(1)}, u32[]{:S(2)}, u32[]{:S(2)}) collective-permute-start(bf16[16,7168]{1,0:T(8,128)(2,1)S(1)} %get-tuple-element.42), channel_id=1, source_target_pairs={{0,6},{1,7},{2,4},{3,5},{4,2},{5,3},{6,0},{7,1},{8,14},{9,15},{10,... | collective-permute-start | bytes 688136 | tf_op jit(solution)/shard_map/ppermute | solution.py:371
  7.8 10.2 %collective-permute-start.3 = (bf16[8,7168]{1,0:T(8,128)(2,1)S(1)}, bf16[8,7168]{1,0:T(8,128)(2,1)S(1)}, u32[]{:S(2)}, u32[]{:S(2)}) collective-permute-start(bf16[8,7168]{1,0:T(8,128)(2,1)S(1)} %get-tuple-element.44), channel_id=1, source_target_pairs={{0,12},{1,13},{2,14},{3,15},{4,8},{5,9},{6,10},{7,11},{8,4},{9,5},... | collective-permute-start | bytes 344072 | tf_op jit(solution)/shard_map/ppermute | solution.py:371
  7.8 13.2 %collective-permute-start.4 = (bf16[8,7168]{1,0:T(8,128)(2,1)S(1)}, bf16[8,7168]{1,0:T(8,128)(2,1)S(1)}, u32[]{:S(2)}, u32[]{:S(2)}) collective-permute-start(bf16[8,7168]{1,0:T(8,128)(2,1)S(1)} %get-tuple-element.45), channel_id=1, source_target_pairs={{0,13},{1,12},{2,15},{3,14},{4,9},{5,8},{6,11},{7,10},{8,5},{9,4},... | collective-permute-start | bytes 344072 | tf_op jit(solution)/shard_map/ppermute | solution.py:371
  21.4 11.9 %collective-permute-start.5 = (bf16[32,7168]{1,0:T(8,128)(2,1)S(1)}, bf16[32,7168]{1,0:T(8,128)(2,1)S(1)}, u32[]{:S(2)}, u32[]{:S(2)}) collective-permute-start(bf16[32,7168]{1,0:T(8,128)(2,1)S(1)} %second_halves.2), channel_id=1, source_target_pairs={{0,1},{1,0},{2,3},{3,2},{4,5},{5,4},{6,7},{7,6},{8,9},{9,8},{10,11... | collective-permute-start | bytes 1376264 | tf_op jit(solution)/shard_map/ppermute | solution.py:371
  24.3 26.1 %collective-permute-start.6 = (bf16[16,7168]{1,0:T(8,128)(2,1)S(1)}, bf16[16,7168]{1,0:T(8,128)(2,1)S(1)}, u32[]{:S(2)}, u32[]{:S(2)}) collective-permute-start(bf16[16,7168]{1,0:T(8,128)(2,1)S(1)} %get-tuple-element.52), channel_id=1, source_target_pairs={{0,10},{1,11},{2,8},{3,9},{4,14},{5,15},{6,12},{7,13},{8,2},{9,3},... | collective-permute-start | bytes 688136 | tf_op jit(solution)/shard_map/ppermute | solution.py:371
  29.5 20.8 %collective-permute-start.7 = (bf16[16,7168]{1,0:T(8,128)(2,1)S(1)}, bf16[16,7168]{1,0:T(8,128)(2,1)S(1)}, u32[]{:S(2)}, u32[]{:S(2)}) collective-permute-start(bf16[16,7168]{1,0:T(8,128)(2,1)S(1)} %get-tuple-element.53), channel_id=1, source_target_pairs={{0,2},{1,3},{2,0},{3,1},{4,6},{5,7},{6,4},{7,5},{8,10},{9,11},{10,... | collective-permute-start | bytes 688136 | tf_op jit(solution)/shard_map/ppermute | solution.py:371
  29.8 20.0 %collective-permute-start.8 = (bf16[8,7168]{1,0:T(8,128)(2,1)S(1)}, bf16[8,7168]{1,0:T(8,128)(2,1)S(1)}, u32[]{:S(2)}, u32[]{:S(2)}) collective-permute-start(bf16[8,7168]{1,0:T(8,128)(2,1)S(1)} %get-tuple-element.54), channel_id=1, source_target_pairs={{0,14},{1,15},{2,12},{3,13},{4,10},{5,11},{6,8},{7,9},{8,6},{9,7},... | collective-permute-start | bytes 344072 | tf_op jit(solution)/shard_map/ppermute | solution.py:371
  30.9 19.5 %collective-permute-start.9 = (bf16[8,7168]{1,0:T(8,128)(2,1)S(1)}, bf16[8,7168]{1,0:T(8,128)(2,1)S(1)}, u32[]{:S(2)}, u32[]{:S(2)}) collective-permute-start(bf16[8,7168]{1,0:T(8,128)(2,1)S(1)} %get-tuple-element.55), channel_id=1, source_target_pairs={{0,15},{1,14},{2,13},{3,12},{4,11},{5,10},{6,9},{7,8},{8,7},{9,6},... | collective-permute-start | bytes 344072 | tf_op jit(solution)/shard_map/ppermute | solution.py:371
  50.4 1.9 %collective-permute-start.10 = (bf16[32,7168]{1,0:T(8,128)(2,1)S(1)}, bf16[32,7168]{1,0:T(8,128)(2,1)S(1)}, u32[]{:S(2)}, u32[]{:S(2)}) collective-permute-start(bf16[32,7168]{1,0:T(8,128)(2,1)S(1)} %after.4), channel_id=1, source_target_pairs={{0,1},{1,0},{2,3},{3,2},{4,5},{5,4},{6,7},{7,6},{8,9},{9,8},{10,11... | collective-permute-start | bytes 1376264 | tf_op jit(solution)/shard_map/ppermute | solution.py:371
  50.9 4.2 %collective-permute-start.11 = (bf16[16,7168]{1,0:T(8,128)(2,1)S(1)}, bf16[16,7168]{1,0:T(8,128)(2,1)S(1)}, u32[]{:S(2)}, u32[]{:S(2)}) collective-permute-start(bf16[16,7168]{1,0:T(8,128)(2,1)S(1)} %second_halves.3), channel_id=1, source_target_pairs={{0,1},{1,0},{2,3},{3,2},{4,5},{5,4},{6,7},{7,6},{8,9},{9,8},{10,11... | collective-permute-start | bytes 688136 | tf_op jit(solution)/shard_map/ppermute | solution.py:371
  52.3 19.0 %collective-permute-start.12 = (bf16[16,7168]{1,0:T(8,128)(2,1)S(1)}, bf16[16,7168]{1,0:T(8,128)(2,1)S(1)}, u32[]{:S(2)}, u32[]{:S(2)}) collective-permute-start(bf16[16,7168]{1,0:T(8,128)(2,1)S(1)} %get-tuple-element.61), channel_id=1, source_target_pairs={{0,4},{1,5},{2,6},{3,7},{4,0},{5,1},{6,2},{7,3},{8,12},{9,13},{10,... | collective-permute-start | bytes 688136 | tf_op jit(solution)/shard_map/ppermute | solution.py:371
  52.5 18.8 %collective-permute-start.14 = (bf16[16,7168]{1,0:T(8,128)(2,1)S(1)}, bf16[16,7168]{1,0:T(8,128)(2,1)S(1)}, u32[]{:S(2)}, u32[]{:S(2)}) collective-permute-start(bf16[16,7168]{1,0:T(8,128)(2,1)S(1)} %get-tuple-element.63), channel_id=1, source_target_pairs={{0,8},{1,9},{2,10},{3,11},{4,12},{5,13},{6,14},{7,15},{8,0},{9,1},... | collective-permute-start | bytes 688136 | tf_op jit(solution)/shard_map/ppermute | solution.py:371
  53.8 46.0 %copy-start = (bf16[128,7168]{1,0:T(8,128)(2,1)S(1)}, bf16[128,7168]{1,0:T(8,128)(2,1)}, u32[]{:S(2)}) copy-start(bf16[128,7168]{1,0:T(8,128)(2,1)} %tokens_ref.1) | copy-start | bytes 5505028
  53.8 17.5 %collective-permute-start.13 = (bf16[8,7168]{1,0:T(8,128)(2,1)S(1)}, bf16[8,7168]{1,0:T(8,128)(2,1)S(1)}, u32[]{:S(2)}, u32[]{:S(2)}) collective-permute-start(bf16[8,7168]{1,0:T(8,128)(2,1)S(1)} %get-tuple-element.62), channel_id=1, source_target_pairs={{0,12},{1,13},{2,14},{3,15},{4,8},{5,9},{6,10},{7,11},{8,4},{9,5},... | collective-permute-start | bytes 344072 | tf_op jit(solution)/shard_map/ppermute | solution.py:371
  71.4 4.2 %collective-permute-start.15 = (bf16[16,7168]{1,0:T(8,128)(2,1)S(1)}, bf16[16,7168]{1,0:T(8,128)(2,1)S(1)}, u32[]{:S(2)}, u32[]{:S(2)}) collective-permute-start(bf16[16,7168]{1,0:T(8,128)(2,1)S(1)} %get-tuple-element.64), channel_id=1, source_target_pairs={{0,1},{1,0},{2,3},{3,2},{4,5},{5,4},{6,7},{7,6},{8,9},{9,8},{10,11... | collective-permute-start | bytes 688136 | tf_op jit(solution)/shard_map/ppermute | solution.py:371
  72.7 8.2 %collective-permute-start.19 = (bf16[8,7168]{1,0:T(8,128)(2,1)S(1)}, bf16[8,7168]{1,0:T(8,128)(2,1)S(1)}, u32[]{:S(2)}, u32[]{:S(2)}) collective-permute-start(bf16[8,7168]{1,0:T(8,128)(2,1)S(1)} %get-tuple-element.68), channel_id=1, source_target_pairs={{0,13},{1,12},{2,15},{3,14},{4,9},{5,8},{6,11},{7,10},{8,5},{9,4},... | collective-permute-start | bytes 344072 | tf_op jit(solution)/shard_map/ppermute | solution.py:371
  72.9 14.2 %collective-permute-start.17 = (bf16[16,7168]{1,0:T(8,128)(2,1)S(1)}, bf16[16,7168]{1,0:T(8,128)(2,1)S(1)}, u32[]{:S(2)}, u32[]{:S(2)}) collective-permute-start(bf16[16,7168]{1,0:T(8,128)(2,1)S(1)} %get-tuple-element.66), channel_id=1, source_target_pairs={{0,6},{1,7},{2,4},{3,5},{4,2},{5,3},{6,0},{7,1},{8,14},{9,15},{10,... | collective-permute-start | bytes 688136 | tf_op jit(solution)/shard_map/ppermute | solution.py:371
  75.6 24.2 %collective-permute-start.16 = (bf16[16,7168]{1,0:T(8,128)(2,1)S(1)}, bf16[16,7168]{1,0:T(8,128)(2,1)S(1)}, u32[]{:S(2)}, u32[]{:S(2)}) collective-permute-start(bf16[16,7168]{1,0:T(8,128)(2,1)S(1)} %get-tuple-element.65), channel_id=1, source_target_pairs={{0,2},{1,3},{2,0},{3,1},{4,6},{5,7},{6,4},{7,5},{8,10},{9,11},{10,... | collective-permute-start | bytes 688136 | tf_op jit(solution)/shard_map/ppermute | solution.py:371
  76.8 22.9 %collective-permute-start.18 = (bf16[16,7168]{1,0:T(8,128)(2,1)S(1)}, bf16[16,7168]{1,0:T(8,128)(2,1)S(1)}, u32[]{:S(2)}, u32[]{:S(2)}) collective-permute-start(bf16[16,7168]{1,0:T(8,128)(2,1)S(1)} %get-tuple-element.67), channel_id=1, source_target_pairs={{0,10},{1,11},{2,8},{3,9},{4,14},{5,15},{6,12},{7,13},{8,2},{9,3},... | collective-permute-start | bytes 688136 | tf_op jit(solution)/shard_map/ppermute | solution.py:371
  76.9 20.2 %collective-permute-start.20 = (bf16[8,7168]{1,0:T(8,128)(2,1)S(1)}, bf16[8,7168]{1,0:T(8,128)(2,1)S(1)}, u32[]{:S(2)}, u32[]{:S(2)}) collective-permute-start(bf16[8,7168]{1,0:T(8,128)(2,1)S(1)} %get-tuple-element.69), channel_id=1, source_target_pairs={{0,14},{1,15},{2,12},{3,13},{4,10},{5,11},{6,8},{7,9},{8,6},{9,7},... | collective-permute-start | bytes 344072 | tf_op jit(solution)/shard_map/ppermute | solution.py:371
  80.8 19.0 %collective-permute-start.21 = (bf16[8,7168]{1,0:T(8,128)(2,1)S(1)}, bf16[8,7168]{1,0:T(8,128)(2,1)S(1)}, u32[]{:S(2)}, u32[]{:S(2)}) collective-permute-start(bf16[8,7168]{1,0:T(8,128)(2,1)S(1)} %get-tuple-element.70), channel_id=1, source_target_pairs={{0,15},{1,14},{2,13},{3,12},{4,11},{5,10},{6,9},{7,8},{8,7},{9,6},... | collective-permute-start | bytes 344072 | tf_op jit(solution)/shard_map/ppermute | solution.py:371
